TPU v7x, 512 devices: a whole 4x8x8 slice. The times are simulated.
512 devices in a mesh: block: 4 (over y_hi, core), req: 16 (over x, y_lo), head: 8 (over z).
Axes of the slice: x: 4, y: 8 (y_hi: 2, y_lo: 4; y = y_hi * 4 + y_lo), z: 8, core: 2. Of those that a mesh axis runs over, the one named last changes fastest.
Arguments:
- tokens: bfloat16 [16, 4, 512, 3072], P('req', 'block', None, 'head'), may hold values from -400 to 400, as said below
- levels: int32 [16, 4], P('req', 'block'), may hold values from 0 to 31
- frames: int32 [16, 4], P('req'), may hold values from 1 to 8, as said below
- segment_mask: int32 [16, 4, 4], P('req'), may hold values 0 or 1
- mod_table: float32 [32, 2, 3072], replicated, may hold values from -3 to 3
- w_qkv: bfloat16 [3072, 9216], P('block', 'head'), may hold values from -0.109375 to 0.109375
- q_gain: float32 [128], replicated, may hold values from 0.1 to 1.9
- k_gain: float32 [128], replicated, may hold values from 0.1 to 1.9
Outputs:
- context: bfloat16 [16, 4, 512, 3072], P('req', 'block', None, 'head')
Inputs may be any that keep to these rules, and one draw needn't show every extreme that they name: The first segment of every request holds all 8 frames. Hidden states of order one after the norm; individual tokens and features differ in scale.
All inputs are finite; a program needn't handle non-finite values. No bound on the sum of `segment_mask` on one device may be relied on, other than what follows from the above.
Results may differ from a plain program's by a relative error of at most 0.0042.
Values may be sent and summed in bfloat16 or wider, within the bound.
No kernel may reach another device: no remote copies, remote signals or barrier semaphores. Data moves between devices by JAX's collectives and lax.ppermute only.
A program may use at most 64 MiB of HBM per device.

v0:
```python
import jax
import jax.numpy as jnp
from jax import lax
from jax.sharding import PartitionSpec as P

HD = 128
TPF = 64


EPS = 1e-06


def rms_scale(inputs):
    return lax.rsqrt(jnp.mean(inputs * inputs, axis=-1, keepdims=True) + EPS)


def key_keep(segment_id, own_segment, counts, mask_row, length):
    slot_ids = lax.iota(jnp.int32, counts.shape[0])
    frame_count = jnp.sum(jnp.where(slot_ids == segment_id, counts, 0))
    earlier = jnp.sum(jnp.where(slot_ids == segment_id, mask_row, 0))
    allowed = (segment_id == own_segment) | (segment_id < own_segment) & (earlier == 1)
    frame_ids = lax.iota(jnp.int32, length) // TPF
    return (frame_ids < frame_count) & allowed


def attend(running, queries, key_heads, values, keep_mask):
    numerator, denominator = running
    scores = jnp.einsum(
        "qhe,khe->qhk", queries, key_heads, preferred_element_type=jnp.float32
    ) * HD ** (-0.5)
    exp_scores = jnp.where(keep_mask[None, None, :], jnp.exp(scores), 0.0)
    denominator = denominator + jnp.sum(exp_scores, axis=-1)
    numerator = numerator + jnp.einsum(
        "qhk,khe->qhe", exp_scores.astype(jnp.bfloat16), values, preferred_element_type=jnp.float32
    )
    return (numerator, denominator)


def body(tokens, levels, frames, segment_mask, mod_table, w_qkv, q_gain, k_gain):
    token_rows = tokens[0, 0]
    level_ids = lax.iota(jnp.int32, mod_table.shape[0])
    picked_level = (level_ids == levels[0, 0]).astype(jnp.float32)
    whole_rows = lax.all_gather(token_rows, "head", axis=1, tiled=True)
    widened = whole_rows.astype(jnp.float32)
    mod_rows = jnp.tensordot(picked_level, mod_table, axes=1, precision=lax.Precision.HIGHEST)
    normed = (widened * rms_scale(widened) * (1.0 + mod_rows[0]) + mod_rows[1]).astype(jnp.bfloat16)
    seg_tokens = normed.shape[0]
    columns = w_qkv.shape[1]
    full_weight = lax.all_gather(w_qkv, "block", axis=0, tiled=True)
    projected = jnp.dot(normed, full_weight, preferred_element_type=jnp.float32)
    local_heads = columns // (3 * HD)
    split_heads = projected.reshape(seg_tokens, local_heads, 3, HD)
    query_part = split_heads[:, :, 0]
    key_part = split_heads[:, :, 1]
    queries = (query_part * rms_scale(query_part) * q_gain).astype(jnp.bfloat16)
    key_heads = (key_part * rms_scale(key_part) * k_gain).astype(jnp.bfloat16)
    values = split_heads[:, :, 2].astype(jnp.bfloat16)
    packed = jnp.stack([key_heads, values]).reshape(1, 2, seg_tokens, local_heads * HD)
    own_segment = lax.axis_index("block")
    counts = frames[0]
    slot_ids = lax.iota(jnp.int32, segment_mask.shape[1])
    mask_row = jnp.sum(jnp.where((slot_ids == own_segment)[:, None], segment_mask[0], 0), axis=0)
    start_state = (
        jnp.zeros((seg_tokens, local_heads, HD), jnp.float32),
        jnp.zeros((seg_tokens, local_heads), jnp.float32),
    )
    running = start_state
    incoming = lax.all_gather(packed, "block", axis=0, tiled=True)
    offset = jnp.int32(0)
    for inner in range(incoming.shape[0]):
        keep_mask = key_keep(offset + inner, own_segment, counts, mask_row, seg_tokens)
        remote_keys = incoming[inner, 0].reshape(seg_tokens, local_heads, HD)
        remote_values = incoming[inner, 1].reshape(seg_tokens, local_heads, HD)
        running = attend(running, queries, remote_keys, remote_values, keep_mask)
    numerator, denominator = running
    result = (numerator / denominator[:, :, None]).astype(jnp.bfloat16)
    return result.reshape(1, 1, seg_tokens, local_heads * HD)


def solution(mesh):
    placed = (
        P("req", "block", None, "head"),
        P("req", "block"),
        P("req", None),
        P("req", None, None),
        P(),
        P("block", "head"),
        P(),
        P(),
    )
    return jax.shard_map(
        body, mesh=mesh, in_specs=placed, out_specs=P("req", "block", None, "head"), check_vma=False
    )
```

profile of v0, /device:TPU:1, one launch (start us, length us, event | category | flops | bytes accessed | tf_op | source)
XLA Modules:
  0.0 254.7 jit_solution(13662099752939646041)
XLA Ops:
  6.5 0.7 all-gather.9.cloned.1.call-update
  7.3 0.0 all-gather.5.cloned.1.call-start
  7.3 0.7 all-gather.5.cloned.1.call-update
  8.0 0.0 all-gather.7.cloned.1.call-start
  8.7 0.6 fusion.32
  9.3 0.7 broadcast_bitcast_fusion
  10.0 52.4 %all-gather.9.cloned.1.call-done = bf16[1,1,512,3072]{3,2,1,0:T(8,128)(2,1)} async-done(((bf16[1,1,512,384]{3,2,1,0:T(8,128)(2,1)}), bf16[1,1,512,3072]{3,2,1,0:T(8,128)(2,1)}) %all-gather.9.cloned.1.call-update) | async-done | bytes 3145744 | tf_op jit(solution)/shard_map/all_gather | solution.py:43
  62.4 2.6 %fusion = f32[512]{0:T(512)S(1)} fusion(bf16[1,1,512,3072]{3,2,1,0:T(8,128)(2,1)} %all-gather.9.cloned.1.call-done), kind=kLoop, calls=%fused_computation.2 | loop fusion | flops 4718080 | bytes 3147776 | tf_op jit(solution)/shard_map/reduce_sum | solution.py:14
  64.9 101.0 %all-gather.5.cloned.1.call-done = bf16[3072,1152]{1,0:T(8,128)(2,1)} async-done(((bf16[768,1152]{1,0:T(8,128)(2,1)}), bf16[3072,1152]{1,0:T(8,128)(2,1)}) %all-gather.5.cloned.1.call-update) | async-done | bytes 7077904 | tf_op jit(solution)/shard_map/all_gather | solution.py:49
  166.0 7.7 %fusion.4 = f32[512,1152]{0,1:T(8,128)S(1)} fusion(bf16[3072,1152]{1,0:T(8,128)(2,1)} %all-gather.5.cloned.1.call-done, bf16[1,1,512,3072]{3,2,1,0:T(8,128)(2,1)} %all-gather.9.cloned.1.call-done, f32[3072]{0:T(1024)S(1)} %bitcast.112, f32[3072]{0:T(1024)S(1)} %bitcast.111, f32[512]{0:T(512)S(1)} %add_rsqrt_fusion.2), kind=kOutput, calls=%fused_computation.6 | convolution fusion | flops 3631742976 | bytes 12609536 | tf_op jit(solution)/shard_map/dot_general | solution.py:50
  173.7 0.1 slice.74
  173.7 0.1 multiply_reduce_fusion.1
  173.9 0.1 mul.105
  173.9 0.0 copy-start.3
  174.0 0.0 copy-start.4
  174.0 0.2 multiply_convert_fusion.1
  174.2 0.9 pad_maximum_fusion
  175.1 2.3 copy.32
  177.4 0.0 all-gather.7.cloned.1.call-update
  177.5 0.1 fusion.40
  177.5 0.7 fusion.55
  180.8 0.7 fusion.54
  181.5 1.3 fusion.42
  182.8 1.3 fusion.44
  184.1 0.1 multiply_reduce_fusion
  184.2 0.9 multiply_convert_fusion
  185.0 46.3 %all-gather.7.cloned.1.call-done = bf16[4,2,512,384]{3,2,1,0:T(8,128)(2,1)} async-done(((bf16[1,2,512,384]{3,2,1,0:T(8,128)(2,1)}), bf16[4,2,512,384]{3,2,1,0:T(8,128)(2,1)}) %all-gather.7.cloned.1.call-update) | async-done | bytes 3145744 | tf_op jit(solution)/shard_map/all_gather | solution.py:68
  231.4 3.1 %fusion.66 = (bf16[1,1,512,384]{3,2,1,0:T(8,128)(2,1)S(1)}, bf16[1,1,512,384]{3,2,1,0:T(8,128)(2,1)S(1)}, bf16[1,1,512,384]{3,2,1,0:T(8,128)(2,1)S(1)}, bf16[1,1...) fusion(bf16[4,2,512,384]{3,2,1,0:T(8,128)(2,1)} %all-gather.7.c, ...), kind=kLoop, calls=%fused_computation.107 | loop fusion | bytes 6291456 | tf_op jit(solution)/shard_map/slice | solution.py:72
  234.4 1.2 copy.33
  235.6 1.9 copy.69
  237.5 0.9 copy.38
  238.4 0.2 copy.70
  238.6 0.2 copy.43
  238.8 0.2 copy.71
  239.0 0.2 copy.48
  239.2 0.2 copy.72
  239.4 2.0 bitcast_reduce_fusion.3
  241.4 0.7 fusion.10
  242.1 0.3 copy-done.2
  242.4 0.9 bitcast_reduce_fusion.2
  243.3 0.9 bitcast_reduce_fusion.1
  244.2 0.0 copy-start.1
  244.2 0.9 bitcast_reduce_fusion
  245.1 0.1 copy-done.1
  245.2 0.7 fusion.29
  245.8 0.7 fusion.28
  246.5 0.7 fusion.31
  247.3 0.9 copy.53
  (15 shorter events, 0.1 us)
Async XLA Ops:
  6.5 2.2 copy-start
  6.5 55.8 %all-gather.9.cloned.1.call-start = ((), (), s32[]{:S(2)}) async-start(), calls=%async_computation.2 | async-start | bytes 3538944 | tf_op jit(solution)/shard_map/all_gather | solution.py:43
  7.3 158.7 %all-gather.5.cloned.1.call-start = ((), (), s32[]{:S(2)}) async-start(), calls=%async_computation | async-start | bytes 8847360 | tf_op jit(solution)/shard_map/all_gather | solution.py:49
  8.0 223.3 %all-gather.7.cloned.1.call-start = ((), (), s32[]{:S(2)}) async-start(), calls=%async_computation.1 | async-start | bytes 3932160 | tf_op jit(solution)/shard_map/all_gather | solution.py:68
  173.9 3.5 %copy-start.3 = (s32[1,4,4]{2,1,0:T(4,128)S(1)}, s32[1,4,4]{2,1,0:T(4,128)}, u32[]{:S(2)}) copy-start(s32[1,4,4]{2,1,0:T(4,128)} %param.11) | copy-start | bytes 196
  174.0 6.9 %copy-start.5 = (s32[1,4]{1,0:T(1,128)S(1)}, s32[1,4]{1,0:T(1,128)}, u32[]{:S(2)}) copy-start(s32[1,4]{1,0:T(1,128)} %param.10) | copy-start | bytes 52
  174.0 10.2 %copy-start.4 = (f32[128]{0:T(128)S(1)}, f32[128]{0:T(128)}, u32[]{:S(2)}) copy-start(f32[128]{0:T(128)} %param.14) | copy-start | bytes 1540
  241.4 1.0 copy-start.2
  244.2 1.0 copy-start.1
Sparse Core Ops, SparseCore 0:
  9.5 52.8 all-gather.8
  64.5 101.4 all-gather.4
  177.5 53.7 all-gather.6
where the time goes:
time: 255 us
  waiting for transfers between devices  201 us (79%)
  between operations  16.6 us (7%)
  matrix products  15.6 us (6%)
  local copies, waits for them, and re-layouts  12.5 us (5%)
  other arithmetic  8.82 us (3%)
    all_gather x1, waiting for transfers between devices, body(): full_weight = lax.all_gather(w_qkv, 'block', axis=0, tiled=True)  101 us
    all_gather x1, waiting for transfers between devices, body(): whole_rows = lax.all_gather(token_rows, 'head', axis=1, tiled=True)  52.4 us
    all_gather x1, waiting for transfers between devices, body(): incoming = lax.all_gather(packed, 'block', axis=0, tiled=True)  46.3 us
    dot_general x1, matrix products, body(): projected = jnp.dot(normed, full_weight, preferred_element_type=jnp.float32)  7.7 us
  transfers between devices with their start and end apart: 3, of which 3 were waited for; matrix products, arithmetic and copies ran while one was open for 3% of the time, Pallas kernels for 0%

commit v1 on v0

v1 whole, which is shorter than its diff:
```python
import functools
import math

import jax
import jax.numpy as jnp
from jax import lax
from jax.experimental import pallas as pl
from jax.experimental.pallas import tpu as pltpu
from jax.sharding import PartitionSpec as P

HD = 128
TPF = 64
EPS = 1e-06
MIB = 1 << 20

HALVES, CORES, XS, YS = 2, 2, 4, 4
RING_Y = HALVES * YS


def place(y, core, x):
    return ((y // YS) * CORES + core) * (XS * YS) + x * YS + y % YS


def pairs(move, keep=lambda y: True):
    out = []
    for y in range(RING_Y):
        for core in range(CORES):
            for x in range(XS):
                if keep(y):
                    out.append((place(y, core, x), place(*move(y, core, x))))
    return out


MIRROR = pairs(lambda y, core, x: (RING_Y - 1 - y, core, x))
X_UP = pairs(lambda y, core, x: (y, core, (x + 1) % XS))
X_DOWN = pairs(lambda y, core, x: (y, core, (x - 1) % XS))
SWAP = pairs(lambda y, core, x: (y, 1 - core, x))
UP_FIRST = pairs(lambda y, core, x: (y + 2, core, x), lambda y: y < 4)
UP_SECOND = pairs(lambda y, core, x: (y + 2, core, x), lambda y: 2 <= y < 6)
DOWN_FIRST = pairs(lambda y, core, x: ((y - 2) % 8, core, x), lambda y: y < 4)
DOWN_SECOND = pairs(lambda y, core, x: (y - 2 if y >= 6 else y + 6, core, x), lambda y: y >= 6 or y < 2)


def move(array, table):
    return lax.ppermute(array, ("block", "req"), table)


def turn(array, step, size):
    return lax.ppermute(array, "head", [(i, (i + step) % size) for i in range(size)])


def project_kernel(n_pieces, spots_ref, *refs):
    spot = spots_ref
    (own, r1, l1, r2, l2, r3, l3, r4, l4, mod, gains, w_own, w_pair) = refs[:13]
    pieces = refs[13 : 13 + n_pieces]
    q_out, lo_out, hi_out = refs[13 + n_pieces : 16 + n_pieces]
    weight, normed, sems = refs[16 + n_pieces :]

    copies = []
    for number, source in enumerate((w_own, w_pair) + tuple(pieces)):
        rows = source.shape[0]
        start = pl.multiple_of(spot[8 + number], 96)
        copies.append(pltpu.make_async_copy(source, weight.at[pl.ds(start, rows), :], sems.at[number]))
    for copy in copies:
        copy.start()

    depth = own.shape[1]
    half = own.shape[0] // 2
    features = normed.shape[1]
    step_rows = 64

    for side, last in ((0, r4), (1, l4)):
        def norm_rows(step, carry, side=side, last=last):
            inner = pl.multiple_of(step * step_rows, step_rows)
            outer = pl.multiple_of(side * half + step * step_rows, step_rows)
            views = [ref.at[pl.ds(outer, step_rows), :] for ref in (own, r1, l1, r2, l2, r3, l3)]
            views.append(last.at[pl.ds(inner, step_rows), :])
            total = jnp.zeros((step_rows, 128), jnp.float32)
            for view in views:
                wide = view[...].astype(jnp.float32)
                square = wide * wide
                for lane in range(0, depth, 128):
                    total = total + square[:, lane : lane + 128]
            scale = lax.rsqrt(jnp.sum(total, axis=-1, keepdims=True) * (1.0 / features) + EPS)
            for number, view in enumerate(views):
                part = spot[number]
                wide = view[...].astype(jnp.float32)
                row = wide * scale * mod[0, part] + mod[1, part]
                column = pl.multiple_of(part * depth, 128)
                normed[pl.ds(outer, step_rows), pl.ds(column, depth)] = row.astype(jnp.bfloat16)
            return carry

        lax.fori_loop(0, half // step_rows, norm_rows, 0)

    for copy in copies:
        copy.wait()

    heads = q_out.shape[1] // HD

    def head_norm(part, gain):
        scale = lax.rsqrt(jnp.mean(part * part, axis=-1, keepdims=True) + EPS)
        return (part * scale * gain).astype(jnp.bfloat16)

    for head in range(heads):
        out = jnp.dot(
            normed[...], weight[:, 3 * HD * head : 3 * HD * (head + 1)], preferred_element_type=jnp.float32
        )
        q_out[:, HD * head : HD * (head + 1)] = head_norm(out[:, :HD], gains[0:1, :])
        keys = head_norm(out[:, HD : 2 * HD], gains[1:2, :])
        values = out[:, 2 * HD :].astype(jnp.bfloat16)
        at_k, at_v = HD * head, HD * (heads + head)
        lo_out[:, at_k : at_k + HD] = keys[:half]
        hi_out[:, at_k : at_k + HD] = keys[half:]
        lo_out[:, at_v : at_v + HD] = values[:half]
        hi_out[:, at_v : at_v + HD] = values[half:]


def attend_part(limit, first, q, kv, num, den, heads):
    rows = 256
    keys = kv.shape[0]
    column = lax.broadcasted_iota(jnp.int32, (1, keys), 1) + first
    keep = column < limit
    factor = HD ** (-0.5) * math.log2(math.e)
    for head in range(heads):
        span = slice(HD * head, HD * (head + 1))
        k = kv[:, span]
        v = kv[:, HD * (heads + head) : HD * (heads + head + 1)]
        for top in range(0, q.shape[0], rows):
            band = slice(top, top + rows)
            scores = lax.dot_general(
                q[band, span], k, (((1,), (1,)), ((), ())), preferred_element_type=jnp.float32
            )
            weights = jnp.where(keep, jnp.exp2(scores * factor), 0.0)
            total = weights[:, :128]
            for lane in range(128, keys, 128):
                total = total + weights[:, lane : lane + 128]
            den[band, span] += total
            num[band, span] += jnp.dot(weights.astype(jnp.bfloat16), v, preferred_element_type=jnp.float32)


def near_kernel(limits, q, lo, hi, pair_lo, pair_hi, num, den):
    heads = q.shape[1] // HD
    half = lo.shape[0]
    num[...] = jnp.zeros_like(num)
    den[...] = jnp.zeros_like(den)
    for slot, (low, high) in enumerate(((lo, hi), (pair_lo, pair_hi))):
        for first, part in ((0, low), (half, high)):
            @pl.when(limits[slot] > first)
            def _(slot=slot, first=first, part=part):
                attend_part(limits[slot], first, q, part, num, den, heads)


def far_kernel(limits, q, num_in, den_in, lo, hi, pair_lo, pair_hi, out, num, den):
    heads = q.shape[1] // HD
    half = lo.shape[0]
    num[...] = num_in[...]
    den[...] = den_in[...]
    for slot, (low, high) in enumerate(((lo, hi), (pair_lo, pair_hi))):
        for first, part in ((0, low), (half, high)):
            @pl.when(limits[2 + slot] > first)
            def _(slot=slot, first=first, part=part):
                attend_part(limits[2 + slot], first, q, part, num, den, heads)
    for head in range(heads):
        span = slice(HD * head, HD * (head + 1))
        total = jnp.sum(den[:, span], axis=-1, keepdims=True)
        out[:, span] = (num[:, span] / total).astype(jnp.bfloat16)


def body(tokens, levels, frames, segment_mask, mod_table, w_qkv, q_gain, k_gain):
    own = tokens[0, 0]
    rows, depth = own.shape
    ring = mod_table.shape[2] // depth
    columns = w_qkv.shape[1]
    heads = columns // (3 * HD)
    part_rows = w_qkv.shape[0]
    quarter = part_rows // XS
    piece = quarter // 2

    z = lax.axis_index("head")
    block = lax.axis_index("block")
    side, core = block // CORES, block % CORES
    x = lax.axis_index("req") // YS

    ya = move(lax.dynamic_slice_in_dim(w_qkv, quarter * x, piece), MIRROR)
    r1, l1 = turn(own, 1, ring), turn(own, -1, ring)
    yb = move(lax.dynamic_slice_in_dim(w_qkv, quarter * x + piece, piece), MIRROR)
    w_pair = move(w_qkv, SWAP)
    r2, l2 = turn(r1, 1, ring), turn(l1, -1, ring)
    a_up, a_down = move(ya, X_UP), move(ya, X_DOWN)
    b_up, b_down = move(yb, X_UP), move(yb, X_DOWN)
    r3, l3 = turn(r2, 1, ring), turn(l2, -1, ring)
    a_far = move(a_up, X_UP)
    b_far = move(b_down, X_DOWN)
    r4, l4 = turn(r3[: rows // 2], 1, ring), turn(l3[rows // 2 :], -1, ring)
    up, down, far = (x + XS - 1) % XS, (x + 1) % XS, (x + 2) % XS
    held = [(ya, x, 0), (yb, x, 1), (a_up, up, 0), (a_down, down, 0), (b_up, up, 1), (b_down, down, 1),
            (a_far, far, 0), (b_far, far, 1)]
    other_side = 1 - side
    arrays, starts = [], []
    for array, which, sub in held:
        at = which * quarter + sub * piece
        arrays += [array, move(array, SWAP)]
        starts += [(other_side * CORES + core) * part_rows + at, (other_side * CORES + 1 - core) * part_rows + at]

    order = [z, z - 1, z + 1, z - 2, z + 2, z - 3, z + 3, z + 4]
    spots = [(item + ring) % ring for item in order]
    spots += [block * part_rows, (side * CORES + 1 - core) * part_rows] + starts
    spots = jnp.stack(spots).astype(jnp.int32)

    mod_rows = lax.dynamic_index_in_dim(mod_table, levels[0, 0], 0, keepdims=False)
    mod = (mod_rows + jnp.array([[1.0], [0.0]], jnp.float32)).reshape(2, ring, 1, depth)
    gains = jnp.stack([q_gain, k_gain])

    smem = pl.BlockSpec(memory_space=pltpu.SMEM)
    vmem = pl.BlockSpec(memory_space=pltpu.VMEM)
    anywhere = pl.BlockSpec(memory_space=pl.ANY)
    n = len(arrays)
    queries, kv_lo, kv_hi = pl.pallas_call(
        functools.partial(project_kernel, n),
        out_shape=(
            jax.ShapeDtypeStruct((rows, heads * HD), jnp.bfloat16),
            jax.ShapeDtypeStruct((rows // 2, 2 * heads * HD), jnp.bfloat16),
            jax.ShapeDtypeStruct((rows // 2, 2 * heads * HD), jnp.bfloat16),
        ),
        in_specs=[smem] + [vmem] * 11 + [anywhere] * (2 + n),
        out_specs=(vmem, vmem, vmem),
        scratch_shapes=[
            pltpu.VMEM((ring * depth, columns), jnp.bfloat16),
            pltpu.VMEM((rows, ring * depth), jnp.bfloat16),
            pltpu.SemaphoreType.DMA((2 + n,)),
        ],
        compiler_params=pltpu.CompilerParams(vmem_limit_bytes=32 * MIB),
        cost_estimate=pl.CostEstimate(
            flops=2 * rows * ring * depth * columns, bytes_accessed=12 * MIB, transcendentals=0
        ),
        name="project",
    )(spots, own, r1, l1, r2, l2, r3, l3, r4, l4, mod, gains, w_qkv, w_pair, *arrays)

    far_lo = move(kv_lo, UP_FIRST)
    far_hi = move(kv_hi, DOWN_FIRST)
    pair_lo, pair_hi = move(kv_lo, SWAP), move(kv_hi, SWAP)
    far_lo = move(far_lo, UP_SECOND)
    far_hi = move(far_hi, DOWN_SECOND)
    far_pair_lo, far_pair_hi = move(far_lo, SWAP), move(far_hi, SWAP)

    def limit(segment):
        seen = (segment == block) | (segment < block) & (segment_mask[0, block, segment] == 1)
        return jnp.where(seen, frames[0, segment] * TPF, 0)

    pair = side * CORES + 1 - core
    limits = [limit(item) for item in (block, pair, other_side * CORES + core, other_side * CORES + 1 - core)]
    limits = jnp.stack(limits).astype(jnp.int32)

    sums = jax.ShapeDtypeStruct((rows, heads * HD), jnp.float32)
    work = pl.CostEstimate(
        flops=8 * rows * rows * heads * HD, bytes_accessed=6 * MIB, transcendentals=2 * rows * rows * heads
    )
    num, den = pl.pallas_call(
        near_kernel,
        out_shape=(sums, sums),
        in_specs=[smem] + [vmem] * 5,
        out_specs=(vmem, vmem),
        compiler_params=pltpu.CompilerParams(vmem_limit_bytes=32 * MIB),
        cost_estimate=work,
        name="near",
    )(limits, queries, kv_lo, kv_hi, pair_lo, pair_hi)
    result = pl.pallas_call(
        far_kernel,
        out_shape=jax.ShapeDtypeStruct((rows, heads * HD), jnp.bfloat16),
        in_specs=[smem] + [vmem] * 7,
        out_specs=vmem,
        scratch_shapes=[pltpu.VMEM((rows, heads * HD), jnp.float32)] * 2,
        compiler_params=pltpu.CompilerParams(vmem_limit_bytes=32 * MIB),
        cost_estimate=work,
        name="far",
    )(limits, queries, num, den, far_lo, far_hi, far_pair_lo, far_pair_hi)
    return result.reshape(1, 1, rows, heads * HD)


def solution(mesh):
    placed = (
        P("req", "block", None, "head"),
        P("req", "block"),
        P("req", None),
        P("req", None, None),
        P(),
        P("block", "head"),
        P(),
        P(),
    )
    return jax.shard_map(
        body, mesh=mesh, in_specs=placed, out_specs=P("req", "block", None, "head"), check_vma=False
    )
```

time: 255 us -> 192 us (0.75)
  the two profiles are of different devices: /device:TPU:1 before, /device:TPU:44 now
where the time goes in v1:
time: 192 us; the launch traced here: 191 us
  starting transfers between devices  93.1 us (48%)
  waiting for transfers between devices  58.6 us (31%)
  Pallas kernels  19.2 us (10%)
  local copies, waits for them, and re-layouts  12.9 us (7%)
  between operations  5.96 us (3%)
    ppermute x25, starting transfers between devices, move(): return lax.ppermute(array, ('block', 'req'), table)  59.6 us
    ppermute x25, waiting for transfers between devices, move(): return lax.ppermute(array, ('block', 'req'), table)  50.5 us
    ppermute x8, starting transfers between devices, turn(): lax.ppermute(array, 'head', [(i, (i + step) % size) for i in range(size)])  33.6 us
    pallas_call x1, Pallas kernels, body(): pl.pallas_call(functools.partial(project_kernel, n), out_shape=(jax.Shape...  11.5 us
    unnamed x36, local copies, waits for them, and re-layouts  10.2 us
    ppermute x8, waiting for transfers between devices, turn(): lax.ppermute(array, 'head', [(i, (i + step) % size) for i in range(size)])  8.07 us
    pallas_call x1, Pallas kernels, body(): pl.pallas_call(far_kernel, out_shape=jax.ShapeDtypeStruct((rows, heads *...  4.91 us
  transfers between devices with their start and end apart: 33, of which 8 were waited for; matrix products, arithmetic and copies ran while one was open for 2% of the time, Pallas kernels for 1%

profile of v1, /device:TPU:44, one launch (start us, length us, event | category | flops | bytes accessed | tf_op | source)
XLA Modules:
  0.0 190.6 jit_solution(10579542854126371080)
XLA Ops:
  0.0 11.1 %collective-permute-start.1 = (bf16[512,384]{1,0:T(8,128)(2,1)}, bf16[512,384]{1,0:T(8,128)(2,1)S(1)}, u32[]{:S(2)}, u32[]{:S(2)}) collective-permute-start(bf16[512,384]{1,0:T(8,128)(2,1)} %bitcast.44), channel_id=1, source_target_pairs={{0,7},{1,0},{2,1},{3,2},{4,3},{5,4},{6,5},{7,6},{8,15},{9,8},{10,9... | collective-permute-start | bytes 1179656 | tf_op jit(solution)/shard_map/ppermute | solution.py:49
  11.1 1.9 %collective-permute-start = (bf16[512,384]{1,0:T(8,128)(2,1)}, bf16[512,384]{1,0:T(8,128)(2,1)}, u32[]{:S(2)}, u32[]{:S(2)}) collective-permute-start(bf16[512,384]{1,0:T(8,128)(2,1)} %bitcast.45), channel_id=1, source_target_pairs={{0,1},{1,2},{2,3},{3,4},{4,5},{5,6},{6,7},{7,0},{8,9},{9,10},{10,1... | collective-permute-start | bytes 1179656 | tf_op jit(solution)/shard_map/ppermute | solution.py:49
  13.1 1.1 constant_dynamic-slice_fusion
  14.1 3.0 %collective-permute-start.11 = (bf16[96,1152]{1,0:T(8,128)(2,1)S(1)}, bf16[96,1152]{1,0:T(8,128)(2,1)S(1)}, u32[]{:S(2)}, u32[]{:S(2)}) collective-permute-start(bf16[96,1152]{1,0:T(8,128)(2,1)S(1)} %get-tuple-element.15), channel_id=1, source_target_pairs={{0,280},{32,312},{64,344},{96,376},{128,408},{160,440},{192,472},{... | collective-permute-start | bytes 663560 | tf_op jit(solution)/shard_map/ppermute | solution.py:45
  17.2 5.8 %collective-permute-start.9 = (bf16[96,1152]{1,0:T(8,128)(2,1)S(1)}, bf16[96,1152]{1,0:T(8,128)(2,1)S(1)}, u32[]{:S(2)}, u32[]{:S(2)}) collective-permute-start(bf16[96,1152]{1,0:T(8,128)(2,1)S(1)} %get-tuple-element.16), channel_id=1, source_target_pairs={{0,280},{32,312},{64,344},{96,376},{128,408},{160,440},{192,472},{... | collective-permute-start | bytes 663560 | tf_op jit(solution)/shard_map/ppermute | solution.py:45
  23.0 1.9 %collective-permute-start.8 = (bf16[768,1152]{1,0:T(8,128)(2,1)}, bf16[768,1152]{1,0:T(8,128)(2,1)}, u32[]{:S(2)}, u32[]{:S(2)}) collective-permute-start(bf16[768,1152]{1,0:T(8,128)(2,1)} %refs_11_.1), channel_id=1, source_target_pairs={{0,128},{32,160},{64,192},{96,224},{128,0},{160,32},{192,64},{224,... | collective-permute-start | bytes 5308424 | tf_op jit(solution)/shard_map/ppermute | solution.py:45
  24.9 2.5 %collective-permute-done.11.refs_15_ = bf16[96,1152]{1,0:T(8,128)(2,1)S(1)} collective-permute-done((bf16[96,1152]{1,0:T(8,128)(2,1)S(1)}, bf16[96,1152]{1,0:T(8,128)(2,1)S(1)}, u32[]{:S(2)}, u32[]{:S(2)}) %collective-permute-start.11) | collective-permute-done | bytes 221216 | tf_op jit(solution)/shard_map/ppermute | solution.py:45
  27.5 2.4 %collective-permute-start.19 = (bf16[96,1152]{1,0:T(8,128)(2,1)S(1)}, bf16[96,1152]{1,0:T(8,128)(2,1)}, u32[]{:S(2)}, u32[]{:S(2)}) collective-permute-start(bf16[96,1152]{1,0:T(8,128)(2,1)S(1)} %collective-permute-done.11.refs_15_), channel_id=1, source_target_pairs={{0,96},{32,0},{64,32},{96,64},{128,224},{160,128},{192,160},{224,1... | collective-permute-start | bytes 663560 | tf_op jit(solution)/shard_map/ppermute | solution.py:45
  30.8 3.1 %collective-permute-start.17 = (bf16[96,1152]{1,0:T(8,128)(2,1)S(1)}, bf16[96,1152]{1,0:T(8,128)(2,1)}, u32[]{:S(2)}, u32[]{:S(2)}) collective-permute-start(bf16[96,1152]{1,0:T(8,128)(2,1)S(1)} %collective-permute-done.11.refs_15_), channel_id=1, source_target_pairs={{0,32},{32,64},{64,96},{96,0},{128,160},{160,192},{192,224},{224,1... | collective-permute-start | bytes 663560 | tf_op jit(solution)/shard_map/ppermute | solution.py:45
  33.9 4.9 %collective-permute-start.3 = (bf16[512,384]{1,0:T(8,128)(2,1)S(1)}, bf16[512,384]{1,0:T(8,128)(2,1)}, u32[]{:S(2)}, u32[]{:S(2)}) collective-permute-start(bf16[512,384]{1,0:T(8,128)(2,1)S(1)} %collective-permute-done.1.refs_2_), channel_id=1, source_target_pairs={{0,7},{1,0},{2,1},{3,2},{4,3},{5,4},{6,5},{7,6},{8,15},{9,8},{10,9... | collective-permute-start | bytes 1179656 | tf_op jit(solution)/shard_map/ppermute | solution.py:49
  39.5 1.9 %collective-permute-start.2 = (bf16[512,384]{1,0:T(8,128)(2,1)}, bf16[512,384]{1,0:T(8,128)(2,1)}, u32[]{:S(2)}, u32[]{:S(2)}) collective-permute-start(bf16[512,384]{1,0:T(8,128)(2,1)} %collective-permute-done.refs_1_), channel_id=1, source_target_pairs={{0,1},{1,2},{2,3},{3,4},{4,5},{5,6},{6,7},{7,0},{8,9},{9,10},{10,1... | collective-permute-start | bytes 1179656 | tf_op jit(solution)/shard_map/ppermute | solution.py:49
  41.4 1.9 %collective-permute-start.12 = (bf16[96,1152]{1,0:T(8,128)(2,1)S(1)}, bf16[96,1152]{1,0:T(8,128)(2,1)S(1)}, u32[]{:S(2)}, u32[]{:S(2)}) collective-permute-start(bf16[96,1152]{1,0:T(8,128)(2,1)S(1)} %collective-permute-done.11.refs_15_), channel_id=1, source_target_pairs={{0,128},{32,160},{64,192},{96,224},{128,0},{160,32},{192,64},{224,... | collective-permute-start | bytes 663560 | tf_op jit(solution)/shard_map/ppermute | solution.py:45
  44.1 2.7 %collective-permute-start.15 = (bf16[96,1152]{1,0:T(8,128)(2,1)S(1)}, bf16[96,1152]{1,0:T(8,128)(2,1)}, u32[]{:S(2)}, u32[]{:S(2)}) collective-permute-start(bf16[96,1152]{1,0:T(8,128)(2,1)S(1)} %collective-permute-done.9.refs_13_), channel_id=1, source_target_pairs={{0,96},{32,0},{64,32},{96,64},{128,224},{160,128},{192,160},{224,1... | collective-permute-start | bytes 663560 | tf_op jit(solution)/shard_map/ppermute | solution.py:45
  47.5 3.2 %collective-permute-start.13 = (bf16[96,1152]{1,0:T(8,128)(2,1)S(1)}, bf16[96,1152]{1,0:T(8,128)(2,1)}, u32[]{:S(2)}, u32[]{:S(2)}) collective-permute-start(bf16[96,1152]{1,0:T(8,128)(2,1)S(1)} %collective-permute-done.9.refs_13_), channel_id=1, source_target_pairs={{0,32},{32,64},{64,96},{96,0},{128,160},{160,192},{192,224},{224,1... | collective-permute-start | bytes 663560 | tf_op jit(solution)/shard_map/ppermute | solution.py:45
  50.7 3.6 %collective-permute-done.15.refs_19_ = bf16[96,1152]{1,0:T(8,128)(2,1)} collective-permute-done((bf16[96,1152]{1,0:T(8,128)(2,1)S(1)}, bf16[96,1152]{1,0:T(8,128)(2,1)}, u32[]{:S(2)}, u32[]{:S(2)}) %collective-permute-start.15) | collective-permute-done | bytes 221216 | tf_op jit(solution)/shard_map/ppermute | solution.py:45
  54.3 1.9 %collective-permute-start.10 = (bf16[96,1152]{1,0:T(8,128)(2,1)S(1)}, bf16[96,1152]{1,0:T(8,128)(2,1)S(1)}, u32[]{:S(2)}, u32[]{:S(2)}) collective-permute-start(bf16[96,1152]{1,0:T(8,128)(2,1)S(1)} %collective-permute-done.9.refs_13_), channel_id=1, source_target_pairs={{0,128},{32,160},{64,192},{96,224},{128,0},{160,32},{192,64},{224,... | collective-permute-start | bytes 663560 | tf_op jit(solution)/shard_map/ppermute | solution.py:45
  56.9 5.1 %collective-permute-start.5 = (bf16[512,384]{1,0:T(8,128)(2,1)}, bf16[512,384]{1,0:T(8,128)(2,1)S(1)}, u32[]{:S(2)}, u32[]{:S(2)}) collective-permute-start(bf16[512,384]{1,0:T(8,128)(2,1)} %collective-permute-done.3.refs_4_), channel_id=1, source_target_pairs={{0,7},{1,0},{2,1},{3,2},{4,3},{5,4},{6,5},{7,6},{8,15},{9,8},{10,9... | collective-permute-start | bytes 1179656 | tf_op jit(solution)/shard_map/ppermute | solution.py:49
  62.0 1.9 %collective-permute-start.4 = (bf16[512,384]{1,0:T(8,128)(2,1)}, bf16[512,384]{1,0:T(8,128)(2,1)S(1)}, u32[]{:S(2)}, u32[]{:S(2)}) collective-permute-start(bf16[512,384]{1,0:T(8,128)(2,1)} %collective-permute-done.2.refs_3_), channel_id=1, source_target_pairs={{0,1},{1,2},{2,3},{3,4},{4,5},{5,6},{6,7},{7,0},{8,9},{9,10},{10,1... | collective-permute-start | bytes 1179656 | tf_op jit(solution)/shard_map/ppermute | solution.py:49
  64.0 2.3 %collective-permute-start.23 = (bf16[96,1152]{1,0:T(8,128)(2,1)}, bf16[96,1152]{1,0:T(8,128)(2,1)}, u32[]{:S(2)}, u32[]{:S(2)}) collective-permute-start(bf16[96,1152]{1,0:T(8,128)(2,1)} %collective-permute-done.19.refs_23_), channel_id=1, source_target_pairs={{0,96},{32,0},{64,32},{96,64},{128,224},{160,128},{192,160},{224,1... | collective-permute-start | bytes 663560 | tf_op jit(solution)/shard_map/ppermute | solution.py:45
  67.0 1.9 %collective-permute-start.20 = (bf16[96,1152]{1,0:T(8,128)(2,1)}, bf16[96,1152]{1,0:T(8,128)(2,1)}, u32[]{:S(2)}, u32[]{:S(2)}) collective-permute-start(bf16[96,1152]{1,0:T(8,128)(2,1)} %collective-permute-done.19.refs_23_), channel_id=1, source_target_pairs={{0,128},{32,160},{64,192},{96,224},{128,0},{160,32},{192,64},{224,... | collective-permute-start | bytes 663560 | tf_op jit(solution)/shard_map/ppermute | solution.py:45
  69.6 5.3 %collective-permute-done.23.refs_27_ = bf16[96,1152]{1,0:T(8,128)(2,1)} collective-permute-done((bf16[96,1152]{1,0:T(8,128)(2,1)}, bf16[96,1152]{1,0:T(8,128)(2,1)}, u32[]{:S(2)}, u32[]{:S(2)}) %collective-permute-start.23) | collective-permute-done | bytes 221216 | tf_op jit(solution)/shard_map/ppermute | solution.py:45
  74.9 4.8 %collective-permute-start.21 = (bf16[96,1152]{1,0:T(8,128)(2,1)}, bf16[96,1152]{1,0:T(8,128)(2,1)}, u32[]{:S(2)}, u32[]{:S(2)}) collective-permute-start(bf16[96,1152]{1,0:T(8,128)(2,1)} %collective-permute-done.13.refs_17_), channel_id=1, source_target_pairs={{0,32},{32,64},{64,96},{96,0},{128,160},{160,192},{192,224},{224,1... | collective-permute-start | bytes 663560 | tf_op jit(solution)/shard_map/ppermute | solution.py:45
  79.8 1.9 %collective-permute-start.14 = (bf16[96,1152]{1,0:T(8,128)(2,1)}, bf16[96,1152]{1,0:T(8,128)(2,1)}, u32[]{:S(2)}, u32[]{:S(2)}) collective-permute-start(bf16[96,1152]{1,0:T(8,128)(2,1)} %collective-permute-done.13.refs_17_), channel_id=1, source_target_pairs={{0,128},{32,160},{64,192},{96,224},{128,0},{160,32},{192,64},{224,... | collective-permute-start | bytes 663560 | tf_op jit(solution)/shard_map/ppermute | solution.py:45
  81.7 2.4 %collective-permute-start.18 = (bf16[96,1152]{1,0:T(8,128)(2,1)}, bf16[96,1152]{1,0:T(8,128)(2,1)}, u32[]{:S(2)}, u32[]{:S(2)}) collective-permute-start(bf16[96,1152]{1,0:T(8,128)(2,1)} %collective-permute-done.17.refs_21_), channel_id=1, source_target_pairs={{0,128},{32,160},{64,192},{96,224},{128,0},{160,32},{192,64},{224,... | collective-permute-start | bytes 663560 | tf_op jit(solution)/shard_map/ppermute | solution.py:45
  84.2 1.9 %collective-permute-start.16 = (bf16[96,1152]{1,0:T(8,128)(2,1)}, bf16[96,1152]{1,0:T(8,128)(2,1)}, u32[]{:S(2)}, u32[]{:S(2)}) collective-permute-start(bf16[96,1152]{1,0:T(8,128)(2,1)} %collective-permute-done.15.refs_19_), channel_id=1, source_target_pairs={{0,128},{32,160},{64,192},{96,224},{128,0},{160,32},{192,64},{224,... | collective-permute-start | bytes 663560 | tf_op jit(solution)/shard_map/ppermute | solution.py:45
  87.3 2.4 %collective-permute-start.24 = (bf16[96,1152]{1,0:T(8,128)(2,1)}, bf16[96,1152]{1,0:T(8,128)(2,1)S(1)}, u32[]{:S(2)}, u32[]{:S(2)}) collective-permute-start(bf16[96,1152]{1,0:T(8,128)(2,1)} %collective-permute-done.23.refs_27_), channel_id=1, source_target_pairs={{0,128},{32,160},{64,192},{96,224},{128,0},{160,32},{192,64},{224,... | collective-permute-start | bytes 663560 | tf_op jit(solution)/shard_map/ppermute | solution.py:45
  89.7 1.9 %collective-permute-start.22 = (bf16[96,1152]{1,0:T(8,128)(2,1)}, bf16[96,1152]{1,0:T(8,128)(2,1)S(1)}, u32[]{:S(2)}, u32[]{:S(2)}) collective-permute-start(bf16[96,1152]{1,0:T(8,128)(2,1)} %collective-permute-done.21.refs_25_), channel_id=1, source_target_pairs={{0,128},{32,160},{64,192},{96,224},{128,0},{160,32},{192,64},{224,... | collective-permute-start | bytes 663560 | tf_op jit(solution)/shard_map/ppermute | solution.py:45
  91.6 4.9 %collective-permute-start.7 = (bf16[256,384]{1,0:T(8,128)(2,1)S(1)}, bf16[256,384]{1,0:T(8,128)(2,1)S(1)}, u32[]{:S(2)}, u32[]{:S(2)}) collective-permute-start(bf16[256,384]{1,0:T(8,128)(2,1)S(1)} %slice.9), channel_id=1, source_target_pairs={{0,7},{1,0},{2,1},{3,2},{4,3},{5,4},{6,5},{7,6},{8,15},{9,8},{10,9... | collective-permute-start | bytes 589832 | tf_op jit(solution)/shard_map/ppermute | solution.py:49
  96.5 1.9 %collective-permute-start.6 = (bf16[256,384]{1,0:T(8,128)(2,1)S(1)}, bf16[256,384]{1,0:T(8,128)(2,1)S(1)}, u32[]{:S(2)}, u32[]{:S(2)}) collective-permute-start(bf16[256,384]{1,0:T(8,128)(2,1)S(1)} %slice.8), channel_id=1, source_target_pairs={{0,1},{1,2},{2,3},{3,4},{4,5},{5,6},{6,7},{7,0},{8,9},{9,10},{10,1... | collective-permute-start | bytes 589832 | tf_op jit(solution)/shard_map/ppermute | solution.py:49
  98.6 2.7 %collective-permute-done.7.refs_8_ = bf16[256,384]{1,0:T(8,128)(2,1)S(1)} collective-permute-done((bf16[256,384]{1,0:T(8,128)(2,1)S(1)}, bf16[256,384]{1,0:T(8,128)(2,1)S(1)}, u32[]{:S(2)}, u32[]{:S(2)}) %collective-permute-start.7) | collective-permute-done | bytes 196640 | tf_op jit(solution)/shard_map/ppermute | solution.py:49
  101.3 5.3 %collective-permute-done.6.refs_7_ = bf16[256,384]{1,0:T(8,128)(2,1)S(1)} collective-permute-done((bf16[256,384]{1,0:T(8,128)(2,1)S(1)}, bf16[256,384]{1,0:T(8,128)(2,1)S(1)}, u32[]{:S(2)}, u32[]{:S(2)}) %collective-permute-start.6) | collective-permute-done | bytes 196640 | tf_op jit(solution)/shard_map/ppermute | solution.py:49
  106.7 1.0 copy-done.3
  107.6 1.0 copy-done.4
  108.6 1.0 copy-done.6
  109.6 0.9 copy-done.8
  111.5 0.9 copy-done.12
  113.4 11.5 %project.1 = (bf16[512,384]{1,0:T(8,128)(2,1)S(1)}, bf16[256,768]{1,0:T(8,128)(2,1)}, bf16[256,768]{1,0:T(8,128)(2,1)}) custom-call(s32[26]{0:T(128)S(1)} %stack.136.spots_ref, bf16[512,384]{1,0:T(8,128)(2,1)S(1)} %bitcast.46, bf16[512,384]{1,0:T(8,128)(2,1)} %collective-permute-done.refs_1_, bf16[512,384]{1,0:T(8,128)(2,1)S(1)} %copy-done.6, ...), custom_call_target="tpu_custom_call" | custom-call | flops 3623878656 | bytes 12582912 | tf_op jit(solution)/shard_map/project/pallas_call | solution.py:218
  124.9 1.3 collective-permute-start.27
  126.9 21.9 %collective-permute-done.27 = bf16[256,768]{1,0:T(8,128)(2,1)S(1)} collective-permute-done((bf16[256,768]{1,0:T(8,128)(2,1)}, bf16[256,768]{1,0:T(8,128)(2,1)S(1)}, u32[]{:S(2)}, u32[]{:S(2)}) %collective-permute-start.27) | collective-permute-done | bytes 393248 | tf_op jit(solution)/shard_map/ppermute | solution.py:45
  148.8 1.9 %collective-permute-start.28 = (bf16[256,768]{1,0:T(8,128)(2,1)S(1)}, bf16[256,768]{1,0:T(8,128)(2,1)S(1)}, u32[]{:S(2)}, u32[]{:S(2)}) collective-permute-start(bf16[256,768]{1,0:T(8,128)(2,1)S(1)} %collective-permute-done.27), channel_id=1, source_target_pairs={{16,256},{48,288},{80,320},{112,352},{144,384},{176,416},{208,448}... | collective-permute-start | bytes 1179656 | tf_op jit(solution)/shard_map/ppermute | solution.py:45
  150.7 1.3 collective-permute-start.30
  152.0 1.9 %collective-permute-start.25 = (bf16[256,768]{1,0:T(8,128)(2,1)}, bf16[256,768]{1,0:T(8,128)(2,1)S(1)}, u32[]{:S(2)}, u32[]{:S(2)}) collective-permute-start(bf16[256,768]{1,0:T(8,128)(2,1)} %get-tuple-element.11.lo), channel_id=1, source_target_pairs={{0,128},{32,160},{64,192},{96,224},{128,0},{160,32},{192,64},{224,... | collective-permute-start | bytes 1179656 | tf_op jit(solution)/shard_map/ppermute | solution.py:45
  153.9 2.4 %collective-permute-start.26 = (bf16[256,768]{1,0:T(8,128)(2,1)}, bf16[256,768]{1,0:T(8,128)(2,1)S(1)}, u32[]{:S(2)}, u32[]{:S(2)}) collective-permute-start(bf16[256,768]{1,0:T(8,128)(2,1)} %get-tuple-element.12.hi), channel_id=1, source_target_pairs={{0,128},{32,160},{64,192},{96,224},{128,0},{160,32},{192,64},{224,... | collective-permute-start | bytes 1179656 | tf_op jit(solution)/shard_map/ppermute | solution.py:45
  156.3 16.3 %collective-permute-done.28.lo = bf16[256,768]{1,0:T(8,128)(2,1)S(1)} collective-permute-done((bf16[256,768]{1,0:T(8,128)(2,1)S(1)}, bf16[256,768]{1,0:T(8,128)(2,1)S(1)}, u32[]{:S(2)}, u32[]{:S(2)}) %collective-permute-start.28) | collective-permute-done | bytes 393248 | tf_op jit(solution)/shard_map/ppermute | solution.py:45
  172.6 1.9 %collective-permute-start.31 = (bf16[256,768]{1,0:T(8,128)(2,1)S(1)}, bf16[256,768]{1,0:T(8,128)(2,1)S(1)}, u32[]{:S(2)}, u32[]{:S(2)}) collective-permute-start(bf16[256,768]{1,0:T(8,128)(2,1)S(1)} %collective-permute-done.28.lo), channel_id=1, source_target_pairs={{0,128},{32,160},{64,192},{96,224},{128,0},{160,32},{192,64},{224,... | collective-permute-start | bytes 1179656 | tf_op jit(solution)/shard_map/ppermute | solution.py:45
  174.6 2.4 %collective-permute-start.32 = (bf16[256,768]{1,0:T(8,128)(2,1)S(1)}, bf16[256,768]{1,0:T(8,128)(2,1)S(1)}, u32[]{:S(2)}, u32[]{:S(2)}) collective-permute-start(bf16[256,768]{1,0:T(8,128)(2,1)S(1)} %collective-permute-done.30.hi), channel_id=1, source_target_pairs={{0,128},{32,160},{64,192},{96,224},{128,0},{160,32},{192,64},{224,... | collective-permute-start | bytes 1179656 | tf_op jit(solution)/shard_map/ppermute | solution.py:45
  182.9 2.8 %near.1 = (f32[512,384]{1,0:T(8,128)S(1)}, f32[512,384]{1,0:T(8,128)S(1)}) custom-call(s32[4]{0:T(128)S(1)} %pad_add_fusion.limits, bf16[512,384]{1,0:T(8,128)(2,1)S(1)} %get-tuple-element.10.q, bf16[256,768]{1,0:T(8,128)(2,1)} %get-tuple-element.11.lo, bf16[256,768]{1,0:T(8,128)(2,1)} %get-tuple-element.12.hi, ...), custom_call_target="tpu_custom_call" | custom-call | flops 805306368 | bytes 6291456 | tf_op jit(solution)/shard_map/near/pallas_call | solution.py:258
  185.7 4.9 %far.1 = bf16[512,384]{1,0:T(8,128)(2,1)} custom-call(s32[4]{0:T(128)S(1)} %pad_add_fusion.limits, bf16[512,384]{1,0:T(8,128)(2,1)S(1)} %get-tuple-element.10.q, f32[512,384]{1,0:T(8,128)S(1)} %get-tuple-element.13.num_in, f32[512,384]{1,0:T(8,128)S(1)} %get-tuple-element.14.den_in, bf16[256,768]{1,0:T(8,128)(2,1)S(1)} %collective-permute-done.28.lo, ...), custom_call_target="tpu_custom_call" | custom-call | flops 805306368 | bytes 6291456 | tf_op jit(solution)/shard_map/far/pallas_call | solution.py:267
  (68 shorter events, 9.4 us)
Async XLA Ops:
  0.0 86.1 %copy-start = (f32[32,2,3072]{2,1,0:T(2,128)S(1)}, f32[32,2,3072]{2,1,0:T(2,128)}, u32[]{:S(2)}) copy-start(f32[32,2,3072]{2,1,0:T(2,128)} %param.13) | copy-start | bytes 2359300
  0.0 98.4 %copy-start.17 = (f32[2]{0:T(128)S(1)}, f32[2]{0:T(128)}, u32[]{:S(2)}) copy-start(f32[2]{0:T(128)} %constant.153) | copy-start | bytes 28
  0.0 106.6 %copy-start.1 = (bf16[768,1152]{1,0:T(8,128)(2,1)S(1)}, bf16[768,1152]{1,0:T(8,128)(2,1)}, u32[]{:S(2)}) copy-start(bf16[768,1152]{1,0:T(8,128)(2,1)} %refs_11_.1) | copy-start | bytes 5308420
  0.0 33.9 %collective-permute-start.1 = (bf16[512,384]{1,0:T(8,128)(2,1)}, bf16[512,384]{1,0:T(8,128)(2,1)S(1)}, u32[]{:S(2)}, u32[]{:S(2)}) collective-permute-start(bf16[512,384]{1,0:T(8,128)(2,1)} %bitcast.44), channel_id=1, source_target_pairs={{0,7},{1,0},{2,1},{3,2},{4,3},{5,4},{6,5},{7,6},{8,15},{9,8},{10,9... | collective-permute-start | bytes 1179656 | tf_op jit(solution)/shard_map/ppermute | solution.py:49
  11.1 28.4 %collective-permute-start = (bf16[512,384]{1,0:T(8,128)(2,1)}, bf16[512,384]{1,0:T(8,128)(2,1)}, u32[]{:S(2)}, u32[]{:S(2)}) collective-permute-start(bf16[512,384]{1,0:T(8,128)(2,1)} %bitcast.45), channel_id=1, source_target_pairs={{0,1},{1,2},{2,3},{3,4},{4,5},{5,6},{6,7},{7,0},{8,9},{9,10},{10,1... | collective-permute-start | bytes 1179656 | tf_op jit(solution)/shard_map/ppermute | solution.py:49
  14.1 13.3 %collective-permute-start.11 = (bf16[96,1152]{1,0:T(8,128)(2,1)S(1)}, bf16[96,1152]{1,0:T(8,128)(2,1)S(1)}, u32[]{:S(2)}, u32[]{:S(2)}) collective-permute-start(bf16[96,1152]{1,0:T(8,128)(2,1)S(1)} %get-tuple-element.15), channel_id=1, source_target_pairs={{0,280},{32,312},{64,344},{96,376},{128,408},{160,440},{192,472},{... | collective-permute-start | bytes 663560 | tf_op jit(solution)/shard_map/ppermute | solution.py:45
  17.2 13.6 %collective-permute-start.9 = (bf16[96,1152]{1,0:T(8,128)(2,1)S(1)}, bf16[96,1152]{1,0:T(8,128)(2,1)S(1)}, u32[]{:S(2)}, u32[]{:S(2)}) collective-permute-start(bf16[96,1152]{1,0:T(8,128)(2,1)S(1)} %get-tuple-element.16), channel_id=1, source_target_pairs={{0,280},{32,312},{64,344},{96,376},{128,408},{160,440},{192,472},{... | collective-permute-start | bytes 663560 | tf_op jit(solution)/shard_map/ppermute | solution.py:45
  23.0 83.6 %collective-permute-start.8 = (bf16[768,1152]{1,0:T(8,128)(2,1)}, bf16[768,1152]{1,0:T(8,128)(2,1)}, u32[]{:S(2)}, u32[]{:S(2)}) collective-permute-start(bf16[768,1152]{1,0:T(8,128)(2,1)} %refs_11_.1), channel_id=1, source_target_pairs={{0,128},{32,160},{64,192},{96,224},{128,0},{160,32},{192,64},{224,... | collective-permute-start | bytes 5308424 | tf_op jit(solution)/shard_map/ppermute | solution.py:45
  27.5 14.0 %collective-permute-start.19 = (bf16[96,1152]{1,0:T(8,128)(2,1)S(1)}, bf16[96,1152]{1,0:T(8,128)(2,1)}, u32[]{:S(2)}, u32[]{:S(2)}) collective-permute-start(bf16[96,1152]{1,0:T(8,128)(2,1)S(1)} %collective-permute-done.11.refs_15_), channel_id=1, source_target_pairs={{0,96},{32,0},{64,32},{96,64},{128,224},{160,128},{192,160},{224,1... | collective-permute-start | bytes 663560 | tf_op jit(solution)/shard_map/ppermute | solution.py:45
  30.8 13.3 %collective-permute-start.17 = (bf16[96,1152]{1,0:T(8,128)(2,1)S(1)}, bf16[96,1152]{1,0:T(8,128)(2,1)}, u32[]{:S(2)}, u32[]{:S(2)}) collective-permute-start(bf16[96,1152]{1,0:T(8,128)(2,1)S(1)} %collective-permute-done.11.refs_15_), channel_id=1, source_target_pairs={{0,32},{32,64},{64,96},{96,0},{128,160},{160,192},{192,224},{224,1... | collective-permute-start | bytes 663560 | tf_op jit(solution)/shard_map/ppermute | solution.py:45
  33.9 23.0 %collective-permute-start.3 = (bf16[512,384]{1,0:T(8,128)(2,1)S(1)}, bf16[512,384]{1,0:T(8,128)(2,1)}, u32[]{:S(2)}, u32[]{:S(2)}) collective-permute-start(bf16[512,384]{1,0:T(8,128)(2,1)S(1)} %collective-permute-done.1.refs_2_), channel_id=1, source_target_pairs={{0,7},{1,0},{2,1},{3,2},{4,3},{5,4},{6,5},{7,6},{8,15},{9,8},{10,9... | collective-permute-start | bytes 1179656 | tf_op jit(solution)/shard_map/ppermute | solution.py:49
  38.8 0.7 copy-start.5
  39.5 22.5 %collective-permute-start.2 = (bf16[512,384]{1,0:T(8,128)(2,1)}, bf16[512,384]{1,0:T(8,128)(2,1)}, u32[]{:S(2)}, u32[]{:S(2)}) collective-permute-start(bf16[512,384]{1,0:T(8,128)(2,1)} %collective-permute-done.refs_1_), channel_id=1, source_target_pairs={{0,1},{1,2},{2,3},{3,4},{4,5},{5,6},{6,7},{7,0},{8,9},{9,10},{10,1... | collective-permute-start | bytes 1179656 | tf_op jit(solution)/shard_map/ppermute | solution.py:49
  41.4 5.4 %collective-permute-start.12 = (bf16[96,1152]{1,0:T(8,128)(2,1)S(1)}, bf16[96,1152]{1,0:T(8,128)(2,1)S(1)}, u32[]{:S(2)}, u32[]{:S(2)}) collective-permute-start(bf16[96,1152]{1,0:T(8,128)(2,1)S(1)} %collective-permute-done.11.refs_15_), channel_id=1, source_target_pairs={{0,128},{32,160},{64,192},{96,224},{128,0},{160,32},{192,64},{224,... | collective-permute-start | bytes 663560 | tf_op jit(solution)/shard_map/ppermute | solution.py:45
  44.1 10.2 %collective-permute-start.15 = (bf16[96,1152]{1,0:T(8,128)(2,1)S(1)}, bf16[96,1152]{1,0:T(8,128)(2,1)}, u32[]{:S(2)}, u32[]{:S(2)}) collective-permute-start(bf16[96,1152]{1,0:T(8,128)(2,1)S(1)} %collective-permute-done.9.refs_13_), channel_id=1, source_target_pairs={{0,96},{32,0},{64,32},{96,64},{128,224},{160,128},{192,160},{224,1... | collective-permute-start | bytes 663560 | tf_op jit(solution)/shard_map/ppermute | solution.py:45
  47.5 16.5 %collective-permute-start.13 = (bf16[96,1152]{1,0:T(8,128)(2,1)S(1)}, bf16[96,1152]{1,0:T(8,128)(2,1)}, u32[]{:S(2)}, u32[]{:S(2)}) collective-permute-start(bf16[96,1152]{1,0:T(8,128)(2,1)S(1)} %collective-permute-done.9.refs_13_), channel_id=1, source_target_pairs={{0,32},{32,64},{64,96},{96,0},{128,160},{160,192},{192,224},{224,1... | collective-permute-start | bytes 663560 | tf_op jit(solution)/shard_map/ppermute | solution.py:45
  54.3 12.0 %collective-permute-start.10 = (bf16[96,1152]{1,0:T(8,128)(2,1)S(1)}, bf16[96,1152]{1,0:T(8,128)(2,1)S(1)}, u32[]{:S(2)}, u32[]{:S(2)}) collective-permute-start(bf16[96,1152]{1,0:T(8,128)(2,1)S(1)} %collective-permute-done.9.refs_13_), channel_id=1, source_target_pairs={{0,128},{32,160},{64,192},{96,224},{128,0},{160,32},{192,64},{224,... | collective-permute-start | bytes 663560 | tf_op jit(solution)/shard_map/ppermute | solution.py:45
  56.9 24.8 %collective-permute-start.5 = (bf16[512,384]{1,0:T(8,128)(2,1)}, bf16[512,384]{1,0:T(8,128)(2,1)S(1)}, u32[]{:S(2)}, u32[]{:S(2)}) collective-permute-start(bf16[512,384]{1,0:T(8,128)(2,1)} %collective-permute-done.3.refs_4_), channel_id=1, source_target_pairs={{0,7},{1,0},{2,1},{3,2},{4,3},{5,4},{6,5},{7,6},{8,15},{9,8},{10,9... | collective-permute-start | bytes 1179656 | tf_op jit(solution)/shard_map/ppermute | solution.py:49
  62.0 22.1 %collective-permute-start.4 = (bf16[512,384]{1,0:T(8,128)(2,1)}, bf16[512,384]{1,0:T(8,128)(2,1)S(1)}, u32[]{:S(2)}, u32[]{:S(2)}) collective-permute-start(bf16[512,384]{1,0:T(8,128)(2,1)} %collective-permute-done.2.refs_3_), channel_id=1, source_target_pairs={{0,1},{1,2},{2,3},{3,4},{4,5},{5,6},{6,7},{7,0},{8,9},{9,10},{10,1... | collective-permute-start | bytes 1179656 | tf_op jit(solution)/shard_map/ppermute | solution.py:49
  64.0 11.0 %collective-permute-start.23 = (bf16[96,1152]{1,0:T(8,128)(2,1)}, bf16[96,1152]{1,0:T(8,128)(2,1)}, u32[]{:S(2)}, u32[]{:S(2)}) collective-permute-start(bf16[96,1152]{1,0:T(8,128)(2,1)} %collective-permute-done.19.refs_23_), channel_id=1, source_target_pairs={{0,96},{32,0},{64,32},{96,64},{128,224},{160,128},{192,160},{224,1... | collective-permute-start | bytes 663560 | tf_op jit(solution)/shard_map/ppermute | solution.py:45
  66.3 0.7 copy-start.13
  67.0 12.8 %collective-permute-start.20 = (bf16[96,1152]{1,0:T(8,128)(2,1)}, bf16[96,1152]{1,0:T(8,128)(2,1)}, u32[]{:S(2)}, u32[]{:S(2)}) collective-permute-start(bf16[96,1152]{1,0:T(8,128)(2,1)} %collective-permute-done.19.refs_23_), channel_id=1, source_target_pairs={{0,128},{32,160},{64,192},{96,224},{128,0},{160,32},{192,64},{224,... | collective-permute-start | bytes 663560 | tf_op jit(solution)/shard_map/ppermute | solution.py:45
  74.9 14.8 %collective-permute-start.21 = (bf16[96,1152]{1,0:T(8,128)(2,1)}, bf16[96,1152]{1,0:T(8,128)(2,1)}, u32[]{:S(2)}, u32[]{:S(2)}) collective-permute-start(bf16[96,1152]{1,0:T(8,128)(2,1)} %collective-permute-done.13.refs_17_), channel_id=1, source_target_pairs={{0,32},{32,64},{64,96},{96,0},{128,160},{160,192},{192,224},{224,1... | collective-permute-start | bytes 663560 | tf_op jit(solution)/shard_map/ppermute | solution.py:45
  79.8 16.7 %collective-permute-start.14 = (bf16[96,1152]{1,0:T(8,128)(2,1)}, bf16[96,1152]{1,0:T(8,128)(2,1)}, u32[]{:S(2)}, u32[]{:S(2)}) collective-permute-start(bf16[96,1152]{1,0:T(8,128)(2,1)} %collective-permute-done.13.refs_17_), channel_id=1, source_target_pairs={{0,128},{32,160},{64,192},{96,224},{128,0},{160,32},{192,64},{224,... | collective-permute-start | bytes 663560 | tf_op jit(solution)/shard_map/ppermute | solution.py:45
  81.7 5.5 %collective-permute-start.18 = (bf16[96,1152]{1,0:T(8,128)(2,1)}, bf16[96,1152]{1,0:T(8,128)(2,1)}, u32[]{:S(2)}, u32[]{:S(2)}) collective-permute-start(bf16[96,1152]{1,0:T(8,128)(2,1)} %collective-permute-done.17.refs_21_), channel_id=1, source_target_pairs={{0,128},{32,160},{64,192},{96,224},{128,0},{160,32},{192,64},{224,... | collective-permute-start | bytes 663560 | tf_op jit(solution)/shard_map/ppermute | solution.py:45
  84.2 22.5 %copy-start.2 = (bf16[512,384]{1,0:T(8,128)(2,1)}, bf16[512,384]{1,0:T(8,128)(2,1)S(1)}, u32[]{:S(2)}) copy-start(bf16[512,384]{1,0:T(8,128)(2,1)S(1)} %collective-permute-done.4.refs_5_) | copy-start | bytes 1179652
  84.2 7.5 %collective-permute-start.16 = (bf16[96,1152]{1,0:T(8,128)(2,1)}, bf16[96,1152]{1,0:T(8,128)(2,1)}, u32[]{:S(2)}, u32[]{:S(2)}) collective-permute-start(bf16[96,1152]{1,0:T(8,128)(2,1)} %collective-permute-done.15.refs_19_), channel_id=1, source_target_pairs={{0,128},{32,160},{64,192},{96,224},{128,0},{160,32},{192,64},{224,... | collective-permute-start | bytes 663560 | tf_op jit(solution)/shard_map/ppermute | solution.py:45
  87.3 11.3 %collective-permute-start.24 = (bf16[96,1152]{1,0:T(8,128)(2,1)}, bf16[96,1152]{1,0:T(8,128)(2,1)S(1)}, u32[]{:S(2)}, u32[]{:S(2)}) collective-permute-start(bf16[96,1152]{1,0:T(8,128)(2,1)} %collective-permute-done.23.refs_27_), channel_id=1, source_target_pairs={{0,128},{32,160},{64,192},{96,224},{128,0},{160,32},{192,64},{224,... | collective-permute-start | bytes 663560 | tf_op jit(solution)/shard_map/ppermute | solution.py:45
  89.7 8.9 %collective-permute-start.22 = (bf16[96,1152]{1,0:T(8,128)(2,1)}, bf16[96,1152]{1,0:T(8,128)(2,1)S(1)}, u32[]{:S(2)}, u32[]{:S(2)}) collective-permute-start(bf16[96,1152]{1,0:T(8,128)(2,1)} %collective-permute-done.21.refs_25_), channel_id=1, source_target_pairs={{0,128},{32,160},{64,192},{96,224},{128,0},{160,32},{192,64},{224,... | collective-permute-start | bytes 663560 | tf_op jit(solution)/shard_map/ppermute | solution.py:45
  91.6 9.7 %collective-permute-start.7 = (bf16[256,384]{1,0:T(8,128)(2,1)S(1)}, bf16[256,384]{1,0:T(8,128)(2,1)S(1)}, u32[]{:S(2)}, u32[]{:S(2)}) collective-permute-start(bf16[256,384]{1,0:T(8,128)(2,1)S(1)} %slice.9), channel_id=1, source_target_pairs={{0,7},{1,0},{2,1},{3,2},{4,3},{5,4},{6,5},{7,6},{8,15},{9,8},{10,9... | collective-permute-start | bytes 589832 | tf_op jit(solution)/shard_map/ppermute | solution.py:49
  96.5 10.1 %collective-permute-start.6 = (bf16[256,384]{1,0:T(8,128)(2,1)S(1)}, bf16[256,384]{1,0:T(8,128)(2,1)S(1)}, u32[]{:S(2)}, u32[]{:S(2)}) collective-permute-start(bf16[256,384]{1,0:T(8,128)(2,1)S(1)} %slice.8), channel_id=1, source_target_pairs={{0,1},{1,2},{2,3},{3,4},{4,5},{5,6},{6,7},{7,0},{8,9},{9,10},{10,1... | collective-permute-start | bytes 589832 | tf_op jit(solution)/shard_map/ppermute | solution.py:49
  98.4 78.6 %copy-start.16 = (s32[1,4,4]{2,1,0:T(4,128)S(1)}, s32[1,4,4]{2,1,0:T(4,128)}, u32[]{:S(2)}) copy-start(s32[1,4,4]{2,1,0:T(4,128)} %param.12) | copy-start | bytes 196
  98.5 81.2 %copy-start.15 = (s32[1,4]{1,0:T(1,128)S(1)}, s32[1,4]{1,0:T(1,128)}, u32[]{:S(2)}) copy-start(s32[1,4]{1,0:T(1,128)} %param.11) | copy-start | bytes 52
  106.6 1.0 copy-start.3
  107.6 1.0 copy-start.4
  108.6 1.0 copy-start.6
  109.6 0.9 copy-start.8
  110.6 0.9 copy-start.10
  111.5 0.9 copy-start.12
  112.4 0.9 copy-start.14
  124.9 23.9 %collective-permute-start.27 = (bf16[256,768]{1,0:T(8,128)(2,1)}, bf16[256,768]{1,0:T(8,128)(2,1)S(1)}, u32[]{:S(2)}, u32[]{:S(2)}) collective-permute-start(bf16[256,768]{1,0:T(8,128)(2,1)} %get-tuple-element.11.lo), channel_id=1, source_target_pairs={{0,16},{32,48},{64,80},{96,112},{128,144},{160,176},{192,208},{224... | collective-permute-start | bytes 1179656 | tf_op jit(solution)/shard_map/ppermute | solution.py:45
  126.2 24.5 %collective-permute-start.29 = (bf16[256,768]{1,0:T(8,128)(2,1)}, bf16[256,768]{1,0:T(8,128)(2,1)S(1)}, u32[]{:S(2)}, u32[]{:S(2)}) collective-permute-start(bf16[256,768]{1,0:T(8,128)(2,1)} %get-tuple-element.12.hi), channel_id=1, source_target_pairs={{0,272},{32,304},{64,336},{96,368},{128,400},{160,432},{192,464},{... | collective-permute-start | bytes 1179656 | tf_op jit(solution)/shard_map/ppermute | solution.py:45
  148.8 23.9 %collective-permute-start.28 = (bf16[256,768]{1,0:T(8,128)(2,1)S(1)}, bf16[256,768]{1,0:T(8,128)(2,1)S(1)}, u32[]{:S(2)}, u32[]{:S(2)}) collective-permute-start(bf16[256,768]{1,0:T(8,128)(2,1)S(1)} %collective-permute-done.27), channel_id=1, source_target_pairs={{16,256},{48,288},{80,320},{112,352},{144,384},{176,416},{208,448}... | collective-permute-start | bytes 1179656 | tf_op jit(solution)/shard_map/ppermute | solution.py:45
  150.7 23.9 %collective-permute-start.30 = (bf16[256,768]{1,0:T(8,128)(2,1)S(1)}, bf16[256,768]{1,0:T(8,128)(2,1)S(1)}, u32[]{:S(2)}, u32[]{:S(2)}) collective-permute-start(bf16[256,768]{1,0:T(8,128)(2,1)S(1)} %collective-permute-done.29), channel_id=1, source_target_pairs={{0,272},{32,304},{64,336},{96,368},{128,400},{160,432},{192,464},{... | collective-permute-start | bytes 1179656 | tf_op jit(solution)/shard_map/ppermute | solution.py:45
  152.0 30.9 %collective-permute-start.25 = (bf16[256,768]{1,0:T(8,128)(2,1)}, bf16[256,768]{1,0:T(8,128)(2,1)S(1)}, u32[]{:S(2)}, u32[]{:S(2)}) collective-permute-start(bf16[256,768]{1,0:T(8,128)(2,1)} %get-tuple-element.11.lo), channel_id=1, source_target_pairs={{0,128},{32,160},{64,192},{96,224},{128,0},{160,32},{192,64},{224,... | collective-permute-start | bytes 1179656 | tf_op jit(solution)/shard_map/ppermute | solution.py:45
  153.9 28.9 %collective-permute-start.26 = (bf16[256,768]{1,0:T(8,128)(2,1)}, bf16[256,768]{1,0:T(8,128)(2,1)S(1)}, u32[]{:S(2)}, u32[]{:S(2)}) collective-permute-start(bf16[256,768]{1,0:T(8,128)(2,1)} %get-tuple-element.12.hi), channel_id=1, source_target_pairs={{0,128},{32,160},{64,192},{96,224},{128,0},{160,32},{192,64},{224,... | collective-permute-start | bytes 1179656 | tf_op jit(solution)/shard_map/ppermute | solution.py:45
  172.6 13.0 %collective-permute-start.31 = (bf16[256,768]{1,0:T(8,128)(2,1)S(1)}, bf16[256,768]{1,0:T(8,128)(2,1)S(1)}, u32[]{:S(2)}, u32[]{:S(2)}) collective-permute-start(bf16[256,768]{1,0:T(8,128)(2,1)S(1)} %collective-permute-done.28.lo), channel_id=1, source_target_pairs={{0,128},{32,160},{64,192},{96,224},{128,0},{160,32},{192,64},{224,... | collective-permute-start | bytes 1179656 | tf_op jit(solution)/shard_map/ppermute | solution.py:45
  174.6 11.1 %collective-permute-start.32 = (bf16[256,768]{1,0:T(8,128)(2,1)S(1)}, bf16[256,768]{1,0:T(8,128)(2,1)S(1)}, u32[]{:S(2)}, u32[]{:S(2)}) collective-permute-start(bf16[256,768]{1,0:T(8,128)(2,1)S(1)} %collective-permute-done.30.hi), channel_id=1, source_target_pairs={{0,128},{32,160},{64,192},{96,224},{128,0},{160,32},{192,64},{224,... | collective-permute-start | bytes 1179656 | tf_op jit(solution)/shard_map/ppermute | solution.py:45
  (3 other events, 2.1 us)

commit v2 on v1

v2 whole, which is shorter than its diff:
```python
import math

import jax
import jax.numpy as jnp
from jax import lax
from jax.experimental import pallas as pl
from jax.experimental.pallas import tpu as pltpu
from jax.sharding import PartitionSpec as P

HD = 128
TPF = 64
EPS = 1e-06
MIB = 1 << 20

HALVES, CORES, XS, YS = 2, 2, 4, 4
RING_Y = HALVES * YS


def place(y, core, x):
    return ((y // YS) * CORES + core) * (XS * YS) + x * YS + y % YS


def pairs(move, keep=lambda y: True):
    out = []
    for y in range(RING_Y):
        for core in range(CORES):
            for x in range(XS):
                if keep(y):
                    out.append((place(y, core, x), place(*move(y, core, x))))
    return out


MIRROR = pairs(lambda y, core, x: (RING_Y - 1 - y, core, x))
X_RING = pairs(lambda y, core, x: (y, core, (x + 1 - 2 * core) % XS))
SWAP = pairs(lambda y, core, x: (y, 1 - core, x))
UP_FIRST = pairs(lambda y, core, x: (y + 2, core, x), lambda y: y < 4)
UP_SECOND = pairs(lambda y, core, x: (y + 2, core, x), lambda y: 2 <= y < 6)
DOWN_FIRST = pairs(lambda y, core, x: ((y - 2) % 8, core, x), lambda y: y < 4)
DOWN_SECOND = pairs(lambda y, core, x: (y - 2 if y >= 6 else y + 6, core, x), lambda y: y >= 6 or y < 2)


def move(array, table):
    return lax.ppermute(array, ("block", "req"), table)


def turn(array, step, size):
    return lax.ppermute(array, "head", [(i, (i + step) % size) for i in range(size)])


def gather_kernel(spots, levels, *refs):
    (own, r1, l1, r2, l2, r3, l3, r4, l4, mod, w_own, w_pair, w_rest) = refs[:13]
    acc, last_columns, normed = refs[13:]
    rows, depth = own.shape
    half = rows // 2
    features = normed.shape[1]
    step_rows = 64
    level = levels[0, 0]

    for side, last in ((0, r4), (1, l4)):
        def norm_rows(step, carry, side=side, last=last):
            inner = pl.multiple_of(step * step_rows, step_rows)
            outer = pl.multiple_of(side * half + step * step_rows, step_rows)
            views = [ref.at[pl.ds(outer, step_rows), :] for ref in (own, r1, l1, r2, l2, r3, l3)]
            views.append(last.at[pl.ds(inner, step_rows), :])
            total = jnp.zeros((step_rows, 128), jnp.float32)
            for view in views:
                wide = view[...].astype(jnp.float32)
                square = wide * wide
                for lane in range(0, depth, 128):
                    total = total + square[:, lane : lane + 128]
            scale = lax.rsqrt(jnp.sum(total, axis=-1, keepdims=True) * (1.0 / features) + EPS)
            for number, view in enumerate(views):
                column = pl.multiple_of(spots[number] * depth, 128)
                wide = view[...].astype(jnp.float32)
                gain = 1.0 + mod[level, 0:1, pl.ds(column, depth)]
                row = wide * scale * gain + mod[level, 1:2, pl.ds(column, depth)]
                normed[pl.ds(outer, step_rows), pl.ds(column, depth)] = row.astype(jnp.bfloat16)
            return carry

        lax.fori_loop(0, half // step_rows, norm_rows, 0)

    part = w_own.shape[0]
    columns = acc.shape[1]

    def block_of(number):
        return normed[:, pl.ds(pl.multiple_of(spots[8 + number] * part, 128), part)]

    for start in range(0, columns, 512):
        span = slice(start, min(start + 512, columns))
        total = jnp.dot(block_of(0), w_own[:, span], preferred_element_type=jnp.float32)
        total += jnp.dot(block_of(1), w_pair[:, span], preferred_element_type=jnp.float32)
        total += jnp.dot(block_of(2), w_rest[:, span], preferred_element_type=jnp.float32)
        acc[:, span] = total
    last_columns[...] = block_of(3)


def project_kernel(acc, last_columns, w_last, q_gain, k_gain, q_out, kv_out):
    heads = q_out.shape[1] // HD

    def head_norm(part, gain):
        scale = lax.rsqrt(jnp.mean(part * part, axis=-1, keepdims=True) + EPS)
        return (part * scale * gain).astype(jnp.bfloat16)

    for head in range(heads):
        span = slice(3 * HD * head, 3 * HD * (head + 1))
        out = acc[:, span] + jnp.dot(last_columns[...], w_last[:, span], preferred_element_type=jnp.float32)
        q_out[:, HD * head : HD * (head + 1)] = head_norm(out[:, :HD], q_gain[...])
        kv_out[:, HD * head : HD * (head + 1)] = head_norm(out[:, HD : 2 * HD], k_gain[...])
        kv_out[:, HD * (heads + head) : HD * (heads + head + 1)] = out[:, 2 * HD :].astype(jnp.bfloat16)


def key_limit(spots, frames, mask, number):
    block, segment = spots[8], spots[8 + number]
    seen = (segment == block) | ((segment < block) & (mask[block, segment] == 1))
    return jnp.where(seen, frames[0, segment] * TPF, 0)


def attend_part(limit, first, q, kv, num, den, heads):
    rows = 256
    keys = kv.shape[0]
    column = lax.broadcasted_iota(jnp.int32, (1, keys), 1) + first
    keep = column < limit
    factor = HD ** (-0.5) * math.log2(math.e)
    for head in range(heads):
        span = slice(HD * head, HD * (head + 1))
        k = kv[:, span]
        v = kv[:, HD * (heads + head) : HD * (heads + head + 1)]
        for top in range(0, q.shape[0], rows):
            band = slice(top, top + rows)
            scores = lax.dot_general(
                q[band, span], k, (((1,), (1,)), ((), ())), preferred_element_type=jnp.float32
            )
            weights = jnp.where(keep, jnp.exp2(scores * factor), 0.0)
            total = weights[:, :128]
            for lane in range(128, keys, 128):
                total = total + weights[:, lane : lane + 128]
            den[band, span] += total
            num[band, span] += jnp.dot(weights.astype(jnp.bfloat16), v, preferred_element_type=jnp.float32)


def near_kernel(spots, frames, mask, q, own, pair, num, den):
    heads = q.shape[1] // HD
    half = q.shape[0] // 2
    num[...] = jnp.zeros_like(num)
    den[...] = jnp.zeros_like(den)
    for number, kv in ((0, own), (1, pair)):
        limit = key_limit(spots, frames, mask, number)
        for first in (0, half):
            @pl.when(limit > first)
            def _(limit=limit, first=first, kv=kv):
                attend_part(limit, first, q, kv.at[first : first + half], num, den, heads)


def far_kernel(number, finish, spots, frames, mask, q, num_in, den_in, lo, hi, *rest):
    heads = q.shape[1] // HD
    half = q.shape[0] // 2
    num, den = rest[-2:]
    num[...] = num_in[...]
    den[...] = den_in[...]
    limit = key_limit(spots, frames, mask, number)
    for first, kv in ((0, lo), (half, hi)):
        @pl.when(limit > first)
        def _(first=first, kv=kv):
            attend_part(limit, first, q, kv, num, den, heads)
    if finish:
        for head in range(heads):
            span = slice(HD * head, HD * (head + 1))
            total = jnp.sum(den[:, span], axis=-1, keepdims=True)
            rest[0][:, span] = (num[:, span] / total).astype(jnp.bfloat16)


def body(tokens, levels, frames, segment_mask, mod_table, w_qkv, q_gain, k_gain):
    own = tokens[0, 0]
    rows, depth = own.shape
    ring = mod_table.shape[2] // depth
    part_rows, columns = w_qkv.shape
    heads = columns // (3 * HD)
    width = heads * HD
    quarter = part_rows // XS
    half = rows // 2

    z = lax.axis_index("head")
    block = lax.axis_index("block")
    side, core = block // CORES, block % CORES
    x = lax.axis_index("req") // YS

    piece = move(lax.dynamic_slice_in_dim(w_qkv, quarter * x, quarter), MIRROR)
    r1, l1 = turn(own, 1, ring), turn(own, -1, ring)
    w_pair = move(w_qkv, SWAP)
    r1, l1, w_pair = lax.optimization_barrier((r1, l1, w_pair))
    r2, l2 = turn(r1, 1, ring), turn(l1, -1, ring)
    piece, r2, l2 = lax.optimization_barrier((piece, r2, l2))
    held = [piece, move(piece, X_RING)]
    r3, l3 = turn(r2, 1, ring), turn(l2, -1, ring)
    held[1], r3, l3 = lax.optimization_barrier((held[1], r3, l3))
    held.append(move(held[1], X_RING))
    r4, l4 = turn(r3[:half], 1, ring), turn(l3[half:], -1, ring)
    held.append(move(held[2], X_RING))
    w_rest = jnp.zeros_like(w_qkv)
    for step, piece in enumerate(held):
        at = (x + (2 * core - 1) * step + XS) % XS
        w_rest = lax.dynamic_update_slice_in_dim(w_rest, piece, at * quarter, 0)
    w_rest, r4, l4 = lax.optimization_barrier((w_rest, r4, l4))
    w_last = move(w_rest, SWAP)

    order = [z, z - 1, z + 1, z - 2, z + 2, z - 3, z + 3, z + 4]
    spots = [(item + ring) % ring for item in order]
    other = (1 - side) * CORES
    spots += [block, side * CORES + 1 - core, other + core, other + 1 - core]
    spots = jnp.stack(spots).astype(jnp.int32)

    smem = pl.BlockSpec(memory_space=pltpu.SMEM)
    vmem = pl.BlockSpec(memory_space=pltpu.VMEM)

    def sized(limit):
        return pltpu.CompilerParams(vmem_limit_bytes=limit * MIB)

    acc, last_columns = pl.pallas_call(
        gather_kernel,
        out_shape=(
            jax.ShapeDtypeStruct((rows, columns), jnp.float32),
            jax.ShapeDtypeStruct((rows, part_rows), jnp.bfloat16),
        ),
        in_specs=[smem] * 2 + [vmem] * 13,
        out_specs=(vmem, vmem),
        scratch_shapes=[pltpu.VMEM((rows, ring * depth), jnp.bfloat16)],
        compiler_params=sized(32),
        cost_estimate=pl.CostEstimate(
            flops=2 * rows * 3 * part_rows * columns, bytes_accessed=12 * MIB, transcendentals=0
        ),
        name="gather",
    )(spots, levels, own, r1, l1, r2, l2, r3, l3, r4, l4, mod_table, w_qkv, w_pair, w_rest)
    queries, kv = pl.pallas_call(
        project_kernel,
        out_shape=(
            jax.ShapeDtypeStruct((rows, width), jnp.bfloat16),
            jax.ShapeDtypeStruct((rows, 2 * width), jnp.bfloat16),
        ),
        in_specs=[vmem] * 5,
        out_specs=(vmem, vmem),
        compiler_params=sized(24),
        cost_estimate=pl.CostEstimate(
            flops=2 * rows * part_rows * columns, bytes_accessed=6 * MIB, transcendentals=0
        ),
        name="project",
    )(acc, last_columns, w_last, q_gain[None, :], k_gain[None, :])

    far_lo = move(kv[:half], UP_FIRST)
    far_hi = move(kv[half:], DOWN_FIRST)
    pair_kv = move(kv, SWAP)

    where = (spots, frames, segment_mask[0])
    sums = (jax.ShapeDtypeStruct((rows, width), jnp.float32),) * 2
    work = pl.CostEstimate(
        flops=8 * rows * rows * width, bytes_accessed=6 * MIB, transcendentals=2 * rows * rows * heads
    )
    num, den = pl.pallas_call(
        near_kernel,
        out_shape=sums,
        in_specs=[smem] * 3 + [vmem] * 3,
        out_specs=(vmem, vmem),
        compiler_params=sized(24),
        cost_estimate=work,
        name="near",
    )(*where, queries, kv, pair_kv)
    far_lo, far_hi, num, den = lax.optimization_barrier((far_lo, far_hi, num, den))
    far_lo = move(far_lo, UP_SECOND)
    far_hi = move(far_hi, DOWN_SECOND)
    far_kv = lax.optimization_barrier(jnp.concatenate([far_lo, far_hi]))
    far_pair = move(far_kv, SWAP)
    num, den = pl.pallas_call(
        lambda *refs: far_kernel(2, False, *refs),
        out_shape=sums,
        in_specs=[smem] * 3 + [vmem] * 5,
        out_specs=(vmem, vmem),
        compiler_params=sized(24),
        cost_estimate=work,
        name="far",
    )(*where, queries, num, den, far_lo, far_hi)
    result = pl.pallas_call(
        lambda *refs: far_kernel(3, True, *refs),
        out_shape=jax.ShapeDtypeStruct((rows, width), jnp.bfloat16),
        in_specs=[smem] * 3 + [vmem] * 5,
        out_specs=vmem,
        scratch_shapes=[pltpu.VMEM((rows, width), jnp.float32)] * 2,
        compiler_params=sized(24),
        cost_estimate=work,
        name="last",
    )(*where, queries, num, den, far_pair[:half], far_pair[half:])
    return result.reshape(1, 1, rows, width)


def solution(mesh):
    placed = (
        P("req", "block", None, "head"),
        P("req", "block"),
        P("req", None),
        P("req", None, None),
        P(),
        P("block", "head"),
        P(),
        P(),
    )
    return jax.shard_map(
        body, mesh=mesh, in_specs=placed, out_specs=P("req", "block", None, "head"), check_vma=False
    )
```

time: 192 us -> 170 us (0.89)
  the two profiles are of different devices: /device:TPU:44 before, /device:TPU:41 now
where the time goes in v2:
time: 170 us; the launch traced here: 169 us
  starting transfers between devices  67.2 us (40%)
  waiting for transfers between devices  64.8 us (38%)
  local copies, waits for them, and re-layouts  21.1 us (12%)
  Pallas kernels  14.6 us (9%)
    ppermute x12, waiting for transfers between devices, move(): return lax.ppermute(array, ('block', 'req'), table)  44.3 us
    ppermute x12, starting transfers between devices, move(): return lax.ppermute(array, ('block', 'req'), table)  33.6 us
    ppermute x8, starting transfers between devices, turn(): lax.ppermute(array, 'head', [(i, (i + step) % size) for i in range(size)])  33.5 us
    ppermute x8, waiting for transfers between devices, turn(): lax.ppermute(array, 'head', [(i, (i + step) % size) for i in range(size)])  20.5 us
    unnamed x50, local copies, waits for them, and re-layouts  18.5 us
    pallas_call x1, Pallas kernels, body(): pl.pallas_call(gather_kernel, out_shape=(jax.ShapeDtypeStruct((rows, colu...  5.78 us
  transfers between devices with their start and end apart: 20, of which 12 were waited for; matrix products, arithmetic and copies ran while one was open for 2% of the time, Pallas kernels for 6%

profile of v2, /device:TPU:41, one launch (start us, length us, event | category | flops | bytes accessed | tf_op | source)
XLA Modules:
  0.0 169.0 jit_solution(11883353613992482577)
XLA Ops:
  0.0 2.6 %collective-permute-start.2 = (bf16[768,1152]{1,0:T(8,128)(2,1)}, bf16[768,1152]{1,0:T(8,128)(2,1)S(1)}, u32[]{:S(2)}, u32[]{:S(2)}) collective-permute-start(bf16[768,1152]{1,0:T(8,128)(2,1)} %refs_10_.1), channel_id=1, source_target_pairs={{0,128},{32,160},{64,192},{96,224},{128,0},{160,32},{192,64},{224,... | collective-permute-start | bytes 5308424 | tf_op jit(solution)/shard_map/ppermute | solution.py:43
  2.6 10.7 %collective-permute-start.1 = (bf16[512,384]{1,0:T(8,128)(2,1)}, bf16[512,384]{1,0:T(8,128)(2,1)S(1)}, u32[]{:S(2)}, u32[]{:S(2)}) collective-permute-start(bf16[512,384]{1,0:T(8,128)(2,1)} %bitcast.22), channel_id=1, source_target_pairs={{0,7},{1,0},{2,1},{3,2},{4,3},{5,4},{6,5},{7,6},{8,15},{9,8},{10,9... | collective-permute-start | bytes 1179656 | tf_op jit(solution)/shard_map/ppermute | solution.py:47
  13.3 1.9 %collective-permute-start = (bf16[512,384]{1,0:T(8,128)(2,1)}, bf16[512,384]{1,0:T(8,128)(2,1)S(1)}, u32[]{:S(2)}, u32[]{:S(2)}) collective-permute-start(bf16[512,384]{1,0:T(8,128)(2,1)} %bitcast.23), channel_id=1, source_target_pairs={{0,1},{1,2},{2,3},{3,4},{4,5},{5,6},{6,7},{7,0},{8,9},{9,10},{10,1... | collective-permute-start | bytes 1179656 | tf_op jit(solution)/shard_map/ppermute | solution.py:47
  15.2 1.1 constant_dynamic-slice_fusion
  16.3 2.7 %collective-permute-start.3 = (bf16[192,1152]{1,0:T(8,128)(2,1)S(1)}, bf16[192,1152]{1,0:T(8,128)(2,1)S(1)}, u32[]{:S(2)}, u32[]{:S(2)}) collective-permute-start(bf16[192,1152]{1,0:T(8,128)(2,1)S(1)} %constant_dynamic-slice_fusion), channel_id=1, source_target_pairs={{0,280},{32,312},{64,344},{96,376},{128,408},{160,440},{192,472},{... | collective-permute-start | bytes 1327112 | tf_op jit(solution)/shard_map/ppermute | solution.py:43
  19.0 3.1 %collective-permute-done.1.refs_2_ = bf16[512,384]{1,0:T(8,128)(2,1)S(1)} collective-permute-done((bf16[512,384]{1,0:T(8,128)(2,1)}, bf16[512,384]{1,0:T(8,128)(2,1)S(1)}, u32[]{:S(2)}, u32[]{:S(2)}) %collective-permute-start.1) | collective-permute-done | bytes 393248 | tf_op jit(solution)/shard_map/ppermute | solution.py:47
  22.1 4.9 %collective-permute-done.refs_1_ = bf16[512,384]{1,0:T(8,128)(2,1)S(1)} collective-permute-done((bf16[512,384]{1,0:T(8,128)(2,1)}, bf16[512,384]{1,0:T(8,128)(2,1)S(1)}, u32[]{:S(2)}, u32[]{:S(2)}) %collective-permute-start) | collective-permute-done | bytes 393248 | tf_op jit(solution)/shard_map/ppermute | solution.py:47
  27.0 1.3 copy-done.9
  28.3 1.9 %collective-permute-start.4 = (bf16[512,384]{1,0:T(8,128)(2,1)S(1)}, bf16[512,384]{1,0:T(8,128)(2,1)S(1)}, u32[]{:S(2)}, u32[]{:S(2)}) collective-permute-start(bf16[512,384]{1,0:T(8,128)(2,1)S(1)} %collective-permute-done.refs_1_), channel_id=1, source_target_pairs={{0,1},{1,2},{2,3},{3,4},{4,5},{5,6},{6,7},{7,0},{8,9},{9,10},{10,1... | collective-permute-start | bytes 1179656 | tf_op jit(solution)/shard_map/ppermute | solution.py:47
  30.9 4.6 %collective-permute-start.5 = (bf16[512,384]{1,0:T(8,128)(2,1)S(1)}, bf16[512,384]{1,0:T(8,128)(2,1)S(1)}, u32[]{:S(2)}, u32[]{:S(2)}) collective-permute-start(bf16[512,384]{1,0:T(8,128)(2,1)S(1)} %collective-permute-done.1.refs_2_), channel_id=1, source_target_pairs={{0,7},{1,0},{2,1},{3,2},{4,3},{5,4},{6,5},{7,6},{8,15},{9,8},{10,9... | collective-permute-start | bytes 1179656 | tf_op jit(solution)/shard_map/ppermute | solution.py:47
  36.3 4.6 %collective-permute-done.4.refs_3_ = bf16[512,384]{1,0:T(8,128)(2,1)S(1)} collective-permute-done((bf16[512,384]{1,0:T(8,128)(2,1)S(1)}, bf16[512,384]{1,0:T(8,128)(2,1)S(1)}, u32[]{:S(2)}, u32[]{:S(2)}) %collective-permute-start.4) | collective-permute-done | bytes 393248 | tf_op jit(solution)/shard_map/ppermute | solution.py:47
  40.8 1.6 collective-permute-done.5.refs_4_
  42.5 4.4 %collective-permute-start.6 = (bf16[192,1152]{1,0:T(8,128)(2,1)S(1)}, bf16[192,1152]{1,0:T(8,128)(2,1)S(1)}, u32[]{:S(2)}, u32[]{:S(2)}) collective-permute-start(bf16[192,1152]{1,0:T(8,128)(2,1)S(1)} %collective-permute-done.3), channel_id=1, source_target_pairs={{0,32},{32,64},{64,96},{96,0},{128,224},{160,128},{192,160},{224,1... | collective-permute-start | bytes 1327112 | tf_op jit(solution)/shard_map/ppermute | solution.py:43
  46.9 1.9 %collective-permute-start.7 = (bf16[512,384]{1,0:T(8,128)(2,1)S(1)}, bf16[512,384]{1,0:T(8,128)(2,1)S(1)}, u32[]{:S(2)}, u32[]{:S(2)}) collective-permute-start(bf16[512,384]{1,0:T(8,128)(2,1)S(1)} %collective-permute-done.4.refs_3_), channel_id=1, source_target_pairs={{0,1},{1,2},{2,3},{3,4},{4,5},{5,6},{6,7},{7,0},{8,9},{9,10},{10,1... | collective-permute-start | bytes 1179656 | tf_op jit(solution)/shard_map/ppermute | solution.py:47
  49.5 5.3 %collective-permute-start.8 = (bf16[512,384]{1,0:T(8,128)(2,1)S(1)}, bf16[512,384]{1,0:T(8,128)(2,1)S(1)}, u32[]{:S(2)}, u32[]{:S(2)}) collective-permute-start(bf16[512,384]{1,0:T(8,128)(2,1)S(1)} %collective-permute-done.5.refs_4_), channel_id=1, source_target_pairs={{0,7},{1,0},{2,1},{3,2},{4,3},{5,4},{6,5},{7,6},{8,15},{9,8},{10,9... | collective-permute-start | bytes 1179656 | tf_op jit(solution)/shard_map/ppermute | solution.py:47
  55.6 4.7 %collective-permute-done.7.refs_5_ = bf16[512,384]{1,0:T(8,128)(2,1)S(1)} collective-permute-done((bf16[512,384]{1,0:T(8,128)(2,1)S(1)}, bf16[512,384]{1,0:T(8,128)(2,1)S(1)}, u32[]{:S(2)}, u32[]{:S(2)}) %collective-permute-start.7) | collective-permute-done | bytes 393248 | tf_op jit(solution)/shard_map/ppermute | solution.py:47
  60.3 1.6 collective-permute-done.8.refs_6_
  61.9 1.9 %collective-permute-start.9 = (bf16[192,1152]{1,0:T(8,128)(2,1)S(1)}, bf16[192,1152]{1,0:T(8,128)(2,1)}, u32[]{:S(2)}, u32[]{:S(2)}) collective-permute-start(bf16[192,1152]{1,0:T(8,128)(2,1)S(1)} %collective-permute-done.6), channel_id=1, source_target_pairs={{0,32},{32,64},{64,96},{96,0},{128,224},{160,128},{192,160},{224,1... | collective-permute-start | bytes 1327112 | tf_op jit(solution)/shard_map/ppermute | solution.py:43
  64.2 5.3 %collective-permute-start.12 = (bf16[256,384]{1,0:T(8,128)(2,1)S(1)}, bf16[256,384]{1,0:T(8,128)(2,1)S(1)}, u32[]{:S(2)}, u32[]{:S(2)}) collective-permute-start(bf16[256,384]{1,0:T(8,128)(2,1)S(1)} %slice.19), channel_id=1, source_target_pairs={{0,7},{1,0},{2,1},{3,2},{4,3},{5,4},{6,5},{7,6},{8,15},{9,8},{10,9... | collective-permute-start | bytes 589832 | tf_op jit(solution)/shard_map/ppermute | solution.py:47
  69.6 1.9 %collective-permute-start.11 = (bf16[256,384]{1,0:T(8,128)(2,1)S(1)}, bf16[256,384]{1,0:T(8,128)(2,1)S(1)}, u32[]{:S(2)}, u32[]{:S(2)}) collective-permute-start(bf16[256,384]{1,0:T(8,128)(2,1)S(1)} %slice.18), channel_id=1, source_target_pairs={{0,1},{1,2},{2,3},{3,4},{4,5},{5,6},{6,7},{7,0},{8,9},{9,10},{10,1... | collective-permute-start | bytes 589832 | tf_op jit(solution)/shard_map/ppermute | solution.py:47
  71.5 2.7 %collective-permute-start.10 = (bf16[192,1152]{1,0:T(8,128)(2,1)}, bf16[192,1152]{1,0:T(8,128)(2,1)S(1)}, u32[]{:S(2)}, u32[]{:S(2)}) collective-permute-start(bf16[192,1152]{1,0:T(8,128)(2,1)} %collective-permute-done.9), channel_id=1, source_target_pairs={{0,32},{32,64},{64,96},{96,0},{128,224},{160,128},{192,160},{224,1... | collective-permute-start | bytes 1327112 | tf_op jit(solution)/shard_map/ppermute | solution.py:43
  74.3 1.1 constant_dynamic-update-slice_fusion.1
  75.3 5.4 %collective-permute-done.10 = bf16[192,1152]{1,0:T(8,128)(2,1)S(1)} collective-permute-done((bf16[192,1152]{1,0:T(8,128)(2,1)}, bf16[192,1152]{1,0:T(8,128)(2,1)S(1)}, u32[]{:S(2)}, u32[]{:S(2)}) %collective-permute-start.10) | collective-permute-done | bytes 442400 | tf_op jit(solution)/shard_map/ppermute | solution.py:43
  82.2 8.4 %collective-permute-start.13 = (bf16[768,1152]{1,0:T(8,128)(2,1)S(1)}, bf16[768,1152]{1,0:T(8,128)(2,1)S(1)}, u32[]{:S(2)}, u32[]{:S(2)}) collective-permute-start(bf16[768,1152]{1,0:T(8,128)(2,1)S(1)} %constant_dynamic-update-slice_fusion.refs_12_), channel_id=1, source_target_pairs={{0,128},{32,160},{64,192},{96,224},{128,0},{160,32},{192,64},{224,... | collective-permute-start | bytes 5308424 | tf_op jit(solution)/shard_map/ppermute | solution.py:43
  91.4 1.5 copy-done
  92.9 1.0 copy-done.2
  93.9 1.0 copy-done.4
  94.9 1.5 copy-done.10
  96.4 1.1 copy-done.11
  97.5 1.0 copy-done.12
  98.5 1.0 copy-done.14
  99.5 1.0 copy-done.16
  100.5 1.0 copy-done.18
  101.5 1.0 copy-done.20
  102.5 0.9 copy-done.22
  104.4 5.8 %gather.1 = (f32[512,1152]{1,0:T(8,128)S(1)}, bf16[512,768]{1,0:T(8,128)(2,1)S(1)}) custom-call(s32[12]{0:T(128)S(1)} %stack.51.spots.refs_0_, s32[1,1]{1,0:T(1,128)S(6)} %copy.13.levels, bf16[512,384]{1,0:T(8,128)(2,1)S(1)} %bitcast.24, bf16[512,384]{1,0:T(8,128)(2,1)S(1)} %copy-done.16, bf16[512,384]{1,0:T(8,128)(2,1)S(1)} %copy-done.14, ...), custom_call_target="tpu_custom_call" | custom-call | flops 2717908992 | bytes 12582912 | tf_op jit(solution)/shard_map/gather/pallas_call | solution.py:218
  110.2 1.5 project.1
  111.7 1.9 %collective-permute-start.16 = (bf16[512,768]{1,0:T(8,128)(2,1)S(1)}, bf16[512,768]{1,0:T(8,128)(2,1)S(1)}, u32[]{:S(2)}, u32[]{:S(2)}) collective-permute-start(bf16[512,768]{1,0:T(8,128)(2,1)S(1)} %get-tuple-element.44.own), channel_id=1, source_target_pairs={{0,128},{32,160},{64,192},{96,224},{128,0},{160,32},{192,64},{224,... | collective-permute-start | bytes 2359304 | tf_op jit(solution)/shard_map/ppermute | solution.py:43
  114.4 1.3 collective-permute-start.14
  115.9 2.2 %near.1 = (f32[512,384]{1,0:T(8,128)S(1)}, f32[512,384]{1,0:T(8,128)S(1)}) custom-call(s32[12]{0:T(128)S(1)} %stack.51.spots.refs_0_, s32[1,4]{1,0:T(1,128)S(1)} %copy-done.6, s32[4,4]{1,0:T(4,128)S(1)} %bitcast.17, bf16[512,384]{1,0:T(8,128)(2,1)S(1)} %get-tuple-element.43.q.refs_3_, bf16[512,768]{1,0:T(8,128)(2,1)S(1)} %get-tuple-element.44.own, ...), custom_call_target="tpu_custom_call" | custom-call | flops 805306368 | bytes 6291456 | tf_op jit(solution)/shard_map/near/pallas_call | solution.py:257
  118.2 18.9 %collective-permute-done.14 = bf16[256,768]{1,0:T(8,128)(2,1)S(1)} collective-permute-done((bf16[256,768]{1,0:T(8,128)(2,1)S(1)}, bf16[256,768]{1,0:T(8,128)(2,1)S(1)}, u32[]{:S(2)}, u32[]{:S(2)}) %collective-permute-start.14) | collective-permute-done | bytes 393248 | tf_op jit(solution)/shard_map/ppermute | solution.py:43
  137.1 1.9 %collective-permute-start.17 = (bf16[256,768]{1,0:T(8,128)(2,1)S(1)}, bf16[256,768]{1,0:T(8,128)(2,1)S(1)}, u32[]{:S(2)}, u32[]{:S(2)}) collective-permute-start(bf16[256,768]{1,0:T(8,128)(2,1)S(1)} %collective-permute-done.14), channel_id=1, source_target_pairs={{16,256},{48,288},{80,320},{112,352},{144,384},{176,416},{208,448}... | collective-permute-start | bytes 1179656 | tf_op jit(solution)/shard_map/ppermute | solution.py:43
  139.0 1.3 collective-permute-start.18
  140.3 15.3 %collective-permute-done.17.refs_6_ = bf16[256,768]{1,0:T(8,128)(2,1)S(1)} collective-permute-done((bf16[256,768]{1,0:T(8,128)(2,1)S(1)}, bf16[256,768]{1,0:T(8,128)(2,1)S(1)}, u32[]{:S(2)}, u32[]{:S(2)}) %collective-permute-start.17) | collective-permute-done | bytes 393248 | tf_op jit(solution)/shard_map/ppermute | solution.py:43
  155.6 4.3 %collective-permute-done.18.refs_7_ = bf16[256,768]{1,0:T(8,128)(2,1)S(1)} collective-permute-done((bf16[256,768]{1,0:T(8,128)(2,1)S(1)}, bf16[256,768]{1,0:T(8,128)(2,1)S(1)}, u32[]{:S(2)}, u32[]{:S(2)}) %collective-permute-start.18) | collective-permute-done | bytes 393248 | tf_op jit(solution)/shard_map/ppermute | solution.py:43
  159.9 3.8 %collective-permute-start.19 = (bf16[512,768]{1,0:T(8,128)(2,1)S(1)}, bf16[512,768]{1,0:T(8,128)(2,1)S(1)}, u32[]{:S(2)}, u32[]{:S(2)}) collective-permute-start(bf16[512,768]{1,0:T(8,128)(2,1)S(1)} %pad_maximum_fusion), channel_id=1, source_target_pairs={{0,128},{32,160},{64,192},{96,224},{128,0},{160,32},{192,64},{224,... | collective-permute-start | bytes 2359304 | tf_op jit(solution)/shard_map/ppermute | solution.py:43
  163.8 1.7 far.1
  165.7 3.3 %last.1 = bf16[512,384]{1,0:T(8,128)(2,1)} custom-call(s32[12]{0:T(128)S(1)} %stack.51.spots.refs_0_, s32[1,4]{1,0:T(1,128)S(1)} %copy-done.6, s32[4,4]{1,0:T(4,128)S(1)} %bitcast.19, bf16[512,384]{1,0:T(8,128)(2,1)S(1)} %get-tuple-element.43.q.refs_3_, f32[512,384]{1,0:T(8,128)S(1)} %get-tuple-element.51.refs_4_, f32[512,384]{1,0:T(8,128)S(1)} %get-tuple-element.52.refs_5_, ...), custom_call_target="tpu_custom_call" | custom-call | flops 805306368 | bytes 6291456 | tf_op jit(solution)/shard_map/last/pallas_call | solution.py:280
  (59 shorter events, 7.0 us)
Async XLA Ops:
  0.0 27.0 %collective-permute-start.2 = (bf16[768,1152]{1,0:T(8,128)(2,1)}, bf16[768,1152]{1,0:T(8,128)(2,1)S(1)}, u32[]{:S(2)}, u32[]{:S(2)}) collective-permute-start(bf16[768,1152]{1,0:T(8,128)(2,1)} %refs_10_.1), channel_id=1, source_target_pairs={{0,128},{32,160},{64,192},{96,224},{128,0},{160,32},{192,64},{224,... | collective-permute-start | bytes 5308424 | tf_op jit(solution)/shard_map/ppermute | solution.py:43
  2.6 19.5 %collective-permute-start.1 = (bf16[512,384]{1,0:T(8,128)(2,1)}, bf16[512,384]{1,0:T(8,128)(2,1)S(1)}, u32[]{:S(2)}, u32[]{:S(2)}) collective-permute-start(bf16[512,384]{1,0:T(8,128)(2,1)} %bitcast.22), channel_id=1, source_target_pairs={{0,7},{1,0},{2,1},{3,2},{4,3},{5,4},{6,5},{7,6},{8,15},{9,8},{10,9... | collective-permute-start | bytes 1179656 | tf_op jit(solution)/shard_map/ppermute | solution.py:47
  13.3 13.7 %collective-permute-start = (bf16[512,384]{1,0:T(8,128)(2,1)}, bf16[512,384]{1,0:T(8,128)(2,1)S(1)}, u32[]{:S(2)}, u32[]{:S(2)}) collective-permute-start(bf16[512,384]{1,0:T(8,128)(2,1)} %bitcast.23), channel_id=1, source_target_pairs={{0,1},{1,2},{2,3},{3,4},{4,5},{5,6},{6,7},{7,0},{8,9},{9,10},{10,1... | collective-permute-start | bytes 1179656 | tf_op jit(solution)/shard_map/ppermute | solution.py:47
  16.3 20.0 %collective-permute-start.3 = (bf16[192,1152]{1,0:T(8,128)(2,1)S(1)}, bf16[192,1152]{1,0:T(8,128)(2,1)S(1)}, u32[]{:S(2)}, u32[]{:S(2)}) collective-permute-start(bf16[192,1152]{1,0:T(8,128)(2,1)S(1)} %constant_dynamic-slice_fusion), channel_id=1, source_target_pairs={{0,280},{32,312},{64,344},{96,376},{128,408},{160,440},{192,472},{... | collective-permute-start | bytes 1327112 | tf_op jit(solution)/shard_map/ppermute | solution.py:43
  27.0 1.3 copy-start.9
  28.3 12.6 %collective-permute-start.4 = (bf16[512,384]{1,0:T(8,128)(2,1)S(1)}, bf16[512,384]{1,0:T(8,128)(2,1)S(1)}, u32[]{:S(2)}, u32[]{:S(2)}) collective-permute-start(bf16[512,384]{1,0:T(8,128)(2,1)S(1)} %collective-permute-done.refs_1_), channel_id=1, source_target_pairs={{0,1},{1,2},{2,3},{3,4},{4,5},{5,6},{6,7},{7,0},{8,9},{9,10},{10,1... | collective-permute-start | bytes 1179656 | tf_op jit(solution)/shard_map/ppermute | solution.py:47
  30.2 0.7 copy-start.15
  30.9 11.6 %collective-permute-start.5 = (bf16[512,384]{1,0:T(8,128)(2,1)S(1)}, bf16[512,384]{1,0:T(8,128)(2,1)S(1)}, u32[]{:S(2)}, u32[]{:S(2)}) collective-permute-start(bf16[512,384]{1,0:T(8,128)(2,1)S(1)} %collective-permute-done.1.refs_2_), channel_id=1, source_target_pairs={{0,7},{1,0},{2,1},{3,2},{4,3},{5,4},{6,5},{7,6},{8,15},{9,8},{10,9... | collective-permute-start | bytes 1179656 | tf_op jit(solution)/shard_map/ppermute | solution.py:47
  35.5 0.8 copy-start.13
  42.5 19.4 %collective-permute-start.6 = (bf16[192,1152]{1,0:T(8,128)(2,1)S(1)}, bf16[192,1152]{1,0:T(8,128)(2,1)S(1)}, u32[]{:S(2)}, u32[]{:S(2)}) collective-permute-start(bf16[192,1152]{1,0:T(8,128)(2,1)S(1)} %collective-permute-done.3), channel_id=1, source_target_pairs={{0,32},{32,64},{64,96},{96,0},{128,224},{160,128},{192,160},{224,1... | collective-permute-start | bytes 1327112 | tf_op jit(solution)/shard_map/ppermute | solution.py:43
  46.9 13.4 %collective-permute-start.7 = (bf16[512,384]{1,0:T(8,128)(2,1)S(1)}, bf16[512,384]{1,0:T(8,128)(2,1)S(1)}, u32[]{:S(2)}, u32[]{:S(2)}) collective-permute-start(bf16[512,384]{1,0:T(8,128)(2,1)S(1)} %collective-permute-done.4.refs_3_), channel_id=1, source_target_pairs={{0,1},{1,2},{2,3},{3,4},{4,5},{5,6},{6,7},{7,0},{8,9},{9,10},{10,1... | collective-permute-start | bytes 1179656 | tf_op jit(solution)/shard_map/ppermute | solution.py:47
  48.8 0.8 copy-start.17
  49.5 12.4 %collective-permute-start.8 = (bf16[512,384]{1,0:T(8,128)(2,1)S(1)}, bf16[512,384]{1,0:T(8,128)(2,1)S(1)}, u32[]{:S(2)}, u32[]{:S(2)}) collective-permute-start(bf16[512,384]{1,0:T(8,128)(2,1)S(1)} %collective-permute-done.5.refs_4_), channel_id=1, source_target_pairs={{0,7},{1,0},{2,1},{3,2},{4,3},{5,4},{6,5},{7,6},{8,15},{9,8},{10,9... | collective-permute-start | bytes 1179656 | tf_op jit(solution)/shard_map/ppermute | solution.py:47
  54.9 0.8 copy-start.19
  60.3 3.9 %copy-start.1 = (bf16[512,384]{1,0:T(8,128)(2,1)}, bf16[512,384]{1,0:T(8,128)(2,1)S(1)}, u32[]{:S(2)}) copy-start(bf16[512,384]{1,0:T(8,128)(2,1)S(1)} %collective-permute-done.7.refs_5_) | copy-start | bytes 1179652
  61.9 2.3 %copy-start.3 = (bf16[512,384]{1,0:T(8,128)(2,1)}, bf16[512,384]{1,0:T(8,128)(2,1)S(1)}, u32[]{:S(2)}) copy-start(bf16[512,384]{1,0:T(8,128)(2,1)S(1)} %collective-permute-done.8.refs_6_) | copy-start | bytes 1179652
  61.9 9.6 %collective-permute-start.9 = (bf16[192,1152]{1,0:T(8,128)(2,1)S(1)}, bf16[192,1152]{1,0:T(8,128)(2,1)}, u32[]{:S(2)}, u32[]{:S(2)}) collective-permute-start(bf16[192,1152]{1,0:T(8,128)(2,1)S(1)} %collective-permute-done.6), channel_id=1, source_target_pairs={{0,32},{32,64},{64,96},{96,0},{128,224},{160,128},{192,160},{224,1... | collective-permute-start | bytes 1327112 | tf_op jit(solution)/shard_map/ppermute | solution.py:43
  64.2 16.6 %collective-permute-start.12 = (bf16[256,384]{1,0:T(8,128)(2,1)S(1)}, bf16[256,384]{1,0:T(8,128)(2,1)S(1)}, u32[]{:S(2)}, u32[]{:S(2)}) collective-permute-start(bf16[256,384]{1,0:T(8,128)(2,1)S(1)} %slice.19), channel_id=1, source_target_pairs={{0,7},{1,0},{2,1},{3,2},{4,3},{5,4},{6,5},{7,6},{8,15},{9,8},{10,9... | collective-permute-start | bytes 589832 | tf_op jit(solution)/shard_map/ppermute | solution.py:47
  69.6 11.9 %collective-permute-start.11 = (bf16[256,384]{1,0:T(8,128)(2,1)S(1)}, bf16[256,384]{1,0:T(8,128)(2,1)S(1)}, u32[]{:S(2)}, u32[]{:S(2)}) collective-permute-start(bf16[256,384]{1,0:T(8,128)(2,1)S(1)} %slice.18), channel_id=1, source_target_pairs={{0,1},{1,2},{2,3},{3,4},{4,5},{5,6},{6,7},{7,0},{8,9},{9,10},{10,1... | collective-permute-start | bytes 589832 | tf_op jit(solution)/shard_map/ppermute | solution.py:47
  71.5 9.3 %collective-permute-start.10 = (bf16[192,1152]{1,0:T(8,128)(2,1)}, bf16[192,1152]{1,0:T(8,128)(2,1)S(1)}, u32[]{:S(2)}, u32[]{:S(2)}) collective-permute-start(bf16[192,1152]{1,0:T(8,128)(2,1)} %collective-permute-done.9), channel_id=1, source_target_pairs={{0,32},{32,64},{64,96},{96,0},{128,224},{160,128},{192,160},{224,1... | collective-permute-start | bytes 1327112 | tf_op jit(solution)/shard_map/ppermute | solution.py:43
  80.8 0.7 copy-start.21
  81.5 0.7 copy-start.23
  82.2 28.0 %collective-permute-start.13 = (bf16[768,1152]{1,0:T(8,128)(2,1)S(1)}, bf16[768,1152]{1,0:T(8,128)(2,1)S(1)}, u32[]{:S(2)}, u32[]{:S(2)}) collective-permute-start(bf16[768,1152]{1,0:T(8,128)(2,1)S(1)} %constant_dynamic-update-slice_fusion.refs_12_), channel_id=1, source_target_pairs={{0,128},{32,160},{64,192},{96,224},{128,0},{160,32},{192,64},{224,... | collective-permute-start | bytes 5308424 | tf_op jit(solution)/shard_map/ppermute | solution.py:43
  91.4 1.5 copy-start
  92.9 1.0 copy-start.2
  93.9 1.0 copy-start.4
  94.9 1.5 copy-start.10
  96.4 1.1 copy-start.11
  97.5 1.0 copy-start.12
  98.5 1.0 copy-start.14
  99.5 1.0 copy-start.16
  100.5 1.0 copy-start.18
  101.5 1.0 copy-start.20
  102.5 0.9 copy-start.22
  103.4 0.9 copy-start.24
  104.4 5.8 %copy-start.7 = (f32[128]{0:T(128)S(1)}, f32[128]{0:T(128)}, u32[]{:S(2)}) copy-start(f32[128]{0:T(128)} %param.14) | copy-start | bytes 1540
  104.4 5.8 %copy-start.8 = (f32[128]{0:T(128)S(1)}, f32[128]{0:T(128)}, u32[]{:S(2)}) copy-start(f32[128]{0:T(128)} %param.15) | copy-start | bytes 1540
  110.2 5.8 %copy-start.5 = (s32[1,4,4]{2,1,0:T(4,128)S(1)}, s32[1,4,4]{2,1,0:T(4,128)}, u32[]{:S(2)}) copy-start(s32[1,4,4]{2,1,0:T(4,128)} %param.11) | copy-start | bytes 196
  110.2 5.7 %copy-start.6 = (s32[1,4]{1,0:T(1,128)S(1)}, s32[1,4]{1,0:T(1,128)}, u32[]{:S(2)}) copy-start(s32[1,4]{1,0:T(1,128)} %refs_1_.3) | copy-start | bytes 52
  111.7 4.2 %collective-permute-start.16 = (bf16[512,768]{1,0:T(8,128)(2,1)S(1)}, bf16[512,768]{1,0:T(8,128)(2,1)S(1)}, u32[]{:S(2)}, u32[]{:S(2)}) collective-permute-start(bf16[512,768]{1,0:T(8,128)(2,1)S(1)} %get-tuple-element.44.own), channel_id=1, source_target_pairs={{0,128},{32,160},{64,192},{96,224},{128,0},{160,32},{192,64},{224,... | collective-permute-start | bytes 2359304 | tf_op jit(solution)/shard_map/ppermute | solution.py:43
  113.7 4.4 %collective-permute-start.15 = (bf16[256,768]{1,0:T(8,128)(2,1)S(1)}, bf16[256,768]{1,0:T(8,128)(2,1)S(1)}, u32[]{:S(2)}, u32[]{:S(2)}) collective-permute-start(bf16[256,768]{1,0:T(8,128)(2,1)S(1)} %get-tuple-element.55), channel_id=1, source_target_pairs={{0,272},{32,304},{64,336},{96,368},{128,400},{160,432},{192,464},{... | collective-permute-start | bytes 1179656 | tf_op jit(solution)/shard_map/ppermute | solution.py:43
  114.4 22.7 %collective-permute-start.14 = (bf16[256,768]{1,0:T(8,128)(2,1)S(1)}, bf16[256,768]{1,0:T(8,128)(2,1)S(1)}, u32[]{:S(2)}, u32[]{:S(2)}) collective-permute-start(bf16[256,768]{1,0:T(8,128)(2,1)S(1)} %get-tuple-element.56), channel_id=1, source_target_pairs={{0,16},{32,48},{64,80},{96,112},{128,144},{160,176},{192,208},{224... | collective-permute-start | bytes 1179656 | tf_op jit(solution)/shard_map/ppermute | solution.py:43
  137.1 18.5 %collective-permute-start.17 = (bf16[256,768]{1,0:T(8,128)(2,1)S(1)}, bf16[256,768]{1,0:T(8,128)(2,1)S(1)}, u32[]{:S(2)}, u32[]{:S(2)}) collective-permute-start(bf16[256,768]{1,0:T(8,128)(2,1)S(1)} %collective-permute-done.14), channel_id=1, source_target_pairs={{16,256},{48,288},{80,320},{112,352},{144,384},{176,416},{208,448}... | collective-permute-start | bytes 1179656 | tf_op jit(solution)/shard_map/ppermute | solution.py:43
  139.0 20.8 %collective-permute-start.18 = (bf16[256,768]{1,0:T(8,128)(2,1)S(1)}, bf16[256,768]{1,0:T(8,128)(2,1)S(1)}, u32[]{:S(2)}, u32[]{:S(2)}) collective-permute-start(bf16[256,768]{1,0:T(8,128)(2,1)S(1)} %collective-permute-done.15), channel_id=1, source_target_pairs={{0,272},{32,304},{64,336},{96,368},{128,400},{160,432},{192,464},{... | collective-permute-start | bytes 1179656 | tf_op jit(solution)/shard_map/ppermute | solution.py:43
  159.9 5.7 %collective-permute-start.19 = (bf16[512,768]{1,0:T(8,128)(2,1)S(1)}, bf16[512,768]{1,0:T(8,128)(2,1)S(1)}, u32[]{:S(2)}, u32[]{:S(2)}) collective-permute-start(bf16[512,768]{1,0:T(8,128)(2,1)S(1)} %pad_maximum_fusion), channel_id=1, source_target_pairs={{0,128},{32,160},{64,192},{96,224},{128,0},{160,32},{192,64},{224,... | collective-permute-start | bytes 2359304 | tf_op jit(solution)/shard_map/ppermute | solution.py:43

commit v3 on v2

--- a/solution.py
+++ b/solution.py
@@ -33,51 +33,64 @@
 MIRROR = pairs(lambda y, core, x: (RING_Y - 1 - y, core, x))
 X_RING = pairs(lambda y, core, x: (y, core, (x + 1 - 2 * core) % XS))
 SWAP = pairs(lambda y, core, x: (y, 1 - core, x))
-UP_FIRST = pairs(lambda y, core, x: (y + 2, core, x), lambda y: y < 4)
-UP_SECOND = pairs(lambda y, core, x: (y + 2, core, x), lambda y: 2 <= y < 6)
-DOWN_FIRST = pairs(lambda y, core, x: ((y - 2) % 8, core, x), lambda y: y < 4)
-DOWN_SECOND = pairs(lambda y, core, x: (y - 2 if y >= 6 else y + 6, core, x), lambda y: y >= 6 or y < 2)
+FIRST = pairs(lambda y, core, x: ((y + 2 - 4 * core) % RING_Y, core, x), lambda y: y < YS)
+SECOND = [(b, place((y + 4) % RING_Y, core, x)) for y in range(YS) for core in range(CORES) for x in range(XS)
+          for b in [place((y + 2 - 4 * core) % RING_Y, core, x)]]
 
 
 def move(array, table):
     return lax.ppermute(array, ("block", "req"), table)
 
 
-def turn(array, step, size):
-    return lax.ppermute(array, "head", [(i, (i + step) % size) for i in range(size)])
+def turn(array, size):
+    per_block = XS * YS * size
+    table = []
+    for block in range(HALVES * CORES):
+        step = 1 - 2 * (block % CORES)
+        for other in range(XS * YS):
+            base = block * per_block + other * size
+            table += [(base + i, base + (i + step) % size) for i in range(size)]
+    return lax.ppermute(array, ("block", "req", "head"), table)
 
 
 def gather_kernel(spots, levels, *refs):
-    (own, r1, l1, r2, l2, r3, l3, r4, l4, mod, w_own, w_pair, w_rest) = refs[:13]
-    acc, last_columns, normed = refs[13:]
-    rows, depth = own.shape
-    half = rows // 2
+    pieces = refs[:8]
+    mod_table, w_own_far, w_pair_far, w_rest = refs[8:12]
+    acc, last_columns, tokens, mod, w_own, w_pair, normed, sems = refs[12:]
+    rows, depth = pieces[0].shape
     features = normed.shape[1]
     step_rows = 64
-    level = levels[0, 0]
-
-    for side, last in ((0, r4), (1, l4)):
-        def norm_rows(step, carry, side=side, last=last):
-            inner = pl.multiple_of(step * step_rows, step_rows)
-            outer = pl.multiple_of(side * half + step * step_rows, step_rows)
-            views = [ref.at[pl.ds(outer, step_rows), :] for ref in (own, r1, l1, r2, l2, r3, l3)]
-            views.append(last.at[pl.ds(inner, step_rows), :])
-            total = jnp.zeros((step_rows, 128), jnp.float32)
-            for view in views:
-                wide = view[...].astype(jnp.float32)
-                square = wide * wide
-                for lane in range(0, depth, 128):
-                    total = total + square[:, lane : lane + 128]
-            scale = lax.rsqrt(jnp.sum(total, axis=-1, keepdims=True) * (1.0 / features) + EPS)
-            for number, view in enumerate(views):
-                column = pl.multiple_of(spots[number] * depth, 128)
-                wide = view[...].astype(jnp.float32)
-                gain = 1.0 + mod[level, 0:1, pl.ds(column, depth)]
-                row = wide * scale * gain + mod[level, 1:2, pl.ds(column, depth)]
-                normed[pl.ds(outer, step_rows), pl.ds(column, depth)] = row.astype(jnp.bfloat16)
-            return carry
-
-        lax.fori_loop(0, half // step_rows, norm_rows, 0)
+
+    loads = [pltpu.make_async_copy(piece, tokens.at[number], sems.at[number]) for number, piece in enumerate(pieces)]
+    loads.append(pltpu.make_async_copy(mod_table.at[levels[0, 0]], mod, sems.at[8]))
+    weights = [
+        pltpu.make_async_copy(w_own_far, w_own, sems.at[9]),
+        pltpu.make_async_copy(w_pair_far, w_pair, sems.at[10]),
+    ]
+    for copy in loads + weights:
+        copy.start()
+    for copy in loads:
+        copy.wait()
+
+    def norm_rows(step, carry):
+        band = pl.ds(pl.multiple_of(step * step_rows, step_rows), step_rows)
+        total = jnp.zeros((step_rows, 128), jnp.float32)
+        for number in range(8):
+            wide = tokens[number, band, :].astype(jnp.float32)
+            square = wide * wide
+            for lane in range(0, depth, 128):
+                total = total + square[:, lane : lane + 128]
+        scale = lax.rsqrt(jnp.sum(total, axis=-1, keepdims=True) * (1.0 / features) + EPS)
+        for number in range(8):
+            column = pl.multiple_of(spots[number] * depth, 128)
+            wide = tokens[number, band, :].astype(jnp.float32)
+            row = wide * scale * (1.0 + mod[0:1, pl.ds(column, depth)]) + mod[1:2, pl.ds(column, depth)]
+            normed[band, pl.ds(column, depth)] = row.astype(jnp.bfloat16)
+        return carry
+
+    lax.fori_loop(0, rows // step_rows, norm_rows, 0)
+    for copy in weights:
+        copy.wait()
 
     part = w_own.shape[0]
     columns = acc.shape[1]
@@ -151,17 +164,17 @@
                 attend_part(limit, first, q, kv.at[first : first + half], num, den, heads)
 
 
-def far_kernel(number, finish, spots, frames, mask, q, num_in, den_in, lo, hi, *rest):
+def far_kernel(number, finish, spots, frames, mask, q, num_in, den_in, kv, *rest):
     heads = q.shape[1] // HD
     half = q.shape[0] // 2
     num, den = rest[-2:]
     num[...] = num_in[...]
     den[...] = den_in[...]
     limit = key_limit(spots, frames, mask, number)
-    for first, kv in ((0, lo), (half, hi)):
+    for first in (0, half):
         @pl.when(limit > first)
-        def _(first=first, kv=kv):
-            attend_part(limit, first, q, kv, num, den, heads)
+        def _(first=first):
+            attend_part(limit, first, q, kv.at[first : first + half], num, den, heads)
     if finish:
         for head in range(heads):
             span = slice(HD * head, HD * (head + 1))
@@ -177,40 +190,41 @@
     heads = columns // (3 * HD)
     width = heads * HD
     quarter = part_rows // XS
-    half = rows // 2
 
     z = lax.axis_index("head")
     block = lax.axis_index("block")
     side, core = block // CORES, block % CORES
     x = lax.axis_index("req") // YS
 
-    piece = move(lax.dynamic_slice_in_dim(w_qkv, quarter * x, quarter), MIRROR)
-    r1, l1 = turn(own, 1, ring), turn(own, -1, ring)
+    mine = [lax.dynamic_slice_in_dim(w_qkv, quarter * x + at, quarter // 2) for at in (0, quarter // 2)]
+    first, second = (move(item, MIRROR) for item in mine)
     w_pair = move(w_qkv, SWAP)
-    r1, l1, w_pair = lax.optimization_barrier((r1, l1, w_pair))
-    r2, l2 = turn(r1, 1, ring), turn(l1, -1, ring)
-    piece, r2, l2 = lax.optimization_barrier((piece, r2, l2))
-    held = [piece, move(piece, X_RING)]
-    r3, l3 = turn(r2, 1, ring), turn(l2, -1, ring)
-    held[1], r3, l3 = lax.optimization_barrier((held[1], r3, l3))
-    held.append(move(held[1], X_RING))
-    r4, l4 = turn(r3[:half], 1, ring), turn(l3[half:], -1, ring)
-    held.append(move(held[2], X_RING))
+    pieces = [own, turn(own, ring)]
+    pieces.append(turn(pieces[1], ring))
+    first, pieces[2] = lax.optimization_barrier((first, pieces[2]))
+    pieces.append(turn(pieces[2], ring))
+    first, second, w_pair, pieces[3] = lax.optimization_barrier((first, second, w_pair, pieces[3]))
+    held = [jnp.concatenate([first, second])]
+    for _ in range(XS - 1):
+        following = turn(pieces[-1], ring)
+        held.append(move(held[-1], X_RING))
+        held[-1], following = lax.optimization_barrier((held[-1], following))
+        pieces.append(following)
+    pieces.append(turn(pieces[-1], ring))
     w_rest = jnp.zeros_like(w_qkv)
     for step, piece in enumerate(held):
         at = (x + (2 * core - 1) * step + XS) % XS
         w_rest = lax.dynamic_update_slice_in_dim(w_rest, piece, at * quarter, 0)
-    w_rest, r4, l4 = lax.optimization_barrier((w_rest, r4, l4))
     w_last = move(w_rest, SWAP)
 
-    order = [z, z - 1, z + 1, z - 2, z + 2, z - 3, z + 3, z + 4]
-    spots = [(item + ring) % ring for item in order]
+    spots = [(z + (2 * core - 1) * step + ring) % ring for step in range(ring)]
     other = (1 - side) * CORES
     spots += [block, side * CORES + 1 - core, other + core, other + 1 - core]
     spots = jnp.stack(spots).astype(jnp.int32)
 
     smem = pl.BlockSpec(memory_space=pltpu.SMEM)
     vmem = pl.BlockSpec(memory_space=pltpu.VMEM)
+    anywhere = pl.BlockSpec(memory_space=pl.ANY)
 
     def sized(limit):
         return pltpu.CompilerParams(vmem_limit_bytes=limit * MIB)
@@ -221,15 +235,22 @@
             jax.ShapeDtypeStruct((rows, columns), jnp.float32),
             jax.ShapeDtypeStruct((rows, part_rows), jnp.bfloat16),
         ),
-        in_specs=[smem] * 2 + [vmem] * 13,
+        in_specs=[smem] * 2 + [anywhere] * 11 + [vmem],
         out_specs=(vmem, vmem),
-        scratch_shapes=[pltpu.VMEM((rows, ring * depth), jnp.bfloat16)],
+        scratch_shapes=[
+            pltpu.VMEM((ring, rows, depth), jnp.bfloat16),
+            pltpu.VMEM(mod_table.shape[1:], jnp.float32),
+            pltpu.VMEM((part_rows, columns), jnp.bfloat16),
+            pltpu.VMEM((part_rows, columns), jnp.bfloat16),
+            pltpu.VMEM((rows, ring * depth), jnp.bfloat16),
+            pltpu.SemaphoreType.DMA((11,)),
+        ],
         compiler_params=sized(32),
         cost_estimate=pl.CostEstimate(
             flops=2 * rows * 3 * part_rows * columns, bytes_accessed=12 * MIB, transcendentals=0
         ),
         name="gather",
-    )(spots, levels, own, r1, l1, r2, l2, r3, l3, r4, l4, mod_table, w_qkv, w_pair, w_rest)
+    )(spots, levels, *pieces, mod_table, w_qkv, w_pair, w_rest)
     queries, kv = pl.pallas_call(
         project_kernel,
         out_shape=(
@@ -245,8 +266,7 @@
         name="project",
     )(acc, last_columns, w_last, q_gain[None, :], k_gain[None, :])
 
-    far_lo = move(kv[:half], UP_FIRST)
-    far_hi = move(kv[half:], DOWN_FIRST)
+    far_kv = move(kv, FIRST)
     pair_kv = move(kv, SWAP)
 
     where = (spots, frames, segment_mask[0])
@@ -263,30 +283,28 @@
         cost_estimate=work,
         name="near",
     )(*where, queries, kv, pair_kv)
-    far_lo, far_hi, num, den = lax.optimization_barrier((far_lo, far_hi, num, den))
-    far_lo = move(far_lo, UP_SECOND)
-    far_hi = move(far_hi, DOWN_SECOND)
-    far_kv = lax.optimization_barrier(jnp.concatenate([far_lo, far_hi]))
+    far_kv, num, den = lax.optimization_barrier((far_kv, num, den))
+    far_kv = move(far_kv, SECOND)
     far_pair = move(far_kv, SWAP)
     num, den = pl.pallas_call(
         lambda *refs: far_kernel(2, False, *refs),
         out_shape=sums,
-        in_specs=[smem] * 3 + [vmem] * 5,
+        in_specs=[smem] * 3 + [vmem] * 4,
         out_specs=(vmem, vmem),
         compiler_params=sized(24),
         cost_estimate=work,
         name="far",
-    )(*where, queries, num, den, far_lo, far_hi)
+    )(*where, queries, num, den, far_kv)
     result = pl.pallas_call(
         lambda *refs: far_kernel(3, True, *refs),
         out_shape=jax.ShapeDtypeStruct((rows, width), jnp.bfloat16),
-        in_specs=[smem] * 3 + [vmem] * 5,
+        in_specs=[smem] * 3 + [vmem] * 4,
         out_specs=vmem,
         scratch_shapes=[pltpu.VMEM((rows, width), jnp.float32)] * 2,
         compiler_params=sized(24),
         cost_estimate=work,
         name="last",
-    )(*where, queries, num, den, far_pair[:half], far_pair[half:])
+    )(*where, queries, num, den, far_pair)
     return result.reshape(1, 1, rows, width)
 
 

time: 170 us -> 183 us (1.076)
  the two profiles are of different devices: /device:TPU:41 before, /device:TPU:1 now
where the time goes in v3:
time: 183 us; the launch traced here: 180 us
  waiting for transfers between devices  78.7 us (43%)
  starting transfers between devices  68.1 us (37%)
  local copies, waits for them, and re-layouts  16.4 us (9%)
  Pallas kernels  15.9 us (9%)
    ppermute x11, waiting for transfers between devices, move(): return lax.ppermute(array, ('block', 'req'), table)  57 us
    ppermute x11, starting transfers between devices, move(): return lax.ppermute(array, ('block', 'req'), table)  42.2 us
    ppermute x7, starting transfers between devices, turn(): return lax.ppermute(array, ('block', 'req', 'head'), table)  25.9 us
    ppermute x7, waiting for transfers between devices, turn(): return lax.ppermute(array, ('block', 'req', 'head'), table)  21.7 us
    unnamed x39, local copies, waits for them, and re-layouts  12.8 us
    pallas_call x1, Pallas kernels, body(): pl.pallas_call(gather_kernel, out_shape=(jax.ShapeDtypeStruct((rows, colu...  8.1 us
    pallas_call x1, Pallas kernels, body(): pl.pallas_call(near_kernel, out_shape=sums, in_specs=[smem] * 3 + [vmem]...  3.86 us
  transfers between devices with their start and end apart: 18, of which 11 were waited for; matrix products, arithmetic and copies ran while one was open for 2% of the time, Pallas kernels for 7%

profile of v3, /device:TPU:1, one launch (start us, length us, event | category | flops | bytes accessed | tf_op | source)
XLA Modules:
  0.0 180.3 jit_solution(6349148061747530532)
XLA Ops:
  0.0 8.8 %collective-permute-start.4 = (bf16[768,1152]{1,0:T(8,128)(2,1)}, bf16[768,1152]{1,0:T(8,128)(2,1)S(1)}, u32[]{:S(2)}, u32[]{:S(2)}) collective-permute-start(bf16[768,1152]{1,0:T(8,128)(2,1)} %refs_9_.1), channel_id=1, source_target_pairs={{0,128},{32,160},{64,192},{96,224},{128,0},{160,32},{192,64},{224,... | collective-permute-start | bytes 5308424 | tf_op jit(solution)/shard_map/ppermute | solution.py:42
  8.8 5.3 %collective-permute-start = (bf16[512,384]{1,0:T(8,128)(2,1)}, bf16[512,384]{1,0:T(8,128)(2,1)S(1)}, u32[]{:S(2)}, u32[]{:S(2)}) collective-permute-start(bf16[512,384]{1,0:T(8,128)(2,1)} %bitcast.22), channel_id=1, source_target_pairs={{0,1},{1,2},{2,3},{3,4},{4,5},{5,6},{6,7},{7,0},{8,9},{9,10},{10,1... | collective-permute-start | bytes 1179656 | tf_op jit(solution)/shard_map/ppermute | solution.py:53
  14.1 5.0 %collective-permute-done.refs_1_ = bf16[512,384]{1,0:T(8,128)(2,1)S(1)} collective-permute-done((bf16[512,384]{1,0:T(8,128)(2,1)}, bf16[512,384]{1,0:T(8,128)(2,1)S(1)}, u32[]{:S(2)}, u32[]{:S(2)}) %collective-permute-start) | collective-permute-done | bytes 393248 | tf_op jit(solution)/shard_map/ppermute | solution.py:53
  19.1 4.9 %collective-permute-start.2 = (bf16[512,384]{1,0:T(8,128)(2,1)S(1)}, bf16[512,384]{1,0:T(8,128)(2,1)S(1)}, u32[]{:S(2)}, u32[]{:S(2)}) collective-permute-start(bf16[512,384]{1,0:T(8,128)(2,1)S(1)} %collective-permute-done.refs_1_), channel_id=1, source_target_pairs={{0,1},{1,2},{2,3},{3,4},{4,5},{5,6},{6,7},{7,0},{8,9},{9,10},{10,1... | collective-permute-start | bytes 1179656 | tf_op jit(solution)/shard_map/ppermute | solution.py:53
  24.0 1.1 constant_dynamic-slice_fusion
  25.1 5.1 %collective-permute-start.1 = (bf16[96,1152]{1,0:T(8,128)(2,1)S(1)}, bf16[96,1152]{1,0:T(8,128)(2,1)S(1)}, u32[]{:S(2)}, u32[]{:S(2)}) collective-permute-start(bf16[96,1152]{1,0:T(8,128)(2,1)S(1)} %get-tuple-element.52), channel_id=1, source_target_pairs={{0,280},{32,312},{64,344},{96,376},{128,408},{160,440},{192,472},{... | collective-permute-start | bytes 663560 | tf_op jit(solution)/shard_map/ppermute | solution.py:42
  30.2 8.8 %collective-permute-done.1 = bf16[96,1152]{1,0:T(8,128)(2,1)S(1)} collective-permute-done((bf16[96,1152]{1,0:T(8,128)(2,1)S(1)}, bf16[96,1152]{1,0:T(8,128)(2,1)S(1)}, u32[]{:S(2)}, u32[]{:S(2)}) %collective-permute-start.1) | collective-permute-done | bytes 221216 | tf_op jit(solution)/shard_map/ppermute | solution.py:42
  39.0 2.4 %collective-permute-start.5 = (bf16[512,384]{1,0:T(8,128)(2,1)S(1)}, bf16[512,384]{1,0:T(8,128)(2,1)S(1)}, u32[]{:S(2)}, u32[]{:S(2)}) collective-permute-start(bf16[512,384]{1,0:T(8,128)(2,1)S(1)} %collective-permute-done.2.refs_2_), channel_id=1, source_target_pairs={{0,1},{1,2},{2,3},{3,4},{4,5},{5,6},{6,7},{7,0},{8,9},{9,10},{10,1... | collective-permute-start | bytes 1179656 | tf_op jit(solution)/shard_map/ppermute | solution.py:53
  41.5 0.7 copy-done.11
  42.2 4.3 %collective-permute-start.3 = (bf16[96,1152]{1,0:T(8,128)(2,1)S(1)}, bf16[96,1152]{1,0:T(8,128)(2,1)S(1)}, u32[]{:S(2)}, u32[]{:S(2)}) collective-permute-start(bf16[96,1152]{1,0:T(8,128)(2,1)S(1)} %get-tuple-element.51), channel_id=1, source_target_pairs={{0,280},{32,312},{64,344},{96,376},{128,408},{160,440},{192,472},{... | collective-permute-start | bytes 663560 | tf_op jit(solution)/shard_map/ppermute | solution.py:42
  46.6 9.0 %collective-permute-done.3 = bf16[96,1152]{1,0:T(8,128)(2,1)S(1)} collective-permute-done((bf16[96,1152]{1,0:T(8,128)(2,1)S(1)}, bf16[96,1152]{1,0:T(8,128)(2,1)S(1)}, u32[]{:S(2)}, u32[]{:S(2)}) %collective-permute-start.3) | collective-permute-done | bytes 221216 | tf_op jit(solution)/shard_map/ppermute | solution.py:42
  55.6 1.2 copy-done.5
  56.9 4.4 %collective-permute-start.6 = (bf16[192,1152]{1,0:T(8,128)(2,1)S(1)}, bf16[192,1152]{1,0:T(8,128)(2,1)}, u32[]{:S(2)}, u32[]{:S(2)}) collective-permute-start(bf16[192,1152]{1,0:T(8,128)(2,1)S(1)} %constant_dynamic-update-slice_fusion), channel_id=1, source_target_pairs={{0,32},{32,64},{64,96},{96,0},{128,224},{160,128},{192,160},{224,1... | collective-permute-start | bytes 1327112 | tf_op jit(solution)/shard_map/ppermute | solution.py:42
  61.3 1.9 %collective-permute-start.7 = (bf16[512,384]{1,0:T(8,128)(2,1)S(1)}, bf16[512,384]{1,0:T(8,128)(2,1)S(1)}, u32[]{:S(2)}, u32[]{:S(2)}) collective-permute-start(bf16[512,384]{1,0:T(8,128)(2,1)S(1)} %collective-permute-done.5.refs_3_), channel_id=1, source_target_pairs={{0,1},{1,2},{2,3},{3,4},{4,5},{5,6},{6,7},{7,0},{8,9},{9,10},{10,1... | collective-permute-start | bytes 1179656 | tf_op jit(solution)/shard_map/ppermute | solution.py:53
  63.2 0.7 copy-done.13
  64.0 6.1 %collective-permute-done.7.refs_4_ = bf16[512,384]{1,0:T(8,128)(2,1)S(1)} collective-permute-done((bf16[512,384]{1,0:T(8,128)(2,1)S(1)}, bf16[512,384]{1,0:T(8,128)(2,1)S(1)}, u32[]{:S(2)}, u32[]{:S(2)}) %collective-permute-start.7) | collective-permute-done | bytes 393248 | tf_op jit(solution)/shard_map/ppermute | solution.py:53
  70.1 2.4 %collective-permute-start.8 = (bf16[192,1152]{1,0:T(8,128)(2,1)}, bf16[192,1152]{1,0:T(8,128)(2,1)}, u32[]{:S(2)}, u32[]{:S(2)}) collective-permute-start(bf16[192,1152]{1,0:T(8,128)(2,1)} %collective-permute-done.6), channel_id=1, source_target_pairs={{0,32},{32,64},{64,96},{96,0},{128,224},{160,128},{192,160},{224,1... | collective-permute-start | bytes 1327112 | tf_op jit(solution)/shard_map/ppermute | solution.py:42
  72.6 2.8 %collective-permute-start.9 = (bf16[512,384]{1,0:T(8,128)(2,1)S(1)}, bf16[512,384]{1,0:T(8,128)(2,1)S(1)}, u32[]{:S(2)}, u32[]{:S(2)}) collective-permute-start(bf16[512,384]{1,0:T(8,128)(2,1)S(1)} %collective-permute-done.7.refs_4_), channel_id=1, source_target_pairs={{0,1},{1,2},{2,3},{3,4},{4,5},{5,6},{6,7},{7,0},{8,9},{9,10},{10,1... | collective-permute-start | bytes 1179656 | tf_op jit(solution)/shard_map/ppermute | solution.py:53
  75.7 5.8 %collective-permute-done.9.refs_5_ = bf16[512,384]{1,0:T(8,128)(2,1)S(1)} collective-permute-done((bf16[512,384]{1,0:T(8,128)(2,1)S(1)}, bf16[512,384]{1,0:T(8,128)(2,1)S(1)}, u32[]{:S(2)}, u32[]{:S(2)}) %collective-permute-start.9) | collective-permute-done | bytes 393248 | tf_op jit(solution)/shard_map/ppermute | solution.py:53
  81.5 3.6 %collective-permute-start.11 = (bf16[512,384]{1,0:T(8,128)(2,1)S(1)}, bf16[512,384]{1,0:T(8,128)(2,1)}, u32[]{:S(2)}, u32[]{:S(2)}) collective-permute-start(bf16[512,384]{1,0:T(8,128)(2,1)S(1)} %collective-permute-done.9.refs_5_), channel_id=1, source_target_pairs={{0,1},{1,2},{2,3},{3,4},{4,5},{5,6},{6,7},{7,0},{8,9},{9,10},{10,1... | collective-permute-start | bytes 1179656 | tf_op jit(solution)/shard_map/ppermute | solution.py:53
  85.1 2.2 %collective-permute-start.10 = (bf16[192,1152]{1,0:T(8,128)(2,1)}, bf16[192,1152]{1,0:T(8,128)(2,1)S(1)}, u32[]{:S(2)}, u32[]{:S(2)}) collective-permute-start(bf16[192,1152]{1,0:T(8,128)(2,1)} %collective-permute-done.8), channel_id=1, source_target_pairs={{0,32},{32,64},{64,96},{96,0},{128,224},{160,128},{192,160},{224,1... | collective-permute-start | bytes 1327112 | tf_op jit(solution)/shard_map/ppermute | solution.py:42
  87.3 1.1 constant_dynamic-update-slice_fusion.4
  88.4 1.1 constant_dynamic-update-slice_fusion.3
  90.1 4.7 %collective-permute-done.10 = bf16[192,1152]{1,0:T(8,128)(2,1)S(1)} collective-permute-done((bf16[192,1152]{1,0:T(8,128)(2,1)}, bf16[192,1152]{1,0:T(8,128)(2,1)S(1)}, u32[]{:S(2)}, u32[]{:S(2)}) %collective-permute-start.10) | collective-permute-done | bytes 442400 | tf_op jit(solution)/shard_map/ppermute | solution.py:42
  94.8 6.5 %collective-permute-start.13 = (bf16[768,1152]{1,0:T(8,128)(2,1)S(1)}, bf16[768,1152]{1,0:T(8,128)(2,1)S(1)}, u32[]{:S(2)}, u32[]{:S(2)}) collective-permute-start(bf16[768,1152]{1,0:T(8,128)(2,1)S(1)} %constant_dynamic-update-slice_fusion.2.refs_11_), channel_id=1, source_target_pairs={{0,128},{32,160},{64,192},{96,224},{128,0},{160,32},{192,64},{224,... | collective-permute-start | bytes 5308424 | tf_op jit(solution)/shard_map/ppermute | solution.py:42
  101.4 4.9 %collective-permute-start.12 = (bf16[512,384]{1,0:T(8,128)(2,1)}, bf16[512,384]{1,0:T(8,128)(2,1)}, u32[]{:S(2)}, u32[]{:S(2)}) collective-permute-start(bf16[512,384]{1,0:T(8,128)(2,1)} %collective-permute-done.11.refs_6_), channel_id=1, source_target_pairs={{0,1},{1,2},{2,3},{3,4},{4,5},{5,6},{6,7},{7,0},{8,9},{9,10},{10,1... | collective-permute-start | bytes 1179656 | tf_op jit(solution)/shard_map/ppermute | solution.py:53
  107.1 4.1 %collective-permute-done.12.refs_7_ = bf16[512,384]{1,0:T(8,128)(2,1)} collective-permute-done((bf16[512,384]{1,0:T(8,128)(2,1)}, bf16[512,384]{1,0:T(8,128)(2,1)}, u32[]{:S(2)}, u32[]{:S(2)}) %collective-permute-start.12) | collective-permute-done | bytes 393248 | tf_op jit(solution)/shard_map/ppermute | solution.py:53
  111.2 1.5 copy-done
  112.7 1.5 copy-done.6
  114.2 1.1 copy-done.7
  115.3 1.0 copy-done.8
  116.3 1.0 copy-done.10
  117.3 1.0 copy-done.12
  118.3 1.0 copy-done.14
  119.3 1.0 copy-done.16
  120.3 1.0 copy-done.18
  121.3 8.1 %gather.1 = (f32[512,1152]{1,0:T(8,128)S(1)}, bf16[512,768]{1,0:T(8,128)(2,1)S(1)}) custom-call(s32[12]{0:T(128)S(1)} %stack.51.spots.refs_0_, s32[1,1]{1,0:T(1,128)S(6)} %copy.14.levels, bf16[512,384]{1,0:T(8,128)(2,1)S(1)} %bitcast.23, bf16[512,384]{1,0:T(8,128)(2,1)S(1)} %copy-done.10, bf16[512,384]{1,0:T(8,128)(2,1)S(1)} %copy-done.12, ...), custom_call_target="tpu_custom_call" | custom-call | flops 2717908992 | bytes 12582912 | tf_op jit(solution)/shard_map/gather/pallas_call | solution.py:232
  129.5 1.5 project.1
  131.0 3.2 %collective-permute-start.15 = (bf16[512,768]{1,0:T(8,128)(2,1)S(1)}, bf16[512,768]{1,0:T(8,128)(2,1)S(1)}, u32[]{:S(2)}, u32[]{:S(2)}) collective-permute-start(bf16[512,768]{1,0:T(8,128)(2,1)S(1)} %get-tuple-element.43.own), channel_id=1, source_target_pairs={{0,128},{32,160},{64,192},{96,224},{128,0},{160,32},{192,64},{224,... | collective-permute-start | bytes 2359304 | tf_op jit(solution)/shard_map/ppermute | solution.py:42
  134.3 1.9 %collective-permute-start.14 = (bf16[512,768]{1,0:T(8,128)(2,1)S(1)}, bf16[512,768]{1,0:T(8,128)(2,1)S(1)}, u32[]{:S(2)}, u32[]{:S(2)}) collective-permute-start(bf16[512,768]{1,0:T(8,128)(2,1)S(1)} %get-tuple-element.43.own), channel_id=1, source_target_pairs={{0,16},{32,48},{64,80},{96,112},{128,400},{160,432},{192,464},{224... | collective-permute-start | bytes 2359304 | tf_op jit(solution)/shard_map/ppermute | solution.py:42
  136.2 3.9 %near.1 = (f32[512,384]{1,0:T(8,128)S(1)}, f32[512,384]{1,0:T(8,128)S(1)}) custom-call(s32[12]{0:T(128)S(1)} %stack.51.spots.refs_0_, s32[1,4]{1,0:T(1,128)S(1)} %copy-done.2, s32[4,4]{1,0:T(4,128)S(1)} %bitcast.17, bf16[512,384]{1,0:T(8,128)(2,1)S(1)} %get-tuple-element.42.q.refs_3_, bf16[512,768]{1,0:T(8,128)(2,1)S(1)} %get-tuple-element.43.own, ...), custom_call_target="tpu_custom_call" | custom-call | flops 805306368 | bytes 6291456 | tf_op jit(solution)/shard_map/near/pallas_call | solution.py:277
  140.1 15.6 %collective-permute-done.14 = bf16[512,768]{1,0:T(8,128)(2,1)S(1)} collective-permute-done((bf16[512,768]{1,0:T(8,128)(2,1)S(1)}, bf16[512,768]{1,0:T(8,128)(2,1)S(1)}, u32[]{:S(2)}, u32[]{:S(2)}) %collective-permute-start.14) | collective-permute-done | bytes 786464 | tf_op jit(solution)/shard_map/ppermute | solution.py:42
  155.7 1.4 collective-permute-start.16
  157.1 17.3 %collective-permute-done.16.refs_6_ = bf16[512,768]{1,0:T(8,128)(2,1)S(1)} collective-permute-done((bf16[512,768]{1,0:T(8,128)(2,1)S(1)}, bf16[512,768]{1,0:T(8,128)(2,1)S(1)}, u32[]{:S(2)}, u32[]{:S(2)}) %collective-permute-start.16) | collective-permute-done | bytes 786464 | tf_op jit(solution)/shard_map/ppermute | solution.py:42
  174.4 1.9 %collective-permute-start.17 = (bf16[512,768]{1,0:T(8,128)(2,1)S(1)}, bf16[512,768]{1,0:T(8,128)(2,1)S(1)}, u32[]{:S(2)}, u32[]{:S(2)}) collective-permute-start(bf16[512,768]{1,0:T(8,128)(2,1)S(1)} %collective-permute-done.16.refs_6_), channel_id=1, source_target_pairs={{0,128},{32,160},{64,192},{96,224},{128,0},{160,32},{192,64},{224,... | collective-permute-start | bytes 2359304 | tf_op jit(solution)/shard_map/ppermute | solution.py:42
  176.3 0.7 far.1
  177.0 1.6 collective-permute-done.17.refs_6_
  178.6 1.7 last.1
  (40 shorter events, 1.1 us)
Async XLA Ops:
  0.0 55.6 %collective-permute-start.4 = (bf16[768,1152]{1,0:T(8,128)(2,1)}, bf16[768,1152]{1,0:T(8,128)(2,1)S(1)}, u32[]{:S(2)}, u32[]{:S(2)}) collective-permute-start(bf16[768,1152]{1,0:T(8,128)(2,1)} %refs_9_.1), channel_id=1, source_target_pairs={{0,128},{32,160},{64,192},{96,224},{128,0},{160,32},{192,64},{224,... | collective-permute-start | bytes 5308424 | tf_op jit(solution)/shard_map/ppermute | solution.py:42
  8.8 10.3 %collective-permute-start = (bf16[512,384]{1,0:T(8,128)(2,1)}, bf16[512,384]{1,0:T(8,128)(2,1)S(1)}, u32[]{:S(2)}, u32[]{:S(2)}) collective-permute-start(bf16[512,384]{1,0:T(8,128)(2,1)} %bitcast.22), channel_id=1, source_target_pairs={{0,1},{1,2},{2,3},{3,4},{4,5},{5,6},{6,7},{7,0},{8,9},{9,10},{10,1... | collective-permute-start | bytes 1179656 | tf_op jit(solution)/shard_map/ppermute | solution.py:53
  19.1 56.5 %copy-start.9 = (bf16[512,384]{1,0:T(8,128)(2,1)}, bf16[512,384]{1,0:T(8,128)(2,1)S(1)}, u32[]{:S(2)}) copy-start(bf16[512,384]{1,0:T(8,128)(2,1)S(1)} %collective-permute-done.refs_1_) | copy-start | bytes 1179652
  19.1 19.9 %collective-permute-start.2 = (bf16[512,384]{1,0:T(8,128)(2,1)S(1)}, bf16[512,384]{1,0:T(8,128)(2,1)S(1)}, u32[]{:S(2)}, u32[]{:S(2)}) collective-permute-start(bf16[512,384]{1,0:T(8,128)(2,1)S(1)} %collective-permute-done.refs_1_), channel_id=1, source_target_pairs={{0,1},{1,2},{2,3},{3,4},{4,5},{5,6},{6,7},{7,0},{8,9},{9,10},{10,1... | collective-permute-start | bytes 1179656 | tf_op jit(solution)/shard_map/ppermute | solution.py:53
  25.1 13.9 %collective-permute-start.1 = (bf16[96,1152]{1,0:T(8,128)(2,1)S(1)}, bf16[96,1152]{1,0:T(8,128)(2,1)S(1)}, u32[]{:S(2)}, u32[]{:S(2)}) collective-permute-start(bf16[96,1152]{1,0:T(8,128)(2,1)S(1)} %get-tuple-element.52), channel_id=1, source_target_pairs={{0,280},{32,312},{64,344},{96,376},{128,408},{160,440},{192,472},{... | collective-permute-start | bytes 663560 | tf_op jit(solution)/shard_map/ppermute | solution.py:42
  39.0 16.5 %collective-permute-start.5 = (bf16[512,384]{1,0:T(8,128)(2,1)S(1)}, bf16[512,384]{1,0:T(8,128)(2,1)S(1)}, u32[]{:S(2)}, u32[]{:S(2)}) collective-permute-start(bf16[512,384]{1,0:T(8,128)(2,1)S(1)} %collective-permute-done.2.refs_2_), channel_id=1, source_target_pairs={{0,1},{1,2},{2,3},{3,4},{4,5},{5,6},{6,7},{7,0},{8,9},{9,10},{10,1... | collective-permute-start | bytes 1179656 | tf_op jit(solution)/shard_map/ppermute | solution.py:53
  41.5 0.7 copy-start.11
  42.2 13.4 %collective-permute-start.3 = (bf16[96,1152]{1,0:T(8,128)(2,1)S(1)}, bf16[96,1152]{1,0:T(8,128)(2,1)S(1)}, u32[]{:S(2)}, u32[]{:S(2)}) collective-permute-start(bf16[96,1152]{1,0:T(8,128)(2,1)S(1)} %get-tuple-element.51), channel_id=1, source_target_pairs={{0,280},{32,312},{64,344},{96,376},{128,408},{160,440},{192,472},{... | collective-permute-start | bytes 663560 | tf_op jit(solution)/shard_map/ppermute | solution.py:42
  55.6 1.2 copy-start.5
  56.9 13.2 %collective-permute-start.6 = (bf16[192,1152]{1,0:T(8,128)(2,1)S(1)}, bf16[192,1152]{1,0:T(8,128)(2,1)}, u32[]{:S(2)}, u32[]{:S(2)}) collective-permute-start(bf16[192,1152]{1,0:T(8,128)(2,1)S(1)} %constant_dynamic-update-slice_fusion), channel_id=1, source_target_pairs={{0,32},{32,64},{64,96},{96,0},{128,224},{160,128},{192,160},{224,1... | collective-permute-start | bytes 1327112 | tf_op jit(solution)/shard_map/ppermute | solution.py:42
  61.3 8.8 %collective-permute-start.7 = (bf16[512,384]{1,0:T(8,128)(2,1)S(1)}, bf16[512,384]{1,0:T(8,128)(2,1)S(1)}, u32[]{:S(2)}, u32[]{:S(2)}) collective-permute-start(bf16[512,384]{1,0:T(8,128)(2,1)S(1)} %collective-permute-done.5.refs_3_), channel_id=1, source_target_pairs={{0,1},{1,2},{2,3},{3,4},{4,5},{5,6},{6,7},{7,0},{8,9},{9,10},{10,1... | collective-permute-start | bytes 1179656 | tf_op jit(solution)/shard_map/ppermute | solution.py:53
  63.2 0.8 copy-start.13
  70.1 18.3 %copy-start.15 = (bf16[512,384]{1,0:T(8,128)(2,1)}, bf16[512,384]{1,0:T(8,128)(2,1)S(1)}, u32[]{:S(2)}) copy-start(bf16[512,384]{1,0:T(8,128)(2,1)S(1)} %collective-permute-done.7.refs_4_) | copy-start | bytes 1179652
  70.1 11.4 %collective-permute-start.8 = (bf16[192,1152]{1,0:T(8,128)(2,1)}, bf16[192,1152]{1,0:T(8,128)(2,1)}, u32[]{:S(2)}, u32[]{:S(2)}) collective-permute-start(bf16[192,1152]{1,0:T(8,128)(2,1)} %collective-permute-done.6), channel_id=1, source_target_pairs={{0,32},{32,64},{64,96},{96,0},{128,224},{160,128},{192,160},{224,1... | collective-permute-start | bytes 1327112 | tf_op jit(solution)/shard_map/ppermute | solution.py:42
  72.6 8.9 %collective-permute-start.9 = (bf16[512,384]{1,0:T(8,128)(2,1)S(1)}, bf16[512,384]{1,0:T(8,128)(2,1)S(1)}, u32[]{:S(2)}, u32[]{:S(2)}) collective-permute-start(bf16[512,384]{1,0:T(8,128)(2,1)S(1)} %collective-permute-done.7.refs_4_), channel_id=1, source_target_pairs={{0,1},{1,2},{2,3},{3,4},{4,5},{5,6},{6,7},{7,0},{8,9},{9,10},{10,1... | collective-permute-start | bytes 1179656 | tf_op jit(solution)/shard_map/ppermute | solution.py:53
  81.5 13.3 %copy-start.17 = (bf16[512,384]{1,0:T(8,128)(2,1)}, bf16[512,384]{1,0:T(8,128)(2,1)S(1)}, u32[]{:S(2)}) copy-start(bf16[512,384]{1,0:T(8,128)(2,1)S(1)} %collective-permute-done.9.refs_5_) | copy-start | bytes 1179652
  81.5 8.6 %collective-permute-start.11 = (bf16[512,384]{1,0:T(8,128)(2,1)S(1)}, bf16[512,384]{1,0:T(8,128)(2,1)}, u32[]{:S(2)}, u32[]{:S(2)}) collective-permute-start(bf16[512,384]{1,0:T(8,128)(2,1)S(1)} %collective-permute-done.9.refs_5_), channel_id=1, source_target_pairs={{0,1},{1,2},{2,3},{3,4},{4,5},{5,6},{6,7},{7,0},{8,9},{9,10},{10,1... | collective-permute-start | bytes 1179656 | tf_op jit(solution)/shard_map/ppermute | solution.py:53
  85.1 9.7 %collective-permute-start.10 = (bf16[192,1152]{1,0:T(8,128)(2,1)}, bf16[192,1152]{1,0:T(8,128)(2,1)S(1)}, u32[]{:S(2)}, u32[]{:S(2)}) collective-permute-start(bf16[192,1152]{1,0:T(8,128)(2,1)} %collective-permute-done.8), channel_id=1, source_target_pairs={{0,32},{32,64},{64,96},{96,0},{128,224},{160,128},{192,160},{224,1... | collective-permute-start | bytes 1327112 | tf_op jit(solution)/shard_map/ppermute | solution.py:42
  94.8 34.6 %collective-permute-start.13 = (bf16[768,1152]{1,0:T(8,128)(2,1)S(1)}, bf16[768,1152]{1,0:T(8,128)(2,1)S(1)}, u32[]{:S(2)}, u32[]{:S(2)}) collective-permute-start(bf16[768,1152]{1,0:T(8,128)(2,1)S(1)} %constant_dynamic-update-slice_fusion.2.refs_11_), channel_id=1, source_target_pairs={{0,128},{32,160},{64,192},{96,224},{128,0},{160,32},{192,64},{224,... | collective-permute-start | bytes 5308424 | tf_op jit(solution)/shard_map/ppermute | solution.py:42
  101.4 9.9 %collective-permute-start.12 = (bf16[512,384]{1,0:T(8,128)(2,1)}, bf16[512,384]{1,0:T(8,128)(2,1)}, u32[]{:S(2)}, u32[]{:S(2)}) collective-permute-start(bf16[512,384]{1,0:T(8,128)(2,1)} %collective-permute-done.11.refs_6_), channel_id=1, source_target_pairs={{0,1},{1,2},{2,3},{3,4},{4,5},{5,6},{6,7},{7,0},{8,9},{9,10},{10,1... | collective-permute-start | bytes 1179656 | tf_op jit(solution)/shard_map/ppermute | solution.py:53
  111.2 1.5 copy-start
  112.7 1.5 copy-start.6
  114.2 1.1 copy-start.7
  115.3 1.0 copy-start.8
  116.3 1.0 copy-start.10
  117.3 1.0 copy-start.12
  118.3 1.0 copy-start.14
  119.3 1.0 copy-start.16
  120.3 1.0 copy-start.18
  121.3 8.1 %copy-start.3 = (f32[128]{0:T(128)S(1)}, f32[128]{0:T(128)}, u32[]{:S(2)}) copy-start(f32[128]{0:T(128)} %param.14) | copy-start | bytes 1540
  121.3 8.1 %copy-start.4 = (f32[128]{0:T(128)S(1)}, f32[128]{0:T(128)}, u32[]{:S(2)}) copy-start(f32[128]{0:T(128)} %param.15) | copy-start | bytes 1540
  129.4 6.8 %copy-start.1 = (s32[1,4,4]{2,1,0:T(4,128)S(1)}, s32[1,4,4]{2,1,0:T(4,128)}, u32[]{:S(2)}) copy-start(s32[1,4,4]{2,1,0:T(4,128)} %param.11) | copy-start | bytes 196
  129.5 6.8 %copy-start.2 = (s32[1,4]{1,0:T(1,128)S(1)}, s32[1,4]{1,0:T(1,128)}, u32[]{:S(2)}) copy-start(s32[1,4]{1,0:T(1,128)} %refs_1_.3) | copy-start | bytes 52
  131.0 5.2 %collective-permute-start.15 = (bf16[512,768]{1,0:T(8,128)(2,1)S(1)}, bf16[512,768]{1,0:T(8,128)(2,1)S(1)}, u32[]{:S(2)}, u32[]{:S(2)}) collective-permute-start(bf16[512,768]{1,0:T(8,128)(2,1)S(1)} %get-tuple-element.43.own), channel_id=1, source_target_pairs={{0,128},{32,160},{64,192},{96,224},{128,0},{160,32},{192,64},{224,... | collective-permute-start | bytes 2359304 | tf_op jit(solution)/shard_map/ppermute | solution.py:42
  134.3 21.4 %collective-permute-start.14 = (bf16[512,768]{1,0:T(8,128)(2,1)S(1)}, bf16[512,768]{1,0:T(8,128)(2,1)S(1)}, u32[]{:S(2)}, u32[]{:S(2)}) collective-permute-start(bf16[512,768]{1,0:T(8,128)(2,1)S(1)} %get-tuple-element.43.own), channel_id=1, source_target_pairs={{0,16},{32,48},{64,80},{96,112},{128,400},{160,432},{192,464},{224... | collective-permute-start | bytes 2359304 | tf_op jit(solution)/shard_map/ppermute | solution.py:42
  155.7 18.8 %collective-permute-start.16 = (bf16[512,768]{1,0:T(8,128)(2,1)S(1)}, bf16[512,768]{1,0:T(8,128)(2,1)S(1)}, u32[]{:S(2)}, u32[]{:S(2)}) collective-permute-start(bf16[512,768]{1,0:T(8,128)(2,1)S(1)} %collective-permute-done.14), channel_id=1, source_target_pairs={{16,256},{48,288},{80,320},{112,352},{400,384},{432,416},{464,448}... | collective-permute-start | bytes 2359304 | tf_op jit(solution)/shard_map/ppermute | solution.py:42
  174.4 4.2 %collective-permute-start.17 = (bf16[512,768]{1,0:T(8,128)(2,1)S(1)}, bf16[512,768]{1,0:T(8,128)(2,1)S(1)}, u32[]{:S(2)}, u32[]{:S(2)}) collective-permute-start(bf16[512,768]{1,0:T(8,128)(2,1)S(1)} %collective-permute-done.16.refs_6_), channel_id=1, source_target_pairs={{0,128},{32,160},{64,192},{96,224},{128,0},{160,32},{192,64},{224,... | collective-permute-start | bytes 2359304 | tf_op jit(solution)/shard_map/ppermute | solution.py:42

commit v4 on v2

v4 whole, which is shorter than its diff:
```python
import functools
import math

import jax
import jax.numpy as jnp
from jax import lax
from jax.experimental import pallas as pl
from jax.experimental.pallas import tpu as pltpu
from jax.sharding import PartitionSpec as P

HD = 128
TPF = 64
EPS = 1e-06
MIB = 1 << 20

HALVES, CORES, XS, YS = 2, 2, 4, 4
RING_Y = HALVES * YS


def place(y, core, x):
    return ((y // YS) * CORES + core) * (XS * YS) + x * YS + y % YS


def pairs(move, keep=lambda y: True):
    out = []
    for y in range(RING_Y):
        for core in range(CORES):
            for x in range(XS):
                if keep(y):
                    out.append((place(y, core, x), place(*move(y, core, x))))
    return out


MIRROR = pairs(lambda y, core, x: (RING_Y - 1 - y, core, x))
X_UP = pairs(lambda y, core, x: (y, core, (x + 1) % XS))
X_DOWN = pairs(lambda y, core, x: (y, core, (x - 1) % XS))
SWAP = pairs(lambda y, core, x: (y, 1 - core, x))
UP_FIRST = pairs(lambda y, core, x: (y + 2, core, x), lambda y: y < 4)
UP_SECOND = pairs(lambda y, core, x: (y + 2, core, x), lambda y: 2 <= y < 6)
DOWN_FIRST = pairs(lambda y, core, x: ((y - 2) % 8, core, x), lambda y: y < 4)
DOWN_SECOND = pairs(lambda y, core, x: (y - 2 if y >= 6 else y + 6, core, x), lambda y: y >= 6 or y < 2)


def move(array, table):
    return lax.ppermute(array, ("block", "req"), table)


def project_kernel(n_pieces, starts, levels, *refs):
    tokens_far, table, q_gain, k_gain = refs[:4]
    pieces = refs[4 : 4 + n_pieces]
    q_out, kv_out, lo_out, hi_out, tokens, mod, weight, normed, token_sems, mod_sem, sems = refs[4 + n_pieces :]
    parts, rows, depth = tokens.shape
    features = parts * depth
    chunks = token_sems.shape[0]
    chunk = rows // chunks
    step_rows = 64

    mod_load = pltpu.make_async_copy(table.at[levels[0, 0]], mod, mod_sem)
    mod_load.start()
    loads = []
    for number in range(chunks):
        band = pl.ds(number * chunk, chunk)
        loads.append(pltpu.make_async_copy(tokens_far.at[:, band, :], tokens.at[:, band, :], token_sems.at[number]))
        loads[-1].start()
    weights = []
    for number, piece in enumerate(pieces):
        band = pl.ds(pl.multiple_of(starts[number], 96), piece.shape[0])
        weights.append(pltpu.make_async_copy(piece, weight.at[band, :], sems.at[number]))
        weights[-1].start()
    mod_load.wait()

    for number in range(chunks):
        loads[number].wait()

        def norm_rows(step, carry, number=number):
            band = pl.ds(pl.multiple_of(number * chunk + step * step_rows, step_rows), step_rows)
            total = jnp.zeros((step_rows, 128), jnp.float32)
            for part in range(parts):
                wide = tokens[part, band, :].astype(jnp.float32)
                square = wide * wide
                for lane in range(0, depth, 128):
                    total = total + square[:, lane : lane + 128]
            scale = lax.rsqrt(jnp.sum(total, axis=-1, keepdims=True) * (1.0 / features) + EPS)
            for part in range(parts):
                span = slice(part * depth, (part + 1) * depth)
                wide = tokens[part, band, :].astype(jnp.float32)
                row = wide * scale * (1.0 + mod[0:1, span]) + mod[1:2, span]
                normed[band, span] = row.astype(jnp.bfloat16)
            return carry

        lax.fori_loop(0, chunk // step_rows, norm_rows, 0)
    for copy in weights:
        copy.wait()

    heads = q_out.shape[1] // HD

    def head_norm(part, gain):
        scale = lax.rsqrt(jnp.mean(part * part, axis=-1, keepdims=True) + EPS)
        return (part * scale * gain).astype(jnp.bfloat16)

    for head in range(heads):
        span = slice(3 * HD * head, 3 * HD * (head + 1))
        out = jnp.dot(normed[...], weight[:, span], preferred_element_type=jnp.float32)
        q_out[:, HD * head : HD * (head + 1)] = head_norm(out[:, :HD], q_gain[...])
        keys = head_norm(out[:, HD : 2 * HD], k_gain[...])
        values = out[:, 2 * HD :].astype(jnp.bfloat16)
        for item, at in ((keys, HD * head), (values, HD * (heads + head))):
            kv_out[:, at : at + HD] = item
            lo_out[:, at : at + HD] = item[: rows // 2]
            hi_out[:, at : at + HD] = item[rows // 2 :]


def key_limit(spots, frames, mask, number):
    block, segment = spots[0], spots[number]
    seen = (segment == block) | ((segment < block) & (mask[block, segment] == 1))
    return jnp.where(seen, frames[0, segment] * TPF, 0)


def attend_part(limit, first, q, kv, num, den, heads):
    rows = 256
    keys = kv.shape[0]
    column = lax.broadcasted_iota(jnp.int32, (1, keys), 1) + first
    keep = column < limit
    factor = HD ** (-0.5) * math.log2(math.e)
    for head in range(heads):
        span = slice(HD * head, HD * (head + 1))
        k = kv[:, span]
        v = kv[:, HD * (heads + head) : HD * (heads + head + 1)]
        for top in range(0, q.shape[0], rows):
            band = slice(top, top + rows)
            scores = lax.dot_general(
                q[band, span], k, (((1,), (1,)), ((), ())), preferred_element_type=jnp.float32
            )
            weights = jnp.where(keep, jnp.exp2(scores * factor), 0.0)
            total = weights[:, :128]
            for lane in range(128, keys, 128):
                total = total + weights[:, lane : lane + 128]
            den[band, span] += total
            num[band, span] += jnp.dot(weights.astype(jnp.bfloat16), v, preferred_element_type=jnp.float32)


def near_kernel(spots, frames, mask, q, own, pair, num, den):
    heads = q.shape[1] // HD
    half = q.shape[0] // 2
    num[...] = jnp.zeros_like(num)
    den[...] = jnp.zeros_like(den)
    for number, kv in ((0, own), (1, pair)):
        limit = key_limit(spots, frames, mask, number)
        for first in (0, half):
            @pl.when(limit > first)
            def _(limit=limit, first=first, kv=kv):
                attend_part(limit, first, q, kv.at[first : first + half], num, den, heads)


def far_kernel(number, finish, spots, frames, mask, q, num_in, den_in, *rest):
    heads = q.shape[1] // HD
    half = q.shape[0] // 2
    num, den = rest[-2:]
    if finish:
        lo, hi = rest[0].at[:half], rest[0].at[half:]
    else:
        lo, hi = rest[:2]
    num[...] = num_in[...]
    den[...] = den_in[...]
    limit = key_limit(spots, frames, mask, number)
    for first, kv in ((0, lo), (half, hi)):
        @pl.when(limit > first)
        def _(first=first, kv=kv):
            attend_part(limit, first, q, kv, num, den, heads)
    if finish:
        for head in range(heads):
            span = slice(HD * head, HD * (head + 1))
            total = jnp.sum(den[:, span], axis=-1, keepdims=True)
            rest[1][:, span] = (num[:, span] / total).astype(jnp.bfloat16)


def body(tokens, levels, frames, segment_mask, mod_table, w_qkv, q_gain, k_gain):
    own = tokens[0, 0]
    rows, depth = own.shape
    ring = mod_table.shape[2] // depth
    part_rows, columns = w_qkv.shape
    heads = columns // (3 * HD)
    width = heads * HD
    quarter = part_rows // XS
    half = rows // 2

    block = lax.axis_index("block")
    side, core = block // CORES, block % CORES
    x = lax.axis_index("req") // YS
    other = (1 - side) * CORES
    spots = jnp.stack([block, side * CORES + 1 - core, other + core, other + 1 - core]).astype(jnp.int32)

    whole = lax.all_gather(own, "head", axis=0, tiled=False)

    w_pair = move(w_qkv, SWAP)
    first = move(lax.dynamic_slice_in_dim(w_qkv, quarter * x, quarter), MIRROR)
    up, down = move(first, X_UP), move(first, X_DOWN)
    far_a, far_b = move(up[: quarter // 2], X_UP), move(down[quarter // 2 :], X_DOWN)
    held = [(first, 0, 0), (up, 3, 0), (down, 1, 0), (far_a, 2, 0), (far_b, 2, quarter // 2)]
    pieces, starts = [w_qkv, w_pair], [block * part_rows, (side * CORES + 1 - core) * part_rows]
    for piece, away, at in held:
        row = (x + away) % XS * quarter + at
        pieces += [piece, move(piece, SWAP)]
        starts += [(other + core) * part_rows + row, (other + 1 - core) * part_rows + row]
    starts = jnp.stack(starts).astype(jnp.int32)

    smem = pl.BlockSpec(memory_space=pltpu.SMEM)
    vmem = pl.BlockSpec(memory_space=pltpu.VMEM)
    hbm = pl.BlockSpec(memory_space=pltpu.HBM)

    def sized(limit):
        return pltpu.CompilerParams(vmem_limit_bytes=int(limit * MIB))

    chunks = 4
    queries, kv, kv_lo, kv_hi = pl.pallas_call(
        functools.partial(project_kernel, len(pieces)),
        out_shape=(
            jax.ShapeDtypeStruct((rows, width), jnp.bfloat16),
            jax.ShapeDtypeStruct((rows, 2 * width), jnp.bfloat16),
            jax.ShapeDtypeStruct((half, 2 * width), jnp.bfloat16),
            jax.ShapeDtypeStruct((half, 2 * width), jnp.bfloat16),
        ),
        in_specs=[smem] * 2 + [hbm] * 2 + [vmem] * 2 + [hbm] * len(pieces),
        out_specs=(vmem,) * 4,
        scratch_shapes=[
            pltpu.VMEM((ring, rows, depth), jnp.bfloat16),
            pltpu.VMEM(mod_table.shape[1:], jnp.float32),
            pltpu.VMEM((ring * depth, columns), jnp.bfloat16),
            pltpu.VMEM((rows, ring * depth), jnp.bfloat16),
            pltpu.SemaphoreType.DMA((chunks,)),
            pltpu.SemaphoreType.DMA,
            pltpu.SemaphoreType.DMA((len(pieces),)),
        ],
        compiler_params=sized(61.5),
        cost_estimate=pl.CostEstimate(
            flops=2 * rows * ring * depth * columns, bytes_accessed=12 * MIB, transcendentals=0
        ),
        name="project",
    )(starts, levels, whole, mod_table, q_gain[None, :], k_gain[None, :], *pieces)

    far_lo = move(kv_lo, UP_FIRST)
    far_hi = move(kv_hi, DOWN_FIRST)
    pair_kv = move(kv, SWAP)

    where = (spots, frames, segment_mask[0])
    sums = (jax.ShapeDtypeStruct((rows, width), jnp.float32),) * 2
    work = pl.CostEstimate(
        flops=8 * rows * rows * width, bytes_accessed=6 * MIB, transcendentals=2 * rows * rows * heads
    )
    num, den = pl.pallas_call(
        near_kernel,
        out_shape=sums,
        in_specs=[smem] * 3 + [vmem] * 3,
        out_specs=(vmem, vmem),
        compiler_params=sized(24),
        cost_estimate=work,
        name="near",
    )(*where, queries, kv, pair_kv)
    far_lo, far_hi, num, den = lax.optimization_barrier((far_lo, far_hi, num, den))
    far_lo = move(far_lo, UP_SECOND)
    far_hi = move(far_hi, DOWN_SECOND)
    far_kv = lax.optimization_barrier(jnp.concatenate([far_lo, far_hi]))
    far_pair = move(far_kv, SWAP)
    num, den = pl.pallas_call(
        lambda *refs: far_kernel(2, False, *refs),
        out_shape=sums,
        in_specs=[smem] * 3 + [vmem] * 5,
        out_specs=(vmem, vmem),
        compiler_params=sized(24),
        cost_estimate=work,
        name="far",
    )(*where, queries, num, den, far_lo, far_hi)
    result = pl.pallas_call(
        lambda *refs: far_kernel(3, True, *refs),
        out_shape=jax.ShapeDtypeStruct((rows, width), jnp.bfloat16),
        in_specs=[smem] * 3 + [vmem] * 4,
        out_specs=vmem,
        scratch_shapes=[pltpu.VMEM((rows, width), jnp.float32)] * 2,
        compiler_params=sized(24),
        cost_estimate=work,
        name="last",
    )(*where, queries, num, den, far_pair)
    return result.reshape(1, 1, rows, width)


def solution(mesh):
    placed = (
        P("req", "block", None, "head"),
        P("req", "block"),
        P("req", None),
        P("req", None, None),
        P(),
        P("block", "head"),
        P(),
        P(),
    )
    return jax.shard_map(
        body, mesh=mesh, in_specs=placed, out_specs=P("req", "block", None, "head"), check_vma=False
    )
```

time: 170 us -> 143 us (0.84)
  the two profiles are of different devices: /device:TPU:41 before, /device:TPU:1 now
where the time goes in v4:
time: 143 us; the launch traced here: 141 us
  waiting for transfers between devices  58.5 us (41%)
  starting transfers between devices  45 us (31%)
  Pallas kernels  18 us (13%)
  between operations  14.5 us (10%)
  local copies, waits for them, and re-layouts  4.81 us (3%)
    ppermute x17, waiting for transfers between devices, move(): return lax.ppermute(array, ('block', 'req'), table)  57.7 us
    ppermute x17, starting transfers between devices, move(): return lax.ppermute(array, ('block', 'req'), table)  45 us
    pallas_call x1, Pallas kernels, body(): pl.pallas_call(functools.partial(project_kernel, len(pieces)), out_shape=...  12.6 us
    unnamed x26, local copies, waits for them, and re-layouts  3.12 us
    pallas_call x1, Pallas kernels, body(): pl.pallas_call(near_kernel, out_shape=sums, in_specs=[smem] * 3 + [vmem]...  3.03 us
  transfers between devices with their start and end apart: 18, of which 6 were waited for; matrix products, arithmetic and copies ran while one was open for 1% of the time, Pallas kernels for 3%

profile of v4, /device:TPU:1, one launch (start us, length us, event | category | flops | bytes accessed | tf_op | source)
XLA Modules:
  0.0 140.9 jit_solution(10215339347310174460)
XLA Ops:
  6.5 0.7 all-gather.3.cloned.1.call-update
  7.3 8.8 %collective-permute-start = (bf16[768,1152]{1,0:T(8,128)(2,1)}, bf16[768,1152]{1,0:T(8,128)(2,1)}, u32[]{:S(2)}, u32[]{:S(2)}) collective-permute-start(bf16[768,1152]{1,0:T(8,128)(2,1)} %refs_4_.1), channel_id=1, source_target_pairs={{0,128},{32,160},{64,192},{96,224},{128,0},{160,32},{192,64},{224,... | collective-permute-start | bytes 5308424 | tf_op jit(solution)/shard_map/ppermute | solution.py:45
  16.1 1.1 constant_dynamic-slice_fusion
  17.1 1.9 %collective-permute-start.1 = (bf16[192,1152]{1,0:T(8,128)(2,1)S(1)}, bf16[192,1152]{1,0:T(8,128)(2,1)S(1)}, u32[]{:S(2)}, u32[]{:S(2)}) collective-permute-start(bf16[192,1152]{1,0:T(8,128)(2,1)S(1)} %constant_dynamic-slice_fusion), channel_id=1, source_target_pairs={{0,280},{32,312},{64,344},{96,376},{128,408},{160,440},{192,472},{... | collective-permute-start | bytes 1327112 | tf_op jit(solution)/shard_map/ppermute | solution.py:45
  19.1 19.4 %collective-permute-done.1.refs_6_ = bf16[192,1152]{1,0:T(8,128)(2,1)S(1)} collective-permute-done((bf16[192,1152]{1,0:T(8,128)(2,1)S(1)}, bf16[192,1152]{1,0:T(8,128)(2,1)S(1)}, u32[]{:S(2)}, u32[]{:S(2)}) %collective-permute-start.1) | collective-permute-done | bytes 442400 | tf_op jit(solution)/shard_map/ppermute | solution.py:45
  38.5 2.8 %collective-permute-start.5 = (bf16[192,1152]{1,0:T(8,128)(2,1)S(1)}, bf16[192,1152]{1,0:T(8,128)(2,1)S(1)}, u32[]{:S(2)}, u32[]{:S(2)}) collective-permute-start(bf16[192,1152]{1,0:T(8,128)(2,1)S(1)} %collective-permute-done.1.refs_6_), channel_id=1, source_target_pairs={{0,96},{32,0},{64,32},{96,64},{128,224},{160,128},{192,160},{224,1... | collective-permute-start | bytes 1327112 | tf_op jit(solution)/shard_map/ppermute | solution.py:45
  41.3 2.4 %collective-permute-start.3 = (bf16[192,1152]{1,0:T(8,128)(2,1)S(1)}, bf16[192,1152]{1,0:T(8,128)(2,1)S(1)}, u32[]{:S(2)}, u32[]{:S(2)}) collective-permute-start(bf16[192,1152]{1,0:T(8,128)(2,1)S(1)} %collective-permute-done.1.refs_6_), channel_id=1, source_target_pairs={{0,32},{32,64},{64,96},{96,0},{128,160},{160,192},{192,224},{224,1... | collective-permute-start | bytes 1327112 | tf_op jit(solution)/shard_map/ppermute | solution.py:45
  43.8 2.8 %collective-permute-start.2 = (bf16[192,1152]{1,0:T(8,128)(2,1)S(1)}, bf16[192,1152]{1,0:T(8,128)(2,1)S(1)}, u32[]{:S(2)}, u32[]{:S(2)}) collective-permute-start(bf16[192,1152]{1,0:T(8,128)(2,1)S(1)} %collective-permute-done.1.refs_6_), channel_id=1, source_target_pairs={{0,128},{32,160},{64,192},{96,224},{128,0},{160,32},{192,64},{224,... | collective-permute-start | bytes 1327112 | tf_op jit(solution)/shard_map/ppermute | solution.py:45
  46.6 5.3 %collective-permute-done.5.refs_10_ = bf16[192,1152]{1,0:T(8,128)(2,1)S(1)} collective-permute-done((bf16[192,1152]{1,0:T(8,128)(2,1)S(1)}, bf16[192,1152]{1,0:T(8,128)(2,1)S(1)}, u32[]{:S(2)}, u32[]{:S(2)}) %collective-permute-start.5) | collective-permute-done | bytes 442400 | tf_op jit(solution)/shard_map/ppermute | solution.py:45
  51.9 3.9 %collective-permute-start.9 = (bf16[96,1152]{1,0:T(8,128)(2,1)S(1)}, bf16[96,1152]{1,0:T(8,128)(2,1)S(1)}, u32[]{:S(2)}, u32[]{:S(2)}) collective-permute-start(bf16[96,1152]{1,0:T(8,128)(2,1)S(1)} %slice.9), channel_id=1, source_target_pairs={{0,96},{32,0},{64,32},{96,64},{128,224},{160,128},{192,160},{224,1... | collective-permute-start | bytes 663560 | tf_op jit(solution)/shard_map/ppermute | solution.py:45
  55.8 0.0 collective-permute-done.3.refs_8_
  55.9 1.9 %collective-permute-start.7 = (bf16[96,1152]{1,0:T(8,128)(2,1)S(1)}, bf16[96,1152]{1,0:T(8,128)(2,1)S(1)}, u32[]{:S(2)}, u32[]{:S(2)}) collective-permute-start(bf16[96,1152]{1,0:T(8,128)(2,1)S(1)} %slice.8), channel_id=1, source_target_pairs={{0,32},{32,64},{64,96},{96,0},{128,160},{160,192},{192,224},{224,1... | collective-permute-start | bytes 663560 | tf_op jit(solution)/shard_map/ppermute | solution.py:45
  57.8 3.4 %collective-permute-start.6 = (bf16[192,1152]{1,0:T(8,128)(2,1)S(1)}, bf16[192,1152]{1,0:T(8,128)(2,1)S(1)}, u32[]{:S(2)}, u32[]{:S(2)}) collective-permute-start(bf16[192,1152]{1,0:T(8,128)(2,1)S(1)} %collective-permute-done.5.refs_10_), channel_id=1, source_target_pairs={{0,128},{32,160},{64,192},{96,224},{128,0},{160,32},{192,64},{224,... | collective-permute-start | bytes 1327112 | tf_op jit(solution)/shard_map/ppermute | solution.py:45
  61.2 0.0 collective-permute-done.2.refs_7_
  61.3 1.9 %collective-permute-start.4 = (bf16[192,1152]{1,0:T(8,128)(2,1)S(1)}, bf16[192,1152]{1,0:T(8,128)(2,1)S(1)}, u32[]{:S(2)}, u32[]{:S(2)}) collective-permute-start(bf16[192,1152]{1,0:T(8,128)(2,1)S(1)} %collective-permute-done.3.refs_8_), channel_id=1, source_target_pairs={{0,128},{32,160},{64,192},{96,224},{128,0},{160,32},{192,64},{224,... | collective-permute-start | bytes 1327112 | tf_op jit(solution)/shard_map/ppermute | solution.py:45
  63.2 0.0 collective-permute-done.9.refs_14_
  63.2 2.4 %collective-permute-start.10 = (bf16[96,1152]{1,0:T(8,128)(2,1)S(1)}, bf16[96,1152]{1,0:T(8,128)(2,1)S(1)}, u32[]{:S(2)}, u32[]{:S(2)}) collective-permute-start(bf16[96,1152]{1,0:T(8,128)(2,1)S(1)} %collective-permute-done.9.refs_14_), channel_id=1, source_target_pairs={{0,128},{32,160},{64,192},{96,224},{128,0},{160,32},{192,64},{224,... | collective-permute-start | bytes 663560 | tf_op jit(solution)/shard_map/ppermute | solution.py:45
  65.6 0.0 collective-permute-done.7.refs_12_
  65.6 3.1 %collective-permute-start.8 = (bf16[96,1152]{1,0:T(8,128)(2,1)S(1)}, bf16[96,1152]{1,0:T(8,128)(2,1)}, u32[]{:S(2)}, u32[]{:S(2)}) collective-permute-start(bf16[96,1152]{1,0:T(8,128)(2,1)S(1)} %collective-permute-done.7.refs_12_), channel_id=1, source_target_pairs={{0,128},{32,160},{64,192},{96,224},{128,0},{160,32},{192,64},{224,... | collective-permute-start | bytes 663560 | tf_op jit(solution)/shard_map/ppermute | solution.py:45
  69.5 0.6 stack.71.starts
  70.1 0.0 collective-permute-done.10.refs_15_
  70.1 0.0 collective-permute-done.6.refs_11_
  70.1 0.0 collective-permute-done.8.refs_13_
  70.1 0.0 collective-permute-done.4.refs_9_
  70.2 0.0 all-gather.3.cloned.1.call-done
  70.2 0.6 copy-done.12
  70.8 0.2 copy-done.9
  71.0 0.1 copy-done.8
  71.2 12.6 %project.1 = (bf16[512,384]{1,0:T(8,128)(2,1)}, bf16[512,768]{1,0:T(8,128)(2,1)}, bf16[256,768]{1,0:T(8,128)(2,1)}, bf16[256,768]{1,0:T(8,128)(2,1)}) custom-call(s32[12]{0:T(128)} %stack.71.starts, s32[1,1]{1,0:T(1,128)S(6)} %copy.10.levels, bf16[8,512,384]{2,1,0:T(8,128)(2,1)} %bitcast.24, f32[32,2,3072]{2,1,0:T(2,128)} %refs_1_.3, f32[1,128]{1,0:T(1,128)} %bitcast.25, ...), custom_call_target="tpu_custom_call" | custom-call | flops 3623878656 | bytes 12582912 | tf_op jit(solution)/shard_map/project/pallas_call | solution.py:215
  83.7 1.9 %collective-permute-start.13 = (bf16[512,768]{1,0:T(8,128)(2,1)}, bf16[512,768]{1,0:T(8,128)(2,1)S(1)}, u32[]{:S(2)}, u32[]{:S(2)}) collective-permute-start(bf16[512,768]{1,0:T(8,128)(2,1)} %get-tuple-element.20.own), channel_id=1, source_target_pairs={{0,128},{32,160},{64,192},{96,224},{128,0},{160,32},{192,64},{224,... | collective-permute-start | bytes 2359304 | tf_op jit(solution)/shard_map/ppermute | solution.py:45
  85.7 1.3 collective-permute-start.11
  87.0 1.9 %collective-permute-start.12 = (bf16[256,768]{1,0:T(8,128)(2,1)}, bf16[256,768]{1,0:T(8,128)(2,1)S(1)}, u32[]{:S(2)}, u32[]{:S(2)}) collective-permute-start(bf16[256,768]{1,0:T(8,128)(2,1)} %get-tuple-element.19), channel_id=1, source_target_pairs={{0,272},{32,304},{64,336},{96,368},{128,400},{160,432},{192,464},{... | collective-permute-start | bytes 1179656 | tf_op jit(solution)/shard_map/ppermute | solution.py:45
  88.9 0.1 pad_add_fusion.spots.refs_0_
  89.0 0.0 copy-start
  89.0 1.0 copy-done
  90.0 1.1 copy-done.3
  91.2 3.0 %near.1 = (f32[512,384]{1,0:T(8,128)S(1)}, f32[512,384]{1,0:T(8,128)S(1)}) custom-call(s32[4]{0:T(128)S(1)} %pad_add_fusion.spots.refs_0_, s32[1,4]{1,0:T(1,128)S(1)} %copy-done.2, s32[4,4]{1,0:T(4,128)S(1)} %bitcast.21, bf16[512,384]{1,0:T(8,128)(2,1)S(1)} %copy-done, bf16[512,768]{1,0:T(8,128)(2,1)S(1)} %copy-done.3, ...), custom_call_target="tpu_custom_call" | custom-call | flops 805306368 | bytes 6291456 | tf_op jit(solution)/shard_map/near/pallas_call | solution.py:250
  94.2 1.4 %collective-permute-done.11 = bf16[256,768]{1,0:T(8,128)(2,1)S(1)} collective-permute-done((bf16[256,768]{1,0:T(8,128)(2,1)}, bf16[256,768]{1,0:T(8,128)(2,1)S(1)}, u32[]{:S(2)}, u32[]{:S(2)}) %collective-permute-start.11) | collective-permute-done | bytes 393248 | tf_op jit(solution)/shard_map/ppermute | solution.py:45
  95.6 16.1 %collective-permute-done.12 = bf16[256,768]{1,0:T(8,128)(2,1)S(1)} collective-permute-done((bf16[256,768]{1,0:T(8,128)(2,1)}, bf16[256,768]{1,0:T(8,128)(2,1)S(1)}, u32[]{:S(2)}, u32[]{:S(2)}) %collective-permute-start.12) | collective-permute-done | bytes 393248 | tf_op jit(solution)/shard_map/ppermute | solution.py:45
  111.7 0.7 collective-permute-start.14
  112.4 1.3 collective-permute-start.15
  113.7 0.0 collective-permute-done.14.refs_6_
  113.7 14.2 %collective-permute-done.15.refs_7_ = bf16[256,768]{1,0:T(8,128)(2,1)S(1)} collective-permute-done((bf16[256,768]{1,0:T(8,128)(2,1)S(1)}, bf16[256,768]{1,0:T(8,128)(2,1)S(1)}, u32[]{:S(2)}, u32[]{:S(2)}) %collective-permute-start.15) | collective-permute-done | bytes 393248 | tf_op jit(solution)/shard_map/ppermute | solution.py:45
  128.0 0.1 pad_maximum_fusion
  128.0 2.4 %collective-permute-start.16 = (bf16[512,768]{1,0:T(8,128)(2,1)S(1)}, bf16[512,768]{1,0:T(8,128)(2,1)S(1)}, u32[]{:S(2)}, u32[]{:S(2)}) collective-permute-start(bf16[512,768]{1,0:T(8,128)(2,1)S(1)} %pad_maximum_fusion), channel_id=1, source_target_pairs={{0,128},{32,160},{64,192},{96,224},{128,0},{160,32},{192,64},{224,... | collective-permute-start | bytes 2359304 | tf_op jit(solution)/shard_map/ppermute | solution.py:45
  130.4 0.7 far.1
  131.1 1.2 collective-permute-done.16.refs_6_
  132.3 1.7 %last.1 = bf16[512,384]{1,0:T(8,128)(2,1)} custom-call(s32[4]{0:T(128)S(1)} %pad_add_fusion.spots.refs_0_, s32[1,4]{1,0:T(1,128)S(1)} %copy-done.2, s32[4,4]{1,0:T(4,128)S(1)} %bitcast.23, bf16[512,384]{1,0:T(8,128)(2,1)S(1)} %copy-done, f32[512,384]{1,0:T(8,128)S(1)} %get-tuple-element.27.refs_4_, f32[512,384]{1,0:T(8,128)S(1)} %get-tuple-element.28.refs_5_, ...), custom_call_target="tpu_custom_call" | custom-call | flops 805306368 | bytes 6291456 | tf_op jit(solution)/shard_map/last/pallas_call | solution.py:273
  (25 shorter events, 0.1 us)
Async XLA Ops:
  6.5 63.6 %all-gather.3.cloned.1.call-start = ((), (), s32[]{:S(2)}) async-start(), calls=%async_computation | async-start | bytes 3538944 | tf_op jit(solution)/shard_map/all_gather | solution.py:193
  7.3 62.9 %collective-permute-start = (bf16[768,1152]{1,0:T(8,128)(2,1)}, bf16[768,1152]{1,0:T(8,128)(2,1)}, u32[]{:S(2)}, u32[]{:S(2)}) collective-permute-start(bf16[768,1152]{1,0:T(8,128)(2,1)} %refs_4_.1), channel_id=1, source_target_pairs={{0,128},{32,160},{64,192},{96,224},{128,0},{160,32},{192,64},{224,... | collective-permute-start | bytes 5308424 | tf_op jit(solution)/shard_map/ppermute | solution.py:45
  17.1 21.4 %collective-permute-start.1 = (bf16[192,1152]{1,0:T(8,128)(2,1)S(1)}, bf16[192,1152]{1,0:T(8,128)(2,1)S(1)}, u32[]{:S(2)}, u32[]{:S(2)}) collective-permute-start(bf16[192,1152]{1,0:T(8,128)(2,1)S(1)} %constant_dynamic-slice_fusion), channel_id=1, source_target_pairs={{0,280},{32,312},{64,344},{96,376},{128,408},{160,440},{192,472},{... | collective-permute-start | bytes 1327112 | tf_op jit(solution)/shard_map/ppermute | solution.py:45
  38.5 32.5 %copy-start.6 = (bf16[192,1152]{1,0:T(8,128)(2,1)}, bf16[192,1152]{1,0:T(8,128)(2,1)S(1)}, u32[]{:S(2)}) copy-start(bf16[192,1152]{1,0:T(8,128)(2,1)S(1)} %collective-permute-done.1.refs_6_) | copy-start | bytes 1327108
  38.5 13.4 %collective-permute-start.5 = (bf16[192,1152]{1,0:T(8,128)(2,1)S(1)}, bf16[192,1152]{1,0:T(8,128)(2,1)S(1)}, u32[]{:S(2)}, u32[]{:S(2)}) collective-permute-start(bf16[192,1152]{1,0:T(8,128)(2,1)S(1)} %collective-permute-done.1.refs_6_), channel_id=1, source_target_pairs={{0,96},{32,0},{64,32},{96,64},{128,224},{160,128},{192,160},{224,1... | collective-permute-start | bytes 1327112 | tf_op jit(solution)/shard_map/ppermute | solution.py:45
  41.3 14.5 %collective-permute-start.3 = (bf16[192,1152]{1,0:T(8,128)(2,1)S(1)}, bf16[192,1152]{1,0:T(8,128)(2,1)S(1)}, u32[]{:S(2)}, u32[]{:S(2)}) collective-permute-start(bf16[192,1152]{1,0:T(8,128)(2,1)S(1)} %collective-permute-done.1.refs_6_), channel_id=1, source_target_pairs={{0,32},{32,64},{64,96},{96,0},{128,160},{160,192},{192,224},{224,1... | collective-permute-start | bytes 1327112 | tf_op jit(solution)/shard_map/ppermute | solution.py:45
  43.8 17.4 %collective-permute-start.2 = (bf16[192,1152]{1,0:T(8,128)(2,1)S(1)}, bf16[192,1152]{1,0:T(8,128)(2,1)S(1)}, u32[]{:S(2)}, u32[]{:S(2)}) collective-permute-start(bf16[192,1152]{1,0:T(8,128)(2,1)S(1)} %collective-permute-done.1.refs_6_), channel_id=1, source_target_pairs={{0,128},{32,160},{64,192},{96,224},{128,0},{160,32},{192,64},{224,... | collective-permute-start | bytes 1327112 | tf_op jit(solution)/shard_map/ppermute | solution.py:45
  51.9 19.1 %copy-start.4 = (bf16[192,1152]{1,0:T(8,128)(2,1)}, bf16[192,1152]{1,0:T(8,128)(2,1)S(1)}, u32[]{:S(2)}) copy-start(bf16[192,1152]{1,0:T(8,128)(2,1)S(1)} %collective-permute-done.5.refs_10_) | copy-start | bytes 1327108
  51.9 11.2 %collective-permute-start.9 = (bf16[96,1152]{1,0:T(8,128)(2,1)S(1)}, bf16[96,1152]{1,0:T(8,128)(2,1)S(1)}, u32[]{:S(2)}, u32[]{:S(2)}) collective-permute-start(bf16[96,1152]{1,0:T(8,128)(2,1)S(1)} %slice.9), channel_id=1, source_target_pairs={{0,96},{32,0},{64,32},{96,64},{128,224},{160,128},{192,160},{224,1... | collective-permute-start | bytes 663560 | tf_op jit(solution)/shard_map/ppermute | solution.py:45
  55.8 15.2 %copy-start.5 = (bf16[192,1152]{1,0:T(8,128)(2,1)}, bf16[192,1152]{1,0:T(8,128)(2,1)S(1)}, u32[]{:S(2)}) copy-start(bf16[192,1152]{1,0:T(8,128)(2,1)S(1)} %collective-permute-done.3.refs_8_) | copy-start | bytes 1327108
  55.9 9.7 %collective-permute-start.7 = (bf16[96,1152]{1,0:T(8,128)(2,1)S(1)}, bf16[96,1152]{1,0:T(8,128)(2,1)S(1)}, u32[]{:S(2)}, u32[]{:S(2)}) collective-permute-start(bf16[96,1152]{1,0:T(8,128)(2,1)S(1)} %slice.8), channel_id=1, source_target_pairs={{0,32},{32,64},{64,96},{96,0},{128,160},{160,192},{192,224},{224,1... | collective-permute-start | bytes 663560 | tf_op jit(solution)/shard_map/ppermute | solution.py:45
  57.8 12.3 %collective-permute-start.6 = (bf16[192,1152]{1,0:T(8,128)(2,1)S(1)}, bf16[192,1152]{1,0:T(8,128)(2,1)S(1)}, u32[]{:S(2)}, u32[]{:S(2)}) collective-permute-start(bf16[192,1152]{1,0:T(8,128)(2,1)S(1)} %collective-permute-done.5.refs_10_), channel_id=1, source_target_pairs={{0,128},{32,160},{64,192},{96,224},{128,0},{160,32},{192,64},{224,... | collective-permute-start | bytes 1327112 | tf_op jit(solution)/shard_map/ppermute | solution.py:45
  61.2 9.8 %copy-start.7 = (bf16[192,1152]{1,0:T(8,128)(2,1)}, bf16[192,1152]{1,0:T(8,128)(2,1)S(1)}, u32[]{:S(2)}) copy-start(bf16[192,1152]{1,0:T(8,128)(2,1)S(1)} %collective-permute-done.2.refs_7_) | copy-start | bytes 1327108
  61.3 8.9 %collective-permute-start.4 = (bf16[192,1152]{1,0:T(8,128)(2,1)S(1)}, bf16[192,1152]{1,0:T(8,128)(2,1)S(1)}, u32[]{:S(2)}, u32[]{:S(2)}) collective-permute-start(bf16[192,1152]{1,0:T(8,128)(2,1)S(1)} %collective-permute-done.3.refs_8_), channel_id=1, source_target_pairs={{0,128},{32,160},{64,192},{96,224},{128,0},{160,32},{192,64},{224,... | collective-permute-start | bytes 1327112 | tf_op jit(solution)/shard_map/ppermute | solution.py:45
  63.2 7.8 %copy-start.10 = (bf16[96,1152]{1,0:T(8,128)(2,1)}, bf16[96,1152]{1,0:T(8,128)(2,1)S(1)}, u32[]{:S(2)}) copy-start(bf16[96,1152]{1,0:T(8,128)(2,1)S(1)} %collective-permute-done.9.refs_14_) | copy-start | bytes 663556
  63.2 6.9 %collective-permute-start.10 = (bf16[96,1152]{1,0:T(8,128)(2,1)S(1)}, bf16[96,1152]{1,0:T(8,128)(2,1)S(1)}, u32[]{:S(2)}, u32[]{:S(2)}) collective-permute-start(bf16[96,1152]{1,0:T(8,128)(2,1)S(1)} %collective-permute-done.9.refs_14_), channel_id=1, source_target_pairs={{0,128},{32,160},{64,192},{96,224},{128,0},{160,32},{192,64},{224,... | collective-permute-start | bytes 663560 | tf_op jit(solution)/shard_map/ppermute | solution.py:45
  65.6 4.6 %copy-start.11 = (bf16[96,1152]{1,0:T(8,128)(2,1)}, bf16[96,1152]{1,0:T(8,128)(2,1)S(1)}, u32[]{:S(2)}) copy-start(bf16[96,1152]{1,0:T(8,128)(2,1)S(1)} %collective-permute-done.7.refs_12_) | copy-start | bytes 663556
  65.6 4.5 %collective-permute-start.8 = (bf16[96,1152]{1,0:T(8,128)(2,1)S(1)}, bf16[96,1152]{1,0:T(8,128)(2,1)}, u32[]{:S(2)}, u32[]{:S(2)}) collective-permute-start(bf16[96,1152]{1,0:T(8,128)(2,1)S(1)} %collective-permute-done.7.refs_12_), channel_id=1, source_target_pairs={{0,128},{32,160},{64,192},{96,224},{128,0},{160,32},{192,64},{224,... | collective-permute-start | bytes 663560 | tf_op jit(solution)/shard_map/ppermute | solution.py:45
  70.1 0.7 copy-start.12
  70.1 1.1 copy-start.8
  70.1 0.9 copy-start.9
  71.2 17.8 %copy-start.1 = (s32[1,4,4]{2,1,0:T(4,128)S(1)}, s32[1,4,4]{2,1,0:T(4,128)}, u32[]{:S(2)}) copy-start(s32[1,4,4]{2,1,0:T(4,128)} %param.11) | copy-start | bytes 196
  71.2 17.8 %copy-start.2 = (s32[1,4]{1,0:T(1,128)S(1)}, s32[1,4]{1,0:T(1,128)}, u32[]{:S(2)}) copy-start(s32[1,4]{1,0:T(1,128)} %refs_1_.5) | copy-start | bytes 52
  83.7 5.3 %collective-permute-start.13 = (bf16[512,768]{1,0:T(8,128)(2,1)}, bf16[512,768]{1,0:T(8,128)(2,1)S(1)}, u32[]{:S(2)}, u32[]{:S(2)}) collective-permute-start(bf16[512,768]{1,0:T(8,128)(2,1)} %get-tuple-element.20.own), channel_id=1, source_target_pairs={{0,128},{32,160},{64,192},{96,224},{128,0},{160,32},{192,64},{224,... | collective-permute-start | bytes 2359304 | tf_op jit(solution)/shard_map/ppermute | solution.py:45
  85.7 9.9 %collective-permute-start.11 = (bf16[256,768]{1,0:T(8,128)(2,1)}, bf16[256,768]{1,0:T(8,128)(2,1)S(1)}, u32[]{:S(2)}, u32[]{:S(2)}) collective-permute-start(bf16[256,768]{1,0:T(8,128)(2,1)} %get-tuple-element.18), channel_id=1, source_target_pairs={{0,16},{32,48},{64,80},{96,112},{128,144},{160,176},{192,208},{224... | collective-permute-start | bytes 1179656 | tf_op jit(solution)/shard_map/ppermute | solution.py:45
  87.0 24.7 %collective-permute-start.12 = (bf16[256,768]{1,0:T(8,128)(2,1)}, bf16[256,768]{1,0:T(8,128)(2,1)S(1)}, u32[]{:S(2)}, u32[]{:S(2)}) collective-permute-start(bf16[256,768]{1,0:T(8,128)(2,1)} %get-tuple-element.19), channel_id=1, source_target_pairs={{0,272},{32,304},{64,336},{96,368},{128,400},{160,432},{192,464},{... | collective-permute-start | bytes 1179656 | tf_op jit(solution)/shard_map/ppermute | solution.py:45
  89.0 1.0 copy-start
  90.0 1.1 copy-start.3
  111.7 2.0 %collective-permute-start.14 = (bf16[256,768]{1,0:T(8,128)(2,1)S(1)}, bf16[256,768]{1,0:T(8,128)(2,1)S(1)}, u32[]{:S(2)}, u32[]{:S(2)}) collective-permute-start(bf16[256,768]{1,0:T(8,128)(2,1)S(1)} %collective-permute-done.11), channel_id=1, source_target_pairs={{16,256},{48,288},{80,320},{112,352},{144,384},{176,416},{208,448}... | collective-permute-start | bytes 1179656 | tf_op jit(solution)/shard_map/ppermute | solution.py:45
  112.4 15.6 %collective-permute-start.15 = (bf16[256,768]{1,0:T(8,128)(2,1)S(1)}, bf16[256,768]{1,0:T(8,128)(2,1)S(1)}, u32[]{:S(2)}, u32[]{:S(2)}) collective-permute-start(bf16[256,768]{1,0:T(8,128)(2,1)S(1)} %collective-permute-done.12), channel_id=1, source_target_pairs={{0,272},{32,304},{64,336},{96,368},{128,400},{160,432},{192,464},{... | collective-permute-start | bytes 1179656 | tf_op jit(solution)/shard_map/ppermute | solution.py:45
  128.0 4.3 %collective-permute-start.16 = (bf16[512,768]{1,0:T(8,128)(2,1)S(1)}, bf16[512,768]{1,0:T(8,128)(2,1)S(1)}, u32[]{:S(2)}, u32[]{:S(2)}) collective-permute-start(bf16[512,768]{1,0:T(8,128)(2,1)S(1)} %pad_maximum_fusion), channel_id=1, source_target_pairs={{0,128},{32,160},{64,192},{96,224},{128,0},{160,32},{192,64},{224,... | collective-permute-start | bytes 2359304 | tf_op jit(solution)/shard_map/ppermute | solution.py:45
Sparse Core Ops, SparseCore 0:
  9.4 53.9 all-gather.2

commit v5 on v4

--- a/solution.py
+++ b/solution.py
@@ -35,20 +35,28 @@
 X_UP = pairs(lambda y, core, x: (y, core, (x + 1) % XS))
 X_DOWN = pairs(lambda y, core, x: (y, core, (x - 1) % XS))
 SWAP = pairs(lambda y, core, x: (y, 1 - core, x))
-UP_FIRST = pairs(lambda y, core, x: (y + 2, core, x), lambda y: y < 4)
-UP_SECOND = pairs(lambda y, core, x: (y + 2, core, x), lambda y: 2 <= y < 6)
-DOWN_FIRST = pairs(lambda y, core, x: ((y - 2) % 8, core, x), lambda y: y < 4)
-DOWN_SECOND = pairs(lambda y, core, x: (y - 2 if y >= 6 else y + 6, core, x), lambda y: y >= 6 or y < 2)
+ACROSS = pairs(lambda y, core, x: (y + YS, core, x), lambda y: y < YS)
 
 
 def move(array, table):
     return lax.ppermute(array, ("block", "req"), table)
+
+
+def pack_kernel(starts, *refs):
+    pieces, out, sems = refs[:-2], refs[-2], refs[-1]
+    copies = []
+    for number, piece in enumerate(pieces):
+        band = pl.ds(pl.multiple_of(starts[number], 96), piece.shape[0])
+        copies.append(pltpu.make_async_copy(piece, out.at[band, :], sems.at[number]))
+        copies[-1].start()
+    for copy in copies:
+        copy.wait()
 
 
 def project_kernel(n_pieces, starts, levels, *refs):
     tokens_far, table, q_gain, k_gain = refs[:4]
     pieces = refs[4 : 4 + n_pieces]
-    q_out, kv_out, lo_out, hi_out, tokens, mod, weight, normed, token_sems, mod_sem, sems = refs[4 + n_pieces :]
+    q_out, kv_out, tokens, mod, weight, normed, projected, token_sems, mod_sem, sems = refs[4 + n_pieces :]
     parts, rows, depth = tokens.shape
     features = parts * depth
     chunks = token_sems.shape[0]
@@ -98,16 +106,23 @@
         scale = lax.rsqrt(jnp.mean(part * part, axis=-1, keepdims=True) + EPS)
         return (part * scale * gain).astype(jnp.bfloat16)
 
+    part = pieces[0].shape[0]
+    columns = weight.shape[1]
+    for at in range(0, columns, 512):
+        span = slice(at, min(at + 512, columns))
+        total = jnp.dot(normed[:, :part], weight[:part, span], preferred_element_type=jnp.float32)
+        for deep in range(part, features, part):
+            total += jnp.dot(
+                normed[:, deep : deep + part], weight[deep : deep + part, span], preferred_element_type=jnp.float32
+            )
+        projected[:, span] = total
     for head in range(heads):
-        span = slice(3 * HD * head, 3 * HD * (head + 1))
-        out = jnp.dot(normed[...], weight[:, span], preferred_element_type=jnp.float32)
-        q_out[:, HD * head : HD * (head + 1)] = head_norm(out[:, :HD], q_gain[...])
-        keys = head_norm(out[:, HD : 2 * HD], k_gain[...])
-        values = out[:, 2 * HD :].astype(jnp.bfloat16)
-        for item, at in ((keys, HD * head), (values, HD * (heads + head))):
-            kv_out[:, at : at + HD] = item
-            lo_out[:, at : at + HD] = item[: rows // 2]
-            hi_out[:, at : at + HD] = item[rows // 2 :]
+        at = 3 * HD * head
+        q_out[:, HD * head : HD * (head + 1)] = head_norm(projected[:, at : at + HD], q_gain[...])
+        keys = head_norm(projected[:, at + HD : at + 2 * HD], k_gain[...])
+        values = projected[:, at + 2 * HD : at + 3 * HD].astype(jnp.bfloat16)
+        kv_out[:, HD * head : HD * (head + 1)] = keys
+        kv_out[:, HD * (heads + head) : HD * (heads + head + 1)] = values
 
 
 def key_limit(spots, frames, mask, number):
@@ -156,10 +171,7 @@
     heads = q.shape[1] // HD
     half = q.shape[0] // 2
     num, den = rest[-2:]
-    if finish:
-        lo, hi = rest[0].at[:half], rest[0].at[half:]
-    else:
-        lo, hi = rest[:2]
+    lo, hi = rest[0].at[:half], rest[0].at[half:]
     num[...] = num_in[...]
     den[...] = den_in[...]
     limit = key_limit(spots, frames, mask, number)
@@ -182,7 +194,6 @@
     heads = columns // (3 * HD)
     width = heads * HD
     quarter = part_rows // XS
-    half = rows // 2
 
     block = lax.axis_index("block")
     side, core = block // CORES, block % CORES
@@ -192,41 +203,56 @@
 
     whole = lax.all_gather(own, "head", axis=0, tiled=False)
 
-    w_pair = move(w_qkv, SWAP)
-    first = move(lax.dynamic_slice_in_dim(w_qkv, quarter * x, quarter), MIRROR)
-    up, down = move(first, X_UP), move(first, X_DOWN)
-    far_a, far_b = move(up[: quarter // 2], X_UP), move(down[quarter // 2 :], X_DOWN)
-    held = [(first, 0, 0), (up, 3, 0), (down, 1, 0), (far_a, 2, 0), (far_b, 2, quarter // 2)]
-    pieces, starts = [w_qkv, w_pair], [block * part_rows, (side * CORES + 1 - core) * part_rows]
-    for piece, away, at in held:
-        row = (x + away) % XS * quarter + at
-        pieces += [piece, move(piece, SWAP)]
-        starts += [(other + core) * part_rows + row, (other + 1 - core) * part_rows + row]
-    starts = jnp.stack(starts).astype(jnp.int32)
+    piece = quarter // 2
+    mine = [lax.dynamic_slice_in_dim(w_qkv, quarter * x + at, piece) for at in (0, piece)]
+    first, second = (move(item, MIRROR) for item in mine)
+    first, local = lax.optimization_barrier((first, w_qkv))
+    w_pair = move(local, SWAP)
+    first_up, first_down = move(first, X_UP), move(first, X_DOWN)
+    second, first_up, first_down = lax.optimization_barrier((second, first_up, first_down))
+    second_up, second_down = move(second, X_UP), move(second, X_DOWN)
+    first_far, second_far = move(first_up, X_UP), move(second_down, X_DOWN)
+    held = [(first, 0, 0), (first_up, 3, 0), (first_down, 1, 0), (first_far, 2, 0),
+            (second, 0, 1), (second_up, 3, 1), (second_down, 1, 1), (second_far, 2, 1)]
+    places = jnp.stack([(x + away) % XS * quarter + sub * piece for _, away, sub in held]).astype(jnp.int32)
+    starts = [block, side * CORES + 1 - core, other + core, other + 1 - core]
+    starts = jnp.stack([item * part_rows for item in starts]).astype(jnp.int32)
 
     smem = pl.BlockSpec(memory_space=pltpu.SMEM)
     vmem = pl.BlockSpec(memory_space=pltpu.VMEM)
     hbm = pl.BlockSpec(memory_space=pltpu.HBM)
+    anywhere = pl.BlockSpec(memory_space=pl.ANY)
 
     def sized(limit):
         return pltpu.CompilerParams(vmem_limit_bytes=int(limit * MIB))
 
+    w_rest = pl.pallas_call(
+        pack_kernel,
+        out_shape=jax.ShapeDtypeStruct(w_qkv.shape, w_qkv.dtype),
+        in_specs=[smem] + [anywhere] * len(held),
+        out_specs=anywhere,
+        scratch_shapes=[pltpu.SemaphoreType.DMA((len(held),))],
+        compiler_params=sized(2),
+        cost_estimate=pl.CostEstimate(flops=0, bytes_accessed=4 * MIB, transcendentals=0),
+        name="pack",
+    )(places, *(item[0] for item in held))
+    pieces = [w_qkv, w_pair, w_rest, move(w_rest, SWAP)]
+
     chunks = 4
-    queries, kv, kv_lo, kv_hi = pl.pallas_call(
+    queries, kv = pl.pallas_call(
         functools.partial(project_kernel, len(pieces)),
         out_shape=(
             jax.ShapeDtypeStruct((rows, width), jnp.bfloat16),
             jax.ShapeDtypeStruct((rows, 2 * width), jnp.bfloat16),
-            jax.ShapeDtypeStruct((half, 2 * width), jnp.bfloat16),
-            jax.ShapeDtypeStruct((half, 2 * width), jnp.bfloat16),
         ),
         in_specs=[smem] * 2 + [hbm] * 2 + [vmem] * 2 + [hbm] * len(pieces),
-        out_specs=(vmem,) * 4,
+        out_specs=(vmem, vmem),
         scratch_shapes=[
             pltpu.VMEM((ring, rows, depth), jnp.bfloat16),
             pltpu.VMEM(mod_table.shape[1:], jnp.float32),
             pltpu.VMEM((ring * depth, columns), jnp.bfloat16),
             pltpu.VMEM((rows, ring * depth), jnp.bfloat16),
+            pltpu.VMEM((rows, columns), jnp.float32),
             pltpu.SemaphoreType.DMA((chunks,)),
             pltpu.SemaphoreType.DMA,
             pltpu.SemaphoreType.DMA((len(pieces),)),
@@ -238,8 +264,7 @@
         name="project",
     )(starts, levels, whole, mod_table, q_gain[None, :], k_gain[None, :], *pieces)
 
-    far_lo = move(kv_lo, UP_FIRST)
-    far_hi = move(kv_hi, DOWN_FIRST)
+    far_kv = move(kv, ACROSS)
     pair_kv = move(kv, SWAP)
 
     where = (spots, frames, segment_mask[0])
@@ -256,20 +281,17 @@
         cost_estimate=work,
         name="near",
     )(*where, queries, kv, pair_kv)
-    far_lo, far_hi, num, den = lax.optimization_barrier((far_lo, far_hi, num, den))
-    far_lo = move(far_lo, UP_SECOND)
-    far_hi = move(far_hi, DOWN_SECOND)
-    far_kv = lax.optimization_barrier(jnp.concatenate([far_lo, far_hi]))
+    far_kv, num, den = lax.optimization_barrier((far_kv, num, den))
     far_pair = move(far_kv, SWAP)
     num, den = pl.pallas_call(
         lambda *refs: far_kernel(2, False, *refs),
         out_shape=sums,
-        in_specs=[smem] * 3 + [vmem] * 5,
+        in_specs=[smem] * 3 + [vmem] * 4,
         out_specs=(vmem, vmem),
         compiler_params=sized(24),
         cost_estimate=work,
         name="far",
-    )(*where, queries, num, den, far_lo, far_hi)
+    )(*where, queries, num, den, far_kv)
     result = pl.pallas_call(
         lambda *refs: far_kernel(3, True, *refs),
         out_shape=jax.ShapeDtypeStruct((rows, width), jnp.bfloat16),

time: 143 us -> 134 us (0.937)
  the two profiles are of different devices: /device:TPU:1 before, /device:TPU:111 now
where the time goes in v5:
time: 134 us
  starting transfers between devices  47 us (35%)
  waiting for transfers between devices  44.2 us (33%)
  Pallas kernels  22.8 us (17%)
  between operations  14.4 us (11%)
  local copies, waits for them, and re-layouts  4.93 us (4%)
    ppermute x13, starting transfers between devices, move(): return lax.ppermute(array, ('block', 'req'), table)  47 us
    ppermute x13, waiting for transfers between devices, move(): return lax.ppermute(array, ('block', 'req'), table)  43.5 us
    pallas_call x1, Pallas kernels, body(): pl.pallas_call(functools.partial(project_kernel, len(pieces)), out_shape=...  11.2 us
    unnamed x14, local copies, waits for them, and re-layouts  3.76 us
    pallas_call x1, Pallas kernels, body(): pl.pallas_call(lambda *refs: far_kernel(3, True, *refs), out_shape=jax.Sh...  3.34 us
    pallas_call x1, Pallas kernels, body(): pl.pallas_call(near_kernel, out_shape=sums, in_specs=[smem] * 3 + [vmem]...  3.01 us
    pallas_call x1, Pallas kernels, body(): pl.pallas_call(pack_kernel, out_shape=jax.ShapeDtypeStruct(w_qkv.shape, w...  2.93 us
  transfers between devices with their start and end apart: 14, of which 6 were waited for; matrix products, arithmetic and copies ran while one was open for 1% of the time, Pallas kernels for 6%

profile of v5, /device:TPU:111, one launch (start us, length us, event | category | flops | bytes accessed | tf_op | source)
XLA Modules:
  0.0 134.0 jit_solution(4026310948877647021)
XLA Ops:
  6.5 0.0 all-gather.3.cloned.1.call-start
  6.5 0.7 all-gather.3.cloned.1.call-update
  7.3 1.1 constant_dynamic-slice_fusion
  8.4 2.7 %collective-permute-start = (bf16[96,1152]{1,0:T(8,128)(2,1)S(1)}, bf16[96,1152]{1,0:T(8,128)(2,1)S(1)}, u32[]{:S(2)}, u32[]{:S(2)}) collective-permute-start(bf16[96,1152]{1,0:T(8,128)(2,1)S(1)} %get-tuple-element.34), channel_id=1, source_target_pairs={{0,280},{32,312},{64,344},{96,376},{128,408},{160,440},{192,472},{... | collective-permute-start | bytes 663560 | tf_op jit(solution)/shard_map/ppermute | solution.py:42
  11.1 5.5 %collective-permute-start.2 = (bf16[96,1152]{1,0:T(8,128)(2,1)S(1)}, bf16[96,1152]{1,0:T(8,128)(2,1)S(1)}, u32[]{:S(2)}, u32[]{:S(2)}) collective-permute-start(bf16[96,1152]{1,0:T(8,128)(2,1)S(1)} %get-tuple-element.33), channel_id=1, source_target_pairs={{0,280},{32,312},{64,344},{96,376},{128,408},{160,440},{192,472},{... | collective-permute-start | bytes 663560 | tf_op jit(solution)/shard_map/ppermute | solution.py:42
  16.7 3.0 %collective-permute-done.refs_0_ = bf16[96,1152]{1,0:T(8,128)(2,1)S(1)} collective-permute-done((bf16[96,1152]{1,0:T(8,128)(2,1)S(1)}, bf16[96,1152]{1,0:T(8,128)(2,1)S(1)}, u32[]{:S(2)}, u32[]{:S(2)}) %collective-permute-start) | collective-permute-done | bytes 221216 | tf_op jit(solution)/shard_map/ppermute | solution.py:42
  19.7 2.4 %collective-permute-start.4 = (bf16[96,1152]{1,0:T(8,128)(2,1)S(1)}, bf16[96,1152]{1,0:T(8,128)(2,1)S(1)}, u32[]{:S(2)}, u32[]{:S(2)}) collective-permute-start(bf16[96,1152]{1,0:T(8,128)(2,1)S(1)} %collective-permute-done.refs_0_), channel_id=1, source_target_pairs={{0,96},{32,0},{64,32},{96,64},{128,224},{160,128},{192,160},{224,1... | collective-permute-start | bytes 663560 | tf_op jit(solution)/shard_map/ppermute | solution.py:42
  22.1 4.0 %collective-permute-start.3 = (bf16[96,1152]{1,0:T(8,128)(2,1)S(1)}, bf16[96,1152]{1,0:T(8,128)(2,1)S(1)}, u32[]{:S(2)}, u32[]{:S(2)}) collective-permute-start(bf16[96,1152]{1,0:T(8,128)(2,1)S(1)} %collective-permute-done.refs_0_), channel_id=1, source_target_pairs={{0,32},{32,64},{64,96},{96,0},{128,160},{160,192},{192,224},{224,1... | collective-permute-start | bytes 663560 | tf_op jit(solution)/shard_map/ppermute | solution.py:42
  26.2 0.0 collective-permute-done.2.refs_4_
  26.2 1.4 %collective-permute-done.4.refs_2_ = bf16[96,1152]{1,0:T(8,128)(2,1)S(1)} collective-permute-done((bf16[96,1152]{1,0:T(8,128)(2,1)S(1)}, bf16[96,1152]{1,0:T(8,128)(2,1)S(1)}, u32[]{:S(2)}, u32[]{:S(2)}) %collective-permute-start.4) | collective-permute-done | bytes 221216 | tf_op jit(solution)/shard_map/ppermute | solution.py:42
  27.5 1.7 %collective-permute-done.3.refs_1_ = bf16[96,1152]{1,0:T(8,128)(2,1)S(1)} collective-permute-done((bf16[96,1152]{1,0:T(8,128)(2,1)S(1)}, bf16[96,1152]{1,0:T(8,128)(2,1)S(1)}, u32[]{:S(2)}, u32[]{:S(2)}) %collective-permute-start.3) | collective-permute-done | bytes 221216 | tf_op jit(solution)/shard_map/ppermute | solution.py:42
  29.2 2.2 %collective-permute-start.7 = (bf16[96,1152]{1,0:T(8,128)(2,1)S(1)}, bf16[96,1152]{1,0:T(8,128)(2,1)S(1)}, u32[]{:S(2)}, u32[]{:S(2)}) collective-permute-start(bf16[96,1152]{1,0:T(8,128)(2,1)S(1)} %collective-permute-done.2.refs_4_), channel_id=1, source_target_pairs={{0,96},{32,0},{64,32},{96,64},{128,224},{160,128},{192,160},{224,1... | collective-permute-start | bytes 663560 | tf_op jit(solution)/shard_map/ppermute | solution.py:42
  31.3 4.6 %collective-permute-start.6 = (bf16[96,1152]{1,0:T(8,128)(2,1)S(1)}, bf16[96,1152]{1,0:T(8,128)(2,1)S(1)}, u32[]{:S(2)}, u32[]{:S(2)}) collective-permute-start(bf16[96,1152]{1,0:T(8,128)(2,1)S(1)} %collective-permute-done.2.refs_4_), channel_id=1, source_target_pairs={{0,32},{32,64},{64,96},{96,0},{128,160},{160,192},{192,224},{224,1... | collective-permute-start | bytes 663560 | tf_op jit(solution)/shard_map/ppermute | solution.py:42
  36.0 3.4 %collective-permute-start.5 = (bf16[96,1152]{1,0:T(8,128)(2,1)S(1)}, bf16[96,1152]{1,0:T(8,128)(2,1)S(1)}, u32[]{:S(2)}, u32[]{:S(2)}) collective-permute-start(bf16[96,1152]{1,0:T(8,128)(2,1)S(1)} %collective-permute-done.3.refs_1_), channel_id=1, source_target_pairs={{0,32},{32,64},{64,96},{96,0},{128,160},{160,192},{192,224},{224,1... | collective-permute-start | bytes 663560 | tf_op jit(solution)/shard_map/ppermute | solution.py:42
  39.3 0.0 collective-permute-done.7.refs_6_
  39.3 1.9 %collective-permute-start.8 = (bf16[96,1152]{1,0:T(8,128)(2,1)S(1)}, bf16[96,1152]{1,0:T(8,128)(2,1)S(1)}, u32[]{:S(2)}, u32[]{:S(2)}) collective-permute-start(bf16[96,1152]{1,0:T(8,128)(2,1)S(1)} %collective-permute-done.7.refs_6_), channel_id=1, source_target_pairs={{0,96},{32,0},{64,32},{96,64},{128,224},{160,128},{192,160},{224,1... | collective-permute-start | bytes 663560 | tf_op jit(solution)/shard_map/ppermute | solution.py:42
  41.3 0.1 stack.75.starts
  41.4 6.8 %collective-permute-start.1 = (bf16[768,1152]{1,0:T(8,128)(2,1)}, bf16[768,1152]{1,0:T(8,128)(2,1)}, u32[]{:S(2)}, u32[]{:S(2)}) collective-permute-start(bf16[768,1152]{1,0:T(8,128)(2,1)} %refs_4_.1), channel_id=1, source_target_pairs={{0,128},{32,160},{64,192},{96,224},{128,0},{160,32},{192,64},{224,... | collective-permute-start | bytes 5308424 | tf_op jit(solution)/shard_map/ppermute | solution.py:42
  48.3 0.0 collective-permute-done.5.refs_3_
  48.3 0.0 collective-permute-done.6.refs_5_
  48.3 0.0 collective-permute-done.8.refs_7_
  48.3 0.0 copy-start.2
  48.3 0.7 copy-done.2
  49.0 0.0 copy-start.3
  49.0 0.9 copy-done.3
  49.9 2.9 %pack.1.refs_6_ = bf16[768,1152]{1,0:T(8,128)(2,1)S(1)} custom-call(s32[8]{0:T(128)S(1)} %stack.75.starts, bf16[96,1152]{1,0:T(8,128)(2,1)S(1)} %collective-permute-done.refs_0_, bf16[96,1152]{1,0:T(8,128)(2,1)S(1)} %collective-permute-done.3.refs_1_, bf16[96,1152]{1,0:T(8,128)(2,1)S(1)} %collective-permute-done.4.refs_2_, ...), custom_call_target="tpu_custom_call" | custom-call | bytes 4194304 | tf_op jit(solution)/shard_map/pack/pallas_call | solution.py:229
  52.9 0.0 copy-start
  52.9 6.9 %collective-permute-start.9 = (bf16[768,1152]{1,0:T(8,128)(2,1)S(1)}, bf16[768,1152]{1,0:T(8,128)(2,1)}, u32[]{:S(2)}, u32[]{:S(2)}) collective-permute-start(bf16[768,1152]{1,0:T(8,128)(2,1)S(1)} %pack.1.refs_6_), channel_id=1, source_target_pairs={{0,128},{32,160},{64,192},{96,224},{128,0},{160,32},{192,64},{224,... | collective-permute-start | bytes 5308424 | tf_op jit(solution)/shard_map/ppermute | solution.py:42
  60.5 0.6 pad_add_fusion.1.starts
  61.1 0.0 collective-permute-done.1.refs_5_
  61.1 2.2 %collective-permute-done.9.refs_7_ = bf16[768,1152]{1,0:T(8,128)(2,1)} collective-permute-done((bf16[768,1152]{1,0:T(8,128)(2,1)S(1)}, bf16[768,1152]{1,0:T(8,128)(2,1)}, u32[]{:S(2)}, u32[]{:S(2)}) %collective-permute-start.9) | collective-permute-done | bytes 1769504 | tf_op jit(solution)/shard_map/ppermute | solution.py:42
  63.2 0.0 all-gather.3.cloned.1.call-done
  63.2 0.0 copy-done
  63.2 11.2 %project.1 = (bf16[512,384]{1,0:T(8,128)(2,1)}, bf16[512,768]{1,0:T(8,128)(2,1)}) custom-call(s32[4]{0:T(128)} %pad_add_fusion.1.starts, s32[1,1]{1,0:T(1,128)S(6)} %copy.10.levels, bf16[8,512,384]{2,1,0:T(8,128)(2,1)} %bitcast.24, f32[32,2,3072]{2,1,0:T(2,128)} %refs_1_.3, f32[1,128]{1,0:T(1,128)} %bitcast.25, f32[1,128]{1,0:T(1,128)} %bitcast.26, ...), custom_call_target="tpu_custom_call" | custom-call | flops 3623878656 | bytes 12582912 | tf_op jit(solution)/shard_map/project/pallas_call | solution.py:242
  74.5 2.3 %collective-permute-start.11 = (bf16[512,768]{1,0:T(8,128)(2,1)}, bf16[512,768]{1,0:T(8,128)(2,1)S(1)}, u32[]{:S(2)}, u32[]{:S(2)}) collective-permute-start(bf16[512,768]{1,0:T(8,128)(2,1)} %get-tuple-element.25.own), channel_id=1, source_target_pairs={{0,128},{32,160},{64,192},{96,224},{128,0},{160,32},{192,64},{224,... | collective-permute-start | bytes 2359304 | tf_op jit(solution)/shard_map/ppermute | solution.py:42
  76.8 1.3 collective-permute-start.10
  78.1 0.1 pad_add_fusion.spots.refs_0_
  78.2 0.7 collective-permute-done.11.pair
  78.9 0.0 copy-done.4
  78.9 0.0 copy-done.5
  78.9 1.0 copy-done.1
  79.9 1.1 copy-done.6
  81.0 3.0 %near.1 = (f32[512,384]{1,0:T(8,128)S(1)}, f32[512,384]{1,0:T(8,128)S(1)}) custom-call(s32[4]{0:T(128)S(1)} %pad_add_fusion.spots.refs_0_, s32[1,4]{1,0:T(1,128)S(1)} %copy-done.5, s32[4,4]{1,0:T(4,128)S(1)} %bitcast.21, bf16[512,384]{1,0:T(8,128)(2,1)S(1)} %copy-done.1, bf16[512,768]{1,0:T(8,128)(2,1)S(1)} %copy-done.6, ...), custom_call_target="tpu_custom_call" | custom-call | flops 805306368 | bytes 6291456 | tf_op jit(solution)/shard_map/near/pallas_call | solution.py:275
  84.0 34.6 %collective-permute-done.10.refs_6_ = bf16[512,768]{1,0:T(8,128)(2,1)S(1)} collective-permute-done((bf16[512,768]{1,0:T(8,128)(2,1)}, bf16[512,768]{1,0:T(8,128)(2,1)S(1)}, u32[]{:S(2)}, u32[]{:S(2)}) %collective-permute-start.10) | collective-permute-done | bytes 786464 | tf_op jit(solution)/shard_map/ppermute | solution.py:42
  118.7 2.8 %collective-permute-start.12 = (bf16[512,768]{1,0:T(8,128)(2,1)S(1)}, bf16[512,768]{1,0:T(8,128)(2,1)S(1)}, u32[]{:S(2)}, u32[]{:S(2)}) collective-permute-start(bf16[512,768]{1,0:T(8,128)(2,1)S(1)} %collective-permute-done.10.refs_6_), channel_id=1, source_target_pairs={{0,128},{32,160},{64,192},{96,224},{128,0},{160,32},{192,64},{224,... | collective-permute-start | bytes 2359304 | tf_op jit(solution)/shard_map/ppermute | solution.py:42
  121.5 2.3 %far.1 = (f32[512,384]{1,0:T(8,128)S(1)}, f32[512,384]{1,0:T(8,128)S(1)}) custom-call(s32[4]{0:T(128)S(1)} %pad_add_fusion.spots.refs_0_, s32[1,4]{1,0:T(1,128)S(1)} %copy-done.5, s32[4,4]{1,0:T(4,128)S(1)} %bitcast.22, bf16[512,384]{1,0:T(8,128)(2,1)S(1)} %copy-done.1, f32[512,384]{1,0:T(8,128)S(1)} %get-tuple-element.28.refs_4_, ...), custom_call_target="tpu_custom_call" | custom-call | flops 805306368 | bytes 6291456 | tf_op jit(solution)/shard_map/far/pallas_call | solution.py:286
  123.8 0.0 collective-permute-done.12.refs_6_
  123.8 3.3 %last.1 = bf16[512,384]{1,0:T(8,128)(2,1)} custom-call(s32[4]{0:T(128)S(1)} %pad_add_fusion.spots.refs_0_, s32[1,4]{1,0:T(1,128)S(1)} %copy-done.5, s32[4,4]{1,0:T(4,128)S(1)} %bitcast.23, bf16[512,384]{1,0:T(8,128)(2,1)S(1)} %copy-done.1, f32[512,384]{1,0:T(8,128)S(1)} %get-tuple-element.31.refs_4_, f32[512,384]{1,0:T(8,128)S(1)} %get-tuple-element.32.refs_5_, ...), custom_call_target="tpu_custom_call" | custom-call | flops 805306368 | bytes 6291456 | tf_op jit(solution)/shard_map/last/pallas_call | solution.py:295
  (4 shorter events, 0.0 us)
Async XLA Ops:
  6.5 56.7 %all-gather.3.cloned.1.call-start = ((), (), s32[]{:S(2)}) async-start(), calls=%async_computation | async-start | bytes 3538944 | tf_op jit(solution)/shard_map/all_gather | solution.py:204
  8.4 11.3 %collective-permute-start = (bf16[96,1152]{1,0:T(8,128)(2,1)S(1)}, bf16[96,1152]{1,0:T(8,128)(2,1)S(1)}, u32[]{:S(2)}, u32[]{:S(2)}) collective-permute-start(bf16[96,1152]{1,0:T(8,128)(2,1)S(1)} %get-tuple-element.34), channel_id=1, source_target_pairs={{0,280},{32,312},{64,344},{96,376},{128,408},{160,440},{192,472},{... | collective-permute-start | bytes 663560 | tf_op jit(solution)/shard_map/ppermute | solution.py:42
  11.1 15.0 %collective-permute-start.2 = (bf16[96,1152]{1,0:T(8,128)(2,1)S(1)}, bf16[96,1152]{1,0:T(8,128)(2,1)S(1)}, u32[]{:S(2)}, u32[]{:S(2)}) collective-permute-start(bf16[96,1152]{1,0:T(8,128)(2,1)S(1)} %get-tuple-element.33), channel_id=1, source_target_pairs={{0,280},{32,312},{64,344},{96,376},{128,408},{160,440},{192,472},{... | collective-permute-start | bytes 663560 | tf_op jit(solution)/shard_map/ppermute | solution.py:42
  19.7 7.9 %collective-permute-start.4 = (bf16[96,1152]{1,0:T(8,128)(2,1)S(1)}, bf16[96,1152]{1,0:T(8,128)(2,1)S(1)}, u32[]{:S(2)}, u32[]{:S(2)}) collective-permute-start(bf16[96,1152]{1,0:T(8,128)(2,1)S(1)} %collective-permute-done.refs_0_), channel_id=1, source_target_pairs={{0,96},{32,0},{64,32},{96,64},{128,224},{160,128},{192,160},{224,1... | collective-permute-start | bytes 663560 | tf_op jit(solution)/shard_map/ppermute | solution.py:42
  22.1 7.1 %collective-permute-start.3 = (bf16[96,1152]{1,0:T(8,128)(2,1)S(1)}, bf16[96,1152]{1,0:T(8,128)(2,1)S(1)}, u32[]{:S(2)}, u32[]{:S(2)}) collective-permute-start(bf16[96,1152]{1,0:T(8,128)(2,1)S(1)} %collective-permute-done.refs_0_), channel_id=1, source_target_pairs={{0,32},{32,64},{64,96},{96,0},{128,160},{160,192},{192,224},{224,1... | collective-permute-start | bytes 663560 | tf_op jit(solution)/shard_map/ppermute | solution.py:42
  29.2 10.1 %collective-permute-start.7 = (bf16[96,1152]{1,0:T(8,128)(2,1)S(1)}, bf16[96,1152]{1,0:T(8,128)(2,1)S(1)}, u32[]{:S(2)}, u32[]{:S(2)}) collective-permute-start(bf16[96,1152]{1,0:T(8,128)(2,1)S(1)} %collective-permute-done.2.refs_4_), channel_id=1, source_target_pairs={{0,96},{32,0},{64,32},{96,64},{128,224},{160,128},{192,160},{224,1... | collective-permute-start | bytes 663560 | tf_op jit(solution)/shard_map/ppermute | solution.py:42
  31.3 16.9 %collective-permute-start.6 = (bf16[96,1152]{1,0:T(8,128)(2,1)S(1)}, bf16[96,1152]{1,0:T(8,128)(2,1)S(1)}, u32[]{:S(2)}, u32[]{:S(2)}) collective-permute-start(bf16[96,1152]{1,0:T(8,128)(2,1)S(1)} %collective-permute-done.2.refs_4_), channel_id=1, source_target_pairs={{0,32},{32,64},{64,96},{96,0},{128,160},{160,192},{192,224},{224,1... | collective-permute-start | bytes 663560 | tf_op jit(solution)/shard_map/ppermute | solution.py:42
  36.0 12.3 %collective-permute-start.5 = (bf16[96,1152]{1,0:T(8,128)(2,1)S(1)}, bf16[96,1152]{1,0:T(8,128)(2,1)S(1)}, u32[]{:S(2)}, u32[]{:S(2)}) collective-permute-start(bf16[96,1152]{1,0:T(8,128)(2,1)S(1)} %collective-permute-done.3.refs_1_), channel_id=1, source_target_pairs={{0,32},{32,64},{64,96},{96,0},{128,160},{160,192},{192,224},{224,1... | collective-permute-start | bytes 663560 | tf_op jit(solution)/shard_map/ppermute | solution.py:42
  39.3 9.0 %collective-permute-start.8 = (bf16[96,1152]{1,0:T(8,128)(2,1)S(1)}, bf16[96,1152]{1,0:T(8,128)(2,1)S(1)}, u32[]{:S(2)}, u32[]{:S(2)}) collective-permute-start(bf16[96,1152]{1,0:T(8,128)(2,1)S(1)} %collective-permute-done.7.refs_6_), channel_id=1, source_target_pairs={{0,96},{32,0},{64,32},{96,64},{128,224},{160,128},{192,160},{224,1... | collective-permute-start | bytes 663560 | tf_op jit(solution)/shard_map/ppermute | solution.py:42
  41.4 19.7 %collective-permute-start.1 = (bf16[768,1152]{1,0:T(8,128)(2,1)}, bf16[768,1152]{1,0:T(8,128)(2,1)}, u32[]{:S(2)}, u32[]{:S(2)}) collective-permute-start(bf16[768,1152]{1,0:T(8,128)(2,1)} %refs_4_.1), channel_id=1, source_target_pairs={{0,128},{32,160},{64,192},{96,224},{128,0},{160,32},{192,64},{224,... | collective-permute-start | bytes 5308424 | tf_op jit(solution)/shard_map/ppermute | solution.py:42
  48.3 0.7 copy-start.2
  49.0 0.9 copy-start.3
  52.9 10.4 %copy-start = (bf16[768,1152]{1,0:T(8,128)(2,1)}, bf16[768,1152]{1,0:T(8,128)(2,1)S(1)}, u32[]{:S(2)}) copy-start(bf16[768,1152]{1,0:T(8,128)(2,1)S(1)} %pack.1.refs_6_) | copy-start | bytes 5308420
  52.9 10.4 %collective-permute-start.9 = (bf16[768,1152]{1,0:T(8,128)(2,1)S(1)}, bf16[768,1152]{1,0:T(8,128)(2,1)}, u32[]{:S(2)}, u32[]{:S(2)}) collective-permute-start(bf16[768,1152]{1,0:T(8,128)(2,1)S(1)} %pack.1.refs_6_), channel_id=1, source_target_pairs={{0,128},{32,160},{64,192},{96,224},{128,0},{160,32},{192,64},{224,... | collective-permute-start | bytes 5308424 | tf_op jit(solution)/shard_map/ppermute | solution.py:42
  63.2 15.7 %copy-start.4 = (s32[1,4,4]{2,1,0:T(4,128)S(1)}, s32[1,4,4]{2,1,0:T(4,128)}, u32[]{:S(2)}) copy-start(s32[1,4,4]{2,1,0:T(4,128)} %param.11) | copy-start | bytes 196
  63.2 15.7 %copy-start.5 = (s32[1,4]{1,0:T(1,128)S(1)}, s32[1,4]{1,0:T(1,128)}, u32[]{:S(2)}) copy-start(s32[1,4]{1,0:T(1,128)} %refs_1_.5) | copy-start | bytes 52
  74.5 4.4 %collective-permute-start.11 = (bf16[512,768]{1,0:T(8,128)(2,1)}, bf16[512,768]{1,0:T(8,128)(2,1)S(1)}, u32[]{:S(2)}, u32[]{:S(2)}) collective-permute-start(bf16[512,768]{1,0:T(8,128)(2,1)} %get-tuple-element.25.own), channel_id=1, source_target_pairs={{0,128},{32,160},{64,192},{96,224},{128,0},{160,32},{192,64},{224,... | collective-permute-start | bytes 2359304 | tf_op jit(solution)/shard_map/ppermute | solution.py:42
  76.8 41.9 %collective-permute-start.10 = (bf16[512,768]{1,0:T(8,128)(2,1)}, bf16[512,768]{1,0:T(8,128)(2,1)S(1)}, u32[]{:S(2)}, u32[]{:S(2)}) collective-permute-start(bf16[512,768]{1,0:T(8,128)(2,1)} %get-tuple-element.25.own), channel_id=1, source_target_pairs={{0,256},{32,288},{64,320},{96,352},{128,384},{160,416},{192,448},{... | collective-permute-start | bytes 2359304 | tf_op jit(solution)/shard_map/ppermute | solution.py:42
  78.9 1.0 copy-start.1
  79.9 1.1 copy-start.6
  118.7 5.2 %collective-permute-start.12 = (bf16[512,768]{1,0:T(8,128)(2,1)S(1)}, bf16[512,768]{1,0:T(8,128)(2,1)S(1)}, u32[]{:S(2)}, u32[]{:S(2)}) collective-permute-start(bf16[512,768]{1,0:T(8,128)(2,1)S(1)} %collective-permute-done.10.refs_6_), channel_id=1, source_target_pairs={{0,128},{32,160},{64,192},{96,224},{128,0},{160,32},{192,64},{224,... | collective-permute-start | bytes 2359304 | tf_op jit(solution)/shard_map/ppermute | solution.py:42
Sparse Core Ops, SparseCore 0:
  9.4 50.4 all-gather.2

commit v6 on v5

--- a/solution.py
+++ b/solution.py
@@ -42,61 +42,51 @@
     return lax.ppermute(array, ("block", "req"), table)
 
 
-def pack_kernel(starts, *refs):
+def pack_kernel(spots, *refs):
     pieces, out, sems = refs[:-2], refs[-2], refs[-1]
     copies = []
     for number, piece in enumerate(pieces):
-        band = pl.ds(pl.multiple_of(starts[number], 96), piece.shape[0])
+        band = pl.ds(pl.multiple_of(spots[4 + number], 96), piece.shape[0])
         copies.append(pltpu.make_async_copy(piece, out.at[band, :], sems.at[number]))
         copies[-1].start()
     for copy in copies:
         copy.wait()
 
 
-def project_kernel(n_pieces, starts, levels, *refs):
-    tokens_far, table, q_gain, k_gain = refs[:4]
+def project_kernel(n_pieces, spots, levels, *refs):
+    tokens, table, q_gain, k_gain = refs[:4]
     pieces = refs[4 : 4 + n_pieces]
-    q_out, kv_out, tokens, mod, weight, normed, projected, token_sems, mod_sem, sems = refs[4 + n_pieces :]
+    q_out, kv_out, mod, weight, normed, projected, mod_sem, sems = refs[4 + n_pieces :]
     parts, rows, depth = tokens.shape
     features = parts * depth
-    chunks = token_sems.shape[0]
-    chunk = rows // chunks
     step_rows = 64
 
     mod_load = pltpu.make_async_copy(table.at[levels[0, 0]], mod, mod_sem)
     mod_load.start()
-    loads = []
-    for number in range(chunks):
-        band = pl.ds(number * chunk, chunk)
-        loads.append(pltpu.make_async_copy(tokens_far.at[:, band, :], tokens.at[:, band, :], token_sems.at[number]))
-        loads[-1].start()
     weights = []
     for number, piece in enumerate(pieces):
-        band = pl.ds(pl.multiple_of(starts[number], 96), piece.shape[0])
+        band = pl.ds(pl.multiple_of(spots[number] * piece.shape[0], 96), piece.shape[0])
         weights.append(pltpu.make_async_copy(piece, weight.at[band, :], sems.at[number]))
         weights[-1].start()
     mod_load.wait()
 
-    for number in range(chunks):
-        loads[number].wait()
-
-        def norm_rows(step, carry, number=number):
-            band = pl.ds(pl.multiple_of(number * chunk + step * step_rows, step_rows), step_rows)
-            total = jnp.zeros((step_rows, 128), jnp.float32)
-            for part in range(parts):
-                wide = tokens[part, band, :].astype(jnp.float32)
-                square = wide * wide
-                for lane in range(0, depth, 128):
-                    total = total + square[:, lane : lane + 128]
-            scale = lax.rsqrt(jnp.sum(total, axis=-1, keepdims=True) * (1.0 / features) + EPS)
-            for part in range(parts):
-                span = slice(part * depth, (part + 1) * depth)
-                wide = tokens[part, band, :].astype(jnp.float32)
-                row = wide * scale * (1.0 + mod[0:1, span]) + mod[1:2, span]
-                normed[band, span] = row.astype(jnp.bfloat16)
-            return carry
-
-        lax.fori_loop(0, chunk // step_rows, norm_rows, 0)
+    def norm_rows(step, carry):
+        band = pl.ds(pl.multiple_of(step * step_rows, step_rows), step_rows)
+        total = jnp.zeros((step_rows, 128), jnp.float32)
+        for part in range(parts):
+            wide = tokens[part, band, :].astype(jnp.float32)
+            square = wide * wide
+            for lane in range(0, depth, 128):
+                total = total + square[:, lane : lane + 128]
+        scale = lax.rsqrt(jnp.sum(total, axis=-1, keepdims=True) * (1.0 / features) + EPS)
+        for part in range(parts):
+            span = slice(part * depth, (part + 1) * depth)
+            wide = tokens[part, band, :].astype(jnp.float32)
+            row = wide * scale * (1.0 + mod[0:1, span]) + mod[1:2, span]
+            normed[band, span] = row.astype(jnp.bfloat16)
+        return carry
+
+    lax.fori_loop(0, rows // step_rows, norm_rows, 0)
     for copy in weights:
         copy.wait()
 
@@ -199,28 +189,27 @@
     side, core = block // CORES, block % CORES
     x = lax.axis_index("req") // YS
     other = (1 - side) * CORES
-    spots = jnp.stack([block, side * CORES + 1 - core, other + core, other + 1 - core]).astype(jnp.int32)
 
     whole = lax.all_gather(own, "head", axis=0, tiled=False)
 
     piece = quarter // 2
     mine = [lax.dynamic_slice_in_dim(w_qkv, quarter * x + at, piece) for at in (0, piece)]
-    first, second = (move(item, MIRROR) for item in mine)
-    first, local = lax.optimization_barrier((first, w_qkv))
+    first = move(mine[0], MIRROR)
+    first, later, local = lax.optimization_barrier((first, mine[1], w_qkv))
     w_pair = move(local, SWAP)
+    second = move(later, MIRROR)
     first_up, first_down = move(first, X_UP), move(first, X_DOWN)
     second, first_up, first_down = lax.optimization_barrier((second, first_up, first_down))
     second_up, second_down = move(second, X_UP), move(second, X_DOWN)
     first_far, second_far = move(first_up, X_UP), move(second_down, X_DOWN)
     held = [(first, 0, 0), (first_up, 3, 0), (first_down, 1, 0), (first_far, 2, 0),
             (second, 0, 1), (second_up, 3, 1), (second_down, 1, 1), (second_far, 2, 1)]
-    places = jnp.stack([(x + away) % XS * quarter + sub * piece for _, away, sub in held]).astype(jnp.int32)
-    starts = [block, side * CORES + 1 - core, other + core, other + 1 - core]
-    starts = jnp.stack([item * part_rows for item in starts]).astype(jnp.int32)
+    blocks = [block, side * CORES + 1 - core, other + core, other + 1 - core]
+    places = [(x + away) % XS * quarter + sub * piece for _, away, sub in held]
+    spots = jnp.stack(blocks + places).astype(jnp.int32)
 
     smem = pl.BlockSpec(memory_space=pltpu.SMEM)
     vmem = pl.BlockSpec(memory_space=pltpu.VMEM)
-    hbm = pl.BlockSpec(memory_space=pltpu.HBM)
     anywhere = pl.BlockSpec(memory_space=pl.ANY)
 
     def sized(limit):
@@ -235,34 +224,31 @@
         compiler_params=sized(2),
         cost_estimate=pl.CostEstimate(flops=0, bytes_accessed=4 * MIB, transcendentals=0),
         name="pack",
-    )(places, *(item[0] for item in held))
+    )(spots, *(item[0] for item in held))
     pieces = [w_qkv, w_pair, w_rest, move(w_rest, SWAP)]
 
-    chunks = 4
     queries, kv = pl.pallas_call(
         functools.partial(project_kernel, len(pieces)),
         out_shape=(
             jax.ShapeDtypeStruct((rows, width), jnp.bfloat16),
             jax.ShapeDtypeStruct((rows, 2 * width), jnp.bfloat16),
         ),
-        in_specs=[smem] * 2 + [hbm] * 2 + [vmem] * 2 + [hbm] * len(pieces),
+        in_specs=[smem] * 2 + [vmem, anywhere, vmem, vmem] + [anywhere] * len(pieces),
         out_specs=(vmem, vmem),
         scratch_shapes=[
-            pltpu.VMEM((ring, rows, depth), jnp.bfloat16),
             pltpu.VMEM(mod_table.shape[1:], jnp.float32),
             pltpu.VMEM((ring * depth, columns), jnp.bfloat16),
             pltpu.VMEM((rows, ring * depth), jnp.bfloat16),
             pltpu.VMEM((rows, columns), jnp.float32),
-            pltpu.SemaphoreType.DMA((chunks,)),
             pltpu.SemaphoreType.DMA,
             pltpu.SemaphoreType.DMA((len(pieces),)),
         ],
-        compiler_params=sized(61.5),
+        compiler_params=sized(40),
         cost_estimate=pl.CostEstimate(
             flops=2 * rows * ring * depth * columns, bytes_accessed=12 * MIB, transcendentals=0
         ),
         name="project",
-    )(starts, levels, whole, mod_table, q_gain[None, :], k_gain[None, :], *pieces)
+    )(spots, levels, whole, mod_table, q_gain[None, :], k_gain[None, :], *pieces)
 
     far_kv = move(kv, ACROSS)
     pair_kv = move(kv, SWAP)

time: 134 us -> 140 us (1.045)
  the two profiles are of different devices: /device:TPU:111 before, /device:TPU:495 now
where the time goes in v6:
time: 140 us; the launch traced here: 139 us
  waiting for transfers between devices  52.6 us (38%)
  starting transfers between devices  43 us (31%)
  Pallas kernels  18.3 us (13%)
  between operations  14.4 us (10%)
  local copies, waits for them, and re-layouts  11.1 us (8%)
    ppermute x13, waiting for transfers between devices, move(): return lax.ppermute(array, ('block', 'req'), table)  51.9 us
    ppermute x13, starting transfers between devices, move(): return lax.ppermute(array, ('block', 'req'), table)  43 us
    unnamed x22, local copies, waits for them, and re-layouts  9.91 us
    pallas_call x1, Pallas kernels, body(): pl.pallas_call(functools.partial(project_kernel, len(pieces)), out_shape=...  8.28 us
    pallas_call x1, Pallas kernels, body(): pl.pallas_call(lambda *refs: far_kernel(3, True, *refs), out_shape=jax.Sh...  3.33 us
    pallas_call x1, Pallas kernels, body(): pl.pallas_call(near_kernel, out_shape=sums, in_specs=[smem] * 3 + [vmem]...  3.04 us
    pallas_call x1, Pallas kernels, body(): pl.pallas_call(pack_kernel, out_shape=jax.ShapeDtypeStruct(w_qkv.shape, w...  2.93 us
  transfers between devices with their start and end apart: 14, of which 9 were waited for; matrix products, arithmetic and copies ran while one was open for 1% of the time, Pallas kernels for 5%

profile of v6, /device:TPU:495, one launch (start us, length us, event | category | flops | bytes accessed | tf_op | source)
XLA Modules:
  0.0 139.3 jit_solution(1795138097390410483)
XLA Ops:
  6.5 0.0 all-gather.3.cloned.1.call-start
  6.5 0.7 all-gather.3.cloned.1.call-update
  7.3 1.1 constant_dynamic-slice_fusion
  8.4 2.7 %collective-permute-start = (bf16[96,1152]{1,0:T(8,128)(2,1)S(1)}, bf16[96,1152]{1,0:T(8,128)(2,1)S(1)}, u32[]{:S(2)}, u32[]{:S(2)}) collective-permute-start(bf16[96,1152]{1,0:T(8,128)(2,1)S(1)} %get-tuple-element.36), channel_id=1, source_target_pairs={{0,280},{32,312},{64,344},{96,376},{128,408},{160,440},{192,472},{... | collective-permute-start | bytes 663560 | tf_op jit(solution)/shard_map/ppermute | solution.py:42
  11.1 8.5 %collective-permute-done.refs_0_ = bf16[96,1152]{1,0:T(8,128)(2,1)S(1)} collective-permute-done((bf16[96,1152]{1,0:T(8,128)(2,1)S(1)}, bf16[96,1152]{1,0:T(8,128)(2,1)S(1)}, u32[]{:S(2)}, u32[]{:S(2)}) %collective-permute-start) | collective-permute-done | bytes 221216 | tf_op jit(solution)/shard_map/ppermute | solution.py:42
  19.7 2.7 %collective-permute-start.2 = (bf16[96,1152]{1,0:T(8,128)(2,1)S(1)}, bf16[96,1152]{1,0:T(8,128)(2,1)S(1)}, u32[]{:S(2)}, u32[]{:S(2)}) collective-permute-start(bf16[96,1152]{1,0:T(8,128)(2,1)S(1)} %get-tuple-element.22), channel_id=1, source_target_pairs={{0,280},{32,312},{64,344},{96,376},{128,408},{160,440},{192,472},{... | collective-permute-start | bytes 663560 | tf_op jit(solution)/shard_map/ppermute | solution.py:42
  22.4 2.5 %collective-permute-start.4 = (bf16[96,1152]{1,0:T(8,128)(2,1)S(1)}, bf16[96,1152]{1,0:T(8,128)(2,1)S(1)}, u32[]{:S(2)}, u32[]{:S(2)}) collective-permute-start(bf16[96,1152]{1,0:T(8,128)(2,1)S(1)} %collective-permute-done.refs_0_), channel_id=1, source_target_pairs={{0,96},{32,0},{64,32},{96,64},{128,224},{160,128},{192,160},{224,1... | collective-permute-start | bytes 663560 | tf_op jit(solution)/shard_map/ppermute | solution.py:42
  24.9 4.0 %collective-permute-start.3 = (bf16[96,1152]{1,0:T(8,128)(2,1)S(1)}, bf16[96,1152]{1,0:T(8,128)(2,1)S(1)}, u32[]{:S(2)}, u32[]{:S(2)}) collective-permute-start(bf16[96,1152]{1,0:T(8,128)(2,1)S(1)} %collective-permute-done.refs_0_), channel_id=1, source_target_pairs={{0,32},{32,64},{64,96},{96,0},{128,160},{160,192},{192,224},{224,1... | collective-permute-start | bytes 663560 | tf_op jit(solution)/shard_map/ppermute | solution.py:42
  28.9 1.0 collective-permute-done.2.refs_4_
  29.9 0.8 collective-permute-done.4.refs_2_
  30.7 1.3 collective-permute-done.3.refs_1_
  31.9 2.2 %collective-permute-start.7 = (bf16[96,1152]{1,0:T(8,128)(2,1)S(1)}, bf16[96,1152]{1,0:T(8,128)(2,1)S(1)}, u32[]{:S(2)}, u32[]{:S(2)}) collective-permute-start(bf16[96,1152]{1,0:T(8,128)(2,1)S(1)} %collective-permute-done.2.refs_4_), channel_id=1, source_target_pairs={{0,96},{32,0},{64,32},{96,64},{128,224},{160,128},{192,160},{224,1... | collective-permute-start | bytes 663560 | tf_op jit(solution)/shard_map/ppermute | solution.py:42
  34.1 5.0 %collective-permute-start.6 = (bf16[96,1152]{1,0:T(8,128)(2,1)S(1)}, bf16[96,1152]{1,0:T(8,128)(2,1)S(1)}, u32[]{:S(2)}, u32[]{:S(2)}) collective-permute-start(bf16[96,1152]{1,0:T(8,128)(2,1)S(1)} %collective-permute-done.2.refs_4_), channel_id=1, source_target_pairs={{0,32},{32,64},{64,96},{96,0},{128,160},{160,192},{192,224},{224,1... | collective-permute-start | bytes 663560 | tf_op jit(solution)/shard_map/ppermute | solution.py:42
  39.1 3.4 %collective-permute-start.5 = (bf16[96,1152]{1,0:T(8,128)(2,1)S(1)}, bf16[96,1152]{1,0:T(8,128)(2,1)S(1)}, u32[]{:S(2)}, u32[]{:S(2)}) collective-permute-start(bf16[96,1152]{1,0:T(8,128)(2,1)S(1)} %collective-permute-done.3.refs_1_), channel_id=1, source_target_pairs={{0,32},{32,64},{64,96},{96,0},{128,160},{160,192},{192,224},{224,1... | collective-permute-start | bytes 663560 | tf_op jit(solution)/shard_map/ppermute | solution.py:42
  42.5 0.0 collective-permute-done.7.refs_6_
  42.5 1.9 %collective-permute-start.8 = (bf16[96,1152]{1,0:T(8,128)(2,1)S(1)}, bf16[96,1152]{1,0:T(8,128)(2,1)S(1)}, u32[]{:S(2)}, u32[]{:S(2)}) collective-permute-start(bf16[96,1152]{1,0:T(8,128)(2,1)S(1)} %collective-permute-done.7.refs_6_), channel_id=1, source_target_pairs={{0,96},{32,0},{64,32},{96,64},{128,224},{160,128},{192,160},{224,1... | collective-permute-start | bytes 663560 | tf_op jit(solution)/shard_map/ppermute | solution.py:42
  44.5 0.1 stack.51.spots.refs_0_
  44.6 0.0 copy-start.9
  44.6 0.0 copy-start.10
  44.6 5.8 %collective-permute-start.1 = (bf16[768,1152]{1,0:T(8,128)(2,1)}, bf16[768,1152]{1,0:T(8,128)(2,1)S(1)}, u32[]{:S(2)}, u32[]{:S(2)}) collective-permute-start(bf16[768,1152]{1,0:T(8,128)(2,1)} %refs_4_.1), channel_id=1, source_target_pairs={{0,128},{32,160},{64,192},{96,224},{128,0},{160,32},{192,64},{224,... | collective-permute-start | bytes 5308424 | tf_op jit(solution)/shard_map/ppermute | solution.py:42
  50.4 0.0 collective-permute-done.5.refs_3_
  50.4 0.0 collective-permute-done.6.refs_5_
  50.4 0.4 collective-permute-done.8.refs_7_
  50.8 2.9 %pack.1.refs_6_ = bf16[768,1152]{1,0:T(8,128)(2,1)S(1)} custom-call(s32[12]{0:T(128)S(1)} %stack.51.spots.refs_0_, bf16[96,1152]{1,0:T(8,128)(2,1)S(1)} %collective-permute-done.refs_0_, bf16[96,1152]{1,0:T(8,128)(2,1)S(1)} %collective-permute-done.3.refs_1_, bf16[96,1152]{1,0:T(8,128)(2,1)S(1)} %collective-permute-done.4.refs_2_, ...), custom_call_target="tpu_custom_call" | custom-call | bytes 4194304 | tf_op jit(solution)/shard_map/pack/pallas_call | solution.py:218
  53.7 6.4 %collective-permute-start.9 = (bf16[768,1152]{1,0:T(8,128)(2,1)S(1)}, bf16[768,1152]{1,0:T(8,128)(2,1)S(1)}, u32[]{:S(2)}, u32[]{:S(2)}) collective-permute-start(bf16[768,1152]{1,0:T(8,128)(2,1)S(1)} %pack.1.refs_6_), channel_id=1, source_target_pairs={{0,128},{32,160},{64,192},{96,224},{128,0},{160,32},{192,64},{224,... | collective-permute-start | bytes 5308424 | tf_op jit(solution)/shard_map/ppermute | solution.py:42
  60.8 0.0 collective-permute-done.1.refs_5_
  60.8 0.0 copy-start.4
  60.8 1.2 copy-done.4
  62.0 1.4 %collective-permute-done.9.refs_7_ = bf16[768,1152]{1,0:T(8,128)(2,1)S(1)} collective-permute-done((bf16[768,1152]{1,0:T(8,128)(2,1)S(1)}, bf16[768,1152]{1,0:T(8,128)(2,1)S(1)}, u32[]{:S(2)}, u32[]{:S(2)}) %collective-permute-start.9) | collective-permute-done | bytes 1769504 | tf_op jit(solution)/shard_map/ppermute | solution.py:42
  63.4 1.2 copy-done.6
  64.6 0.0 copy-done.9
  64.6 0.0 copy-done.10
  64.7 1.5 %copy-done = bf16[768,1152]{1,0:T(8,128)(2,1)S(1)} copy-done((bf16[768,1152]{1,0:T(8,128)(2,1)S(1)}, bf16[768,1152]{1,0:T(8,128)(2,1)}, u32[]{:S(2)}) %copy-start) | copy-done | bytes 1769496
  66.1 1.9 %copy-done.3 = bf16[8,1,512,384]{3,2,1,0:T(8,128)(2,1)S(1)} copy-done((bf16[8,1,512,384]{3,2,1,0:T(8,128)(2,1)S(1)}, bf16[8,1,512,384]{3,2,1,0:T(8,128)(2,1)}, u32[]{:S(2)}) %copy-start.3) | copy-done | bytes 3145752
  68.0 1.5 %copy-done.5 = bf16[768,1152]{1,0:T(8,128)(2,1)S(1)} copy-done((bf16[768,1152]{1,0:T(8,128)(2,1)S(1)}, bf16[768,1152]{1,0:T(8,128)(2,1)}, u32[]{:S(2)}) %copy-start.5) | copy-done | bytes 1769496
  69.5 1.5 %copy-done.7 = bf16[768,1152]{1,0:T(8,128)(2,1)S(1)} copy-done((bf16[768,1152]{1,0:T(8,128)(2,1)S(1)}, bf16[768,1152]{1,0:T(8,128)(2,1)}, u32[]{:S(2)}) %copy-start.7) | copy-done | bytes 1769496
  71.0 1.1 copy-done.8
  72.1 8.3 %project.1 = (bf16[512,384]{1,0:T(8,128)(2,1)S(1)}, bf16[512,768]{1,0:T(8,128)(2,1)S(1)}) custom-call(s32[12]{0:T(128)S(1)} %stack.51.spots.refs_0_, s32[1,1]{1,0:T(1,128)S(6)} %copy.10.levels, bf16[8,512,384]{2,1,0:T(8,128)(2,1)S(1)} %bitcast.20, f32[32,2,3072]{2,1,0:T(2,128)S(1)} %copy-done.8, f32[1,128]{1,0:T(1,128)S(1)} %bitcast.21, ...), custom_call_target="tpu_custom_call" | custom-call | flops 3623878656 | bytes 12582912 | tf_op jit(solution)/shard_map/project/pallas_call | solution.py:230
  80.4 2.3 %collective-permute-start.11 = (bf16[512,768]{1,0:T(8,128)(2,1)S(1)}, bf16[512,768]{1,0:T(8,128)(2,1)S(1)}, u32[]{:S(2)}, u32[]{:S(2)}) collective-permute-start(bf16[512,768]{1,0:T(8,128)(2,1)S(1)} %get-tuple-element.27.own), channel_id=1, source_target_pairs={{0,128},{32,160},{64,192},{96,224},{128,0},{160,32},{192,64},{224,... | collective-permute-start | bytes 2359304 | tf_op jit(solution)/shard_map/ppermute | solution.py:42
  82.7 1.3 collective-permute-start.10
  84.0 0.6 collective-permute-done.11.pair
  84.6 0.0 copy-done.1
  84.6 3.0 %near.1 = (f32[512,384]{1,0:T(8,128)S(1)}, f32[512,384]{1,0:T(8,128)S(1)}) custom-call(s32[12]{0:T(128)S(1)} %stack.51.spots.refs_0_, s32[1,4]{1,0:T(1,128)S(1)} %copy-done.2, s32[4,4]{1,0:T(4,128)S(1)} %bitcast.17, bf16[512,384]{1,0:T(8,128)(2,1)S(1)} %get-tuple-element.26.q.refs_3_, bf16[512,768]{1,0:T(8,128)(2,1)S(1)} %get-tuple-element.27.own, ...), custom_call_target="tpu_custom_call" | custom-call | flops 805306368 | bytes 6291456 | tf_op jit(solution)/shard_map/near/pallas_call | solution.py:261
  87.6 36.7 %collective-permute-done.10.refs_6_ = bf16[512,768]{1,0:T(8,128)(2,1)S(1)} collective-permute-done((bf16[512,768]{1,0:T(8,128)(2,1)S(1)}, bf16[512,768]{1,0:T(8,128)(2,1)S(1)}, u32[]{:S(2)}, u32[]{:S(2)}) %collective-permute-start.10) | collective-permute-done | bytes 786464 | tf_op jit(solution)/shard_map/ppermute | solution.py:42
  124.4 2.8 %collective-permute-start.12 = (bf16[512,768]{1,0:T(8,128)(2,1)S(1)}, bf16[512,768]{1,0:T(8,128)(2,1)S(1)}, u32[]{:S(2)}, u32[]{:S(2)}) collective-permute-start(bf16[512,768]{1,0:T(8,128)(2,1)S(1)} %collective-permute-done.10.refs_6_), channel_id=1, source_target_pairs={{0,128},{32,160},{64,192},{96,224},{128,0},{160,32},{192,64},{224,... | collective-permute-start | bytes 2359304 | tf_op jit(solution)/shard_map/ppermute | solution.py:42
  127.2 0.7 far.1
  127.9 1.2 collective-permute-done.12.refs_6_
  129.1 3.3 %last.1 = bf16[512,384]{1,0:T(8,128)(2,1)} custom-call(s32[12]{0:T(128)S(1)} %stack.51.spots.refs_0_, s32[1,4]{1,0:T(1,128)S(1)} %copy-done.2, s32[4,4]{1,0:T(4,128)S(1)} %bitcast.19, bf16[512,384]{1,0:T(8,128)(2,1)S(1)} %get-tuple-element.26.q.refs_3_, f32[512,384]{1,0:T(8,128)S(1)} %get-tuple-element.33.refs_4_, f32[512,384]{1,0:T(8,128)S(1)} %get-tuple-element.34.refs_5_, ...), custom_call_target="tpu_custom_call" | custom-call | flops 805306368 | bytes 6291456 | tf_op jit(solution)/shard_map/last/pallas_call | solution.py:281
  (10 shorter events, 0.0 us)
Async XLA Ops:
  6.5 58.1 %all-gather.3.cloned.1.call-start = ((), (), s32[]{:S(2)}) async-start(), calls=%async_computation | async-start | bytes 3538944 | tf_op jit(solution)/shard_map/all_gather | solution.py:193
  8.4 11.3 %collective-permute-start = (bf16[96,1152]{1,0:T(8,128)(2,1)S(1)}, bf16[96,1152]{1,0:T(8,128)(2,1)S(1)}, u32[]{:S(2)}, u32[]{:S(2)}) collective-permute-start(bf16[96,1152]{1,0:T(8,128)(2,1)S(1)} %get-tuple-element.36), channel_id=1, source_target_pairs={{0,280},{32,312},{64,344},{96,376},{128,408},{160,440},{192,472},{... | collective-permute-start | bytes 663560 | tf_op jit(solution)/shard_map/ppermute | solution.py:42
  19.7 10.2 %collective-permute-start.2 = (bf16[96,1152]{1,0:T(8,128)(2,1)S(1)}, bf16[96,1152]{1,0:T(8,128)(2,1)S(1)}, u32[]{:S(2)}, u32[]{:S(2)}) collective-permute-start(bf16[96,1152]{1,0:T(8,128)(2,1)S(1)} %get-tuple-element.22), channel_id=1, source_target_pairs={{0,280},{32,312},{64,344},{96,376},{128,408},{160,440},{192,472},{... | collective-permute-start | bytes 663560 | tf_op jit(solution)/shard_map/ppermute | solution.py:42
  22.4 8.3 %collective-permute-start.4 = (bf16[96,1152]{1,0:T(8,128)(2,1)S(1)}, bf16[96,1152]{1,0:T(8,128)(2,1)S(1)}, u32[]{:S(2)}, u32[]{:S(2)}) collective-permute-start(bf16[96,1152]{1,0:T(8,128)(2,1)S(1)} %collective-permute-done.refs_0_), channel_id=1, source_target_pairs={{0,96},{32,0},{64,32},{96,64},{128,224},{160,128},{192,160},{224,1... | collective-permute-start | bytes 663560 | tf_op jit(solution)/shard_map/ppermute | solution.py:42
  24.9 7.1 %collective-permute-start.3 = (bf16[96,1152]{1,0:T(8,128)(2,1)S(1)}, bf16[96,1152]{1,0:T(8,128)(2,1)S(1)}, u32[]{:S(2)}, u32[]{:S(2)}) collective-permute-start(bf16[96,1152]{1,0:T(8,128)(2,1)S(1)} %collective-permute-done.refs_0_), channel_id=1, source_target_pairs={{0,32},{32,64},{64,96},{96,0},{128,160},{160,192},{192,224},{224,1... | collective-permute-start | bytes 663560 | tf_op jit(solution)/shard_map/ppermute | solution.py:42
  31.9 10.5 %collective-permute-start.7 = (bf16[96,1152]{1,0:T(8,128)(2,1)S(1)}, bf16[96,1152]{1,0:T(8,128)(2,1)S(1)}, u32[]{:S(2)}, u32[]{:S(2)}) collective-permute-start(bf16[96,1152]{1,0:T(8,128)(2,1)S(1)} %collective-permute-done.2.refs_4_), channel_id=1, source_target_pairs={{0,96},{32,0},{64,32},{96,64},{128,224},{160,128},{192,160},{224,1... | collective-permute-start | bytes 663560 | tf_op jit(solution)/shard_map/ppermute | solution.py:42
  34.1 16.3 %collective-permute-start.6 = (bf16[96,1152]{1,0:T(8,128)(2,1)S(1)}, bf16[96,1152]{1,0:T(8,128)(2,1)S(1)}, u32[]{:S(2)}, u32[]{:S(2)}) collective-permute-start(bf16[96,1152]{1,0:T(8,128)(2,1)S(1)} %collective-permute-done.2.refs_4_), channel_id=1, source_target_pairs={{0,32},{32,64},{64,96},{96,0},{128,160},{160,192},{192,224},{224,1... | collective-permute-start | bytes 663560 | tf_op jit(solution)/shard_map/ppermute | solution.py:42
  39.1 11.3 %collective-permute-start.5 = (bf16[96,1152]{1,0:T(8,128)(2,1)S(1)}, bf16[96,1152]{1,0:T(8,128)(2,1)S(1)}, u32[]{:S(2)}, u32[]{:S(2)}) collective-permute-start(bf16[96,1152]{1,0:T(8,128)(2,1)S(1)} %collective-permute-done.3.refs_1_), channel_id=1, source_target_pairs={{0,32},{32,64},{64,96},{96,0},{128,160},{160,192},{192,224},{224,1... | collective-permute-start | bytes 663560 | tf_op jit(solution)/shard_map/ppermute | solution.py:42
  42.5 8.3 %collective-permute-start.8 = (bf16[96,1152]{1,0:T(8,128)(2,1)S(1)}, bf16[96,1152]{1,0:T(8,128)(2,1)S(1)}, u32[]{:S(2)}, u32[]{:S(2)}) collective-permute-start(bf16[96,1152]{1,0:T(8,128)(2,1)S(1)} %collective-permute-done.7.refs_6_), channel_id=1, source_target_pairs={{0,96},{32,0},{64,32},{96,64},{128,224},{160,128},{192,160},{224,1... | collective-permute-start | bytes 663560 | tf_op jit(solution)/shard_map/ppermute | solution.py:42
  44.6 20.0 %copy-start.9 = (f32[128]{0:T(128)S(1)}, f32[128]{0:T(128)}, u32[]{:S(2)}) copy-start(f32[128]{0:T(128)} %param.14) | copy-start | bytes 1540
  44.6 20.0 %copy-start.10 = (f32[128]{0:T(128)S(1)}, f32[128]{0:T(128)}, u32[]{:S(2)}) copy-start(f32[128]{0:T(128)} %param.15) | copy-start | bytes 1540
  44.6 16.1 %collective-permute-start.1 = (bf16[768,1152]{1,0:T(8,128)(2,1)}, bf16[768,1152]{1,0:T(8,128)(2,1)S(1)}, u32[]{:S(2)}, u32[]{:S(2)}) collective-permute-start(bf16[768,1152]{1,0:T(8,128)(2,1)} %refs_4_.1), channel_id=1, source_target_pairs={{0,128},{32,160},{64,192},{96,224},{128,0},{160,32},{192,64},{224,... | collective-permute-start | bytes 5308424 | tf_op jit(solution)/shard_map/ppermute | solution.py:42
  53.7 9.7 %collective-permute-start.9 = (bf16[768,1152]{1,0:T(8,128)(2,1)S(1)}, bf16[768,1152]{1,0:T(8,128)(2,1)S(1)}, u32[]{:S(2)}, u32[]{:S(2)}) collective-permute-start(bf16[768,1152]{1,0:T(8,128)(2,1)S(1)} %pack.1.refs_6_), channel_id=1, source_target_pairs={{0,128},{32,160},{64,192},{96,224},{128,0},{160,32},{192,64},{224,... | collective-permute-start | bytes 5308424 | tf_op jit(solution)/shard_map/ppermute | solution.py:42
  60.8 1.2 copy-start.4
  63.4 1.2 copy-start.6
  64.7 1.5 %copy-start = (bf16[768,1152]{1,0:T(8,128)(2,1)S(1)}, bf16[768,1152]{1,0:T(8,128)(2,1)}, u32[]{:S(2)}) copy-start(bf16[768,1152]{1,0:T(8,128)(2,1)} %refs_4_.1) | copy-start | bytes 5308420
  66.1 1.9 %copy-start.3 = (bf16[8,1,512,384]{3,2,1,0:T(8,128)(2,1)S(1)}, bf16[8,1,512,384]{3,2,1,0:T(8,128)(2,1)}, u32[]{:S(2)}) copy-start(bf16[8,1,512,384]{3,2,1,0:T(8,128)(2,1)} %all-gather.3.cloned.1.call-done) | copy-start | bytes 9437188
  68.0 1.5 %copy-start.5 = (bf16[768,1152]{1,0:T(8,128)(2,1)S(1)}, bf16[768,1152]{1,0:T(8,128)(2,1)}, u32[]{:S(2)}) copy-start(bf16[768,1152]{1,0:T(8,128)(2,1)} %copy-done.4) | copy-start | bytes 5308420
  69.5 1.5 %copy-start.7 = (bf16[768,1152]{1,0:T(8,128)(2,1)S(1)}, bf16[768,1152]{1,0:T(8,128)(2,1)}, u32[]{:S(2)}) copy-start(bf16[768,1152]{1,0:T(8,128)(2,1)} %copy-done.6) | copy-start | bytes 5308420
  71.0 1.1 copy-start.8
  72.1 12.5 %copy-start.1 = (s32[1,4,4]{2,1,0:T(4,128)S(1)}, s32[1,4,4]{2,1,0:T(4,128)}, u32[]{:S(2)}) copy-start(s32[1,4,4]{2,1,0:T(4,128)} %param.11) | copy-start | bytes 196
  72.1 12.5 %copy-start.2 = (s32[1,4]{1,0:T(1,128)S(1)}, s32[1,4]{1,0:T(1,128)}, u32[]{:S(2)}) copy-start(s32[1,4]{1,0:T(1,128)} %refs_1_.5) | copy-start | bytes 52
  80.4 4.2 %collective-permute-start.11 = (bf16[512,768]{1,0:T(8,128)(2,1)S(1)}, bf16[512,768]{1,0:T(8,128)(2,1)S(1)}, u32[]{:S(2)}, u32[]{:S(2)}) collective-permute-start(bf16[512,768]{1,0:T(8,128)(2,1)S(1)} %get-tuple-element.27.own), channel_id=1, source_target_pairs={{0,128},{32,160},{64,192},{96,224},{128,0},{160,32},{192,64},{224,... | collective-permute-start | bytes 2359304 | tf_op jit(solution)/shard_map/ppermute | solution.py:42
  82.7 41.7 %collective-permute-start.10 = (bf16[512,768]{1,0:T(8,128)(2,1)S(1)}, bf16[512,768]{1,0:T(8,128)(2,1)S(1)}, u32[]{:S(2)}, u32[]{:S(2)}) collective-permute-start(bf16[512,768]{1,0:T(8,128)(2,1)S(1)} %get-tuple-element.27.own), channel_id=1, source_target_pairs={{0,256},{32,288},{64,320},{96,352},{128,384},{160,416},{192,448},{... | collective-permute-start | bytes 2359304 | tf_op jit(solution)/shard_map/ppermute | solution.py:42
  124.4 4.7 %collective-permute-start.12 = (bf16[512,768]{1,0:T(8,128)(2,1)S(1)}, bf16[512,768]{1,0:T(8,128)(2,1)S(1)}, u32[]{:S(2)}, u32[]{:S(2)}) collective-permute-start(bf16[512,768]{1,0:T(8,128)(2,1)S(1)} %collective-permute-done.10.refs_6_), channel_id=1, source_target_pairs={{0,128},{32,160},{64,192},{96,224},{128,0},{160,32},{192,64},{224,... | collective-permute-start | bytes 2359304 | tf_op jit(solution)/shard_map/ppermute | solution.py:42
Sparse Core Ops, SparseCore 0:
  9.4 44.8 all-gather.2

commit v7 on v5

--- a/solution.py
+++ b/solution.py
@@ -42,18 +42,18 @@
     return lax.ppermute(array, ("block", "req"), table)
 
 
-def pack_kernel(starts, *refs):
+def pack_kernel(spots, *refs):
     pieces, out, sems = refs[:-2], refs[-2], refs[-1]
     copies = []
     for number, piece in enumerate(pieces):
-        band = pl.ds(pl.multiple_of(starts[number], 96), piece.shape[0])
+        band = pl.ds(pl.multiple_of(spots[4 + number], 96), piece.shape[0])
         copies.append(pltpu.make_async_copy(piece, out.at[band, :], sems.at[number]))
         copies[-1].start()
     for copy in copies:
         copy.wait()
 
 
-def project_kernel(n_pieces, starts, levels, *refs):
+def project_kernel(n_pieces, spots, levels, *refs):
     tokens_far, table, q_gain, k_gain = refs[:4]
     pieces = refs[4 : 4 + n_pieces]
     q_out, kv_out, tokens, mod, weight, normed, projected, token_sems, mod_sem, sems = refs[4 + n_pieces :]
@@ -72,7 +72,7 @@
         loads[-1].start()
     weights = []
     for number, piece in enumerate(pieces):
-        band = pl.ds(pl.multiple_of(starts[number], 96), piece.shape[0])
+        band = pl.ds(pl.multiple_of(spots[number] * piece.shape[0], 96), piece.shape[0])
         weights.append(pltpu.make_async_copy(piece, weight.at[band, :], sems.at[number]))
         weights[-1].start()
     mod_load.wait()
@@ -199,24 +199,24 @@
     side, core = block // CORES, block % CORES
     x = lax.axis_index("req") // YS
     other = (1 - side) * CORES
-    spots = jnp.stack([block, side * CORES + 1 - core, other + core, other + 1 - core]).astype(jnp.int32)
 
     whole = lax.all_gather(own, "head", axis=0, tiled=False)
 
     piece = quarter // 2
     mine = [lax.dynamic_slice_in_dim(w_qkv, quarter * x + at, piece) for at in (0, piece)]
-    first, second = (move(item, MIRROR) for item in mine)
-    first, local = lax.optimization_barrier((first, w_qkv))
+    first = move(mine[0], MIRROR)
+    first, later, local = lax.optimization_barrier((first, mine[1], w_qkv))
     w_pair = move(local, SWAP)
+    second = move(later, MIRROR)
     first_up, first_down = move(first, X_UP), move(first, X_DOWN)
     second, first_up, first_down = lax.optimization_barrier((second, first_up, first_down))
     second_up, second_down = move(second, X_UP), move(second, X_DOWN)
     first_far, second_far = move(first_up, X_UP), move(second_down, X_DOWN)
     held = [(first, 0, 0), (first_up, 3, 0), (first_down, 1, 0), (first_far, 2, 0),
             (second, 0, 1), (second_up, 3, 1), (second_down, 1, 1), (second_far, 2, 1)]
-    places = jnp.stack([(x + away) % XS * quarter + sub * piece for _, away, sub in held]).astype(jnp.int32)
-    starts = [block, side * CORES + 1 - core, other + core, other + 1 - core]
-    starts = jnp.stack([item * part_rows for item in starts]).astype(jnp.int32)
+    blocks = [block, side * CORES + 1 - core, other + core, other + 1 - core]
+    places = [(x + away) % XS * quarter + sub * piece for _, away, sub in held]
+    spots = jnp.stack(blocks + places).astype(jnp.int32)
 
     smem = pl.BlockSpec(memory_space=pltpu.SMEM)
     vmem = pl.BlockSpec(memory_space=pltpu.VMEM)
@@ -235,7 +235,7 @@
         compiler_params=sized(2),
         cost_estimate=pl.CostEstimate(flops=0, bytes_accessed=4 * MIB, transcendentals=0),
         name="pack",
-    )(places, *(item[0] for item in held))
+    )(spots, *(item[0] for item in held))
     pieces = [w_qkv, w_pair, w_rest, move(w_rest, SWAP)]
 
     chunks = 4
@@ -262,7 +262,7 @@
             flops=2 * rows * ring * depth * columns, bytes_accessed=12 * MIB, transcendentals=0
         ),
         name="project",
-    )(starts, levels, whole, mod_table, q_gain[None, :], k_gain[None, :], *pieces)
+    )(spots, levels, whole, mod_table, q_gain[None, :], k_gain[None, :], *pieces)
 
     far_kv = move(kv, ACROSS)
     pair_kv = move(kv, SWAP)

time: 134 us -> 136 us (1.015)
  waiting for transfers between devices: 44.2 us -> 50.8 us
  starting transfers between devices: 47 us -> 43.4 us
  Pallas kernels: 22.8 us -> 21.4 us
    ppermute x13, waiting for transfers between devices: 43.5 us -> 50.1 us  [move(): return lax.ppermute(array, ('block', 'req'), table)]
    ppermute x13, starting transfers between devices: 47 us -> 43.4 us  [move(): return lax.ppermute(array, ('block', 'req'), table)]
    unnamed x14 -> x18, local copies, waits for them, and re-layouts: 3.76 us -> 4.31 us
  transfers between devices with their start and end apart: 14 -> 14, of which waited for: 6 -> 8; matrix products, arithmetic and copies ran while one was open for 1% -> 1% of each run, Pallas kernels for 6% -> 6%
where the time goes in v7:
time: 136 us; the launch traced here: 135 us
  waiting for transfers between devices  50.8 us (37%)
  starting transfers between devices  43.4 us (32%)
  Pallas kernels  21.4 us (16%)
  between operations  14.4 us (11%)
  local copies, waits for them, and re-layouts  5.49 us (4%)
    ppermute x13, waiting for transfers between devices, move(): return lax.ppermute(array, ('block', 'req'), table)  50.1 us
    ppermute x13, starting transfers between devices, move(): return lax.ppermute(array, ('block', 'req'), table)  43.4 us
    pallas_call x1, Pallas kernels, body(): pl.pallas_call(functools.partial(project_kernel, len(pieces)), out_shape=...  10.6 us
    unnamed x18, local copies, waits for them, and re-layouts  4.31 us
    pallas_call x1, Pallas kernels, body(): pl.pallas_call(lambda *refs: far_kernel(3, True, *refs), out_shape=jax.Sh...  3.34 us
    pallas_call x1, Pallas kernels, body(): pl.pallas_call(near_kernel, out_shape=sums, in_specs=[smem] * 3 + [vmem]...  3.06 us
    pallas_call x1, Pallas kernels, body(): pl.pallas_call(pack_kernel, out_shape=jax.ShapeDtypeStruct(w_qkv.shape, w...  2.93 us
  transfers between devices with their start and end apart: 14, of which 8 were waited for; matrix products, arithmetic and copies ran while one was open for 1% of the time, Pallas kernels for 6%

profile of v7, /device:TPU:111, one launch (start us, length us, event | category | flops | bytes accessed | tf_op | source)
XLA Modules:
  0.0 135.4 jit_solution(16609588861954554683)
XLA Ops:
  6.5 0.0 all-gather.3.cloned.1.call-start
  6.5 0.7 all-gather.3.cloned.1.call-update
  7.3 1.1 constant_dynamic-slice_fusion
  8.4 2.7 %collective-permute-start = (bf16[96,1152]{1,0:T(8,128)(2,1)S(1)}, bf16[96,1152]{1,0:T(8,128)(2,1)S(1)}, u32[]{:S(2)}, u32[]{:S(2)}) collective-permute-start(bf16[96,1152]{1,0:T(8,128)(2,1)S(1)} %get-tuple-element.36), channel_id=1, source_target_pairs={{0,280},{32,312},{64,344},{96,376},{128,408},{160,440},{192,472},{... | collective-permute-start | bytes 663560 | tf_op jit(solution)/shard_map/ppermute | solution.py:42
  11.1 8.5 %collective-permute-done.refs_0_ = bf16[96,1152]{1,0:T(8,128)(2,1)S(1)} collective-permute-done((bf16[96,1152]{1,0:T(8,128)(2,1)S(1)}, bf16[96,1152]{1,0:T(8,128)(2,1)S(1)}, u32[]{:S(2)}, u32[]{:S(2)}) %collective-permute-start) | collective-permute-done | bytes 221216 | tf_op jit(solution)/shard_map/ppermute | solution.py:42
  19.7 2.7 %collective-permute-start.2 = (bf16[96,1152]{1,0:T(8,128)(2,1)S(1)}, bf16[96,1152]{1,0:T(8,128)(2,1)S(1)}, u32[]{:S(2)}, u32[]{:S(2)}) collective-permute-start(bf16[96,1152]{1,0:T(8,128)(2,1)S(1)} %get-tuple-element.22), channel_id=1, source_target_pairs={{0,280},{32,312},{64,344},{96,376},{128,408},{160,440},{192,472},{... | collective-permute-start | bytes 663560 | tf_op jit(solution)/shard_map/ppermute | solution.py:42
  22.4 2.5 %collective-permute-start.4 = (bf16[96,1152]{1,0:T(8,128)(2,1)S(1)}, bf16[96,1152]{1,0:T(8,128)(2,1)S(1)}, u32[]{:S(2)}, u32[]{:S(2)}) collective-permute-start(bf16[96,1152]{1,0:T(8,128)(2,1)S(1)} %collective-permute-done.refs_0_), channel_id=1, source_target_pairs={{0,96},{32,0},{64,32},{96,64},{128,224},{160,128},{192,160},{224,1... | collective-permute-start | bytes 663560 | tf_op jit(solution)/shard_map/ppermute | solution.py:42
  24.9 4.0 %collective-permute-start.3 = (bf16[96,1152]{1,0:T(8,128)(2,1)S(1)}, bf16[96,1152]{1,0:T(8,128)(2,1)S(1)}, u32[]{:S(2)}, u32[]{:S(2)}) collective-permute-start(bf16[96,1152]{1,0:T(8,128)(2,1)S(1)} %collective-permute-done.refs_0_), channel_id=1, source_target_pairs={{0,32},{32,64},{64,96},{96,0},{128,160},{160,192},{192,224},{224,1... | collective-permute-start | bytes 663560 | tf_op jit(solution)/shard_map/ppermute | solution.py:42
  28.9 1.0 collective-permute-done.2.refs_4_
  29.9 0.7 collective-permute-done.4.refs_2_
  30.6 1.4 %collective-permute-done.3.refs_1_ = bf16[96,1152]{1,0:T(8,128)(2,1)S(1)} collective-permute-done((bf16[96,1152]{1,0:T(8,128)(2,1)S(1)}, bf16[96,1152]{1,0:T(8,128)(2,1)S(1)}, u32[]{:S(2)}, u32[]{:S(2)}) %collective-permute-start.3) | collective-permute-done | bytes 221216 | tf_op jit(solution)/shard_map/ppermute | solution.py:42
  31.9 2.2 %collective-permute-start.7 = (bf16[96,1152]{1,0:T(8,128)(2,1)S(1)}, bf16[96,1152]{1,0:T(8,128)(2,1)S(1)}, u32[]{:S(2)}, u32[]{:S(2)}) collective-permute-start(bf16[96,1152]{1,0:T(8,128)(2,1)S(1)} %collective-permute-done.2.refs_4_), channel_id=1, source_target_pairs={{0,96},{32,0},{64,32},{96,64},{128,224},{160,128},{192,160},{224,1... | collective-permute-start | bytes 663560 | tf_op jit(solution)/shard_map/ppermute | solution.py:42
  34.1 4.6 %collective-permute-start.6 = (bf16[96,1152]{1,0:T(8,128)(2,1)S(1)}, bf16[96,1152]{1,0:T(8,128)(2,1)S(1)}, u32[]{:S(2)}, u32[]{:S(2)}) collective-permute-start(bf16[96,1152]{1,0:T(8,128)(2,1)S(1)} %collective-permute-done.2.refs_4_), channel_id=1, source_target_pairs={{0,32},{32,64},{64,96},{96,0},{128,160},{160,192},{192,224},{224,1... | collective-permute-start | bytes 663560 | tf_op jit(solution)/shard_map/ppermute | solution.py:42
  38.7 3.4 %collective-permute-start.5 = (bf16[96,1152]{1,0:T(8,128)(2,1)S(1)}, bf16[96,1152]{1,0:T(8,128)(2,1)S(1)}, u32[]{:S(2)}, u32[]{:S(2)}) collective-permute-start(bf16[96,1152]{1,0:T(8,128)(2,1)S(1)} %collective-permute-done.3.refs_1_), channel_id=1, source_target_pairs={{0,32},{32,64},{64,96},{96,0},{128,160},{160,192},{192,224},{224,1... | collective-permute-start | bytes 663560 | tf_op jit(solution)/shard_map/ppermute | solution.py:42
  42.1 0.0 collective-permute-done.7.refs_6_
  42.1 1.9 %collective-permute-start.8 = (bf16[96,1152]{1,0:T(8,128)(2,1)S(1)}, bf16[96,1152]{1,0:T(8,128)(2,1)S(1)}, u32[]{:S(2)}, u32[]{:S(2)}) collective-permute-start(bf16[96,1152]{1,0:T(8,128)(2,1)S(1)} %collective-permute-done.7.refs_6_), channel_id=1, source_target_pairs={{0,96},{32,0},{64,32},{96,64},{128,224},{160,128},{192,160},{224,1... | collective-permute-start | bytes 663560 | tf_op jit(solution)/shard_map/ppermute | solution.py:42
  44.1 0.1 stack.51.spots.refs_0_
  44.2 6.0 %collective-permute-start.1 = (bf16[768,1152]{1,0:T(8,128)(2,1)}, bf16[768,1152]{1,0:T(8,128)(2,1)}, u32[]{:S(2)}, u32[]{:S(2)}) collective-permute-start(bf16[768,1152]{1,0:T(8,128)(2,1)} %refs_4_.1), channel_id=1, source_target_pairs={{0,128},{32,160},{64,192},{96,224},{128,0},{160,32},{192,64},{224,... | collective-permute-start | bytes 5308424 | tf_op jit(solution)/shard_map/ppermute | solution.py:42
  50.2 0.0 collective-permute-done.5.refs_3_
  50.3 0.0 collective-permute-done.6.refs_5_
  50.3 0.0 collective-permute-done.8.refs_7_
  50.3 0.0 copy-start.2
  50.3 0.7 copy-done.2
  51.0 0.0 copy-start.3
  51.0 0.9 copy-done.3
  51.9 2.9 %pack.1.refs_6_ = bf16[768,1152]{1,0:T(8,128)(2,1)S(1)} custom-call(s32[12]{0:T(128)S(1)} %stack.51.spots.refs_0_, bf16[96,1152]{1,0:T(8,128)(2,1)S(1)} %collective-permute-done.refs_0_, bf16[96,1152]{1,0:T(8,128)(2,1)S(1)} %collective-permute-done.3.refs_1_, bf16[96,1152]{1,0:T(8,128)(2,1)S(1)} %collective-permute-done.4.refs_2_, ...), custom_call_target="tpu_custom_call" | custom-call | bytes 4194304 | tf_op jit(solution)/shard_map/pack/pallas_call | solution.py:229
  54.8 0.0 copy-start.4
  54.9 0.6 copy-done.4
  55.4 6.9 %collective-permute-start.9 = (bf16[768,1152]{1,0:T(8,128)(2,1)S(1)}, bf16[768,1152]{1,0:T(8,128)(2,1)}, u32[]{:S(2)}, u32[]{:S(2)}) collective-permute-start(bf16[768,1152]{1,0:T(8,128)(2,1)S(1)} %pack.1.refs_6_), channel_id=1, source_target_pairs={{0,128},{32,160},{64,192},{96,224},{128,0},{160,32},{192,64},{224,... | collective-permute-start | bytes 5308424 | tf_op jit(solution)/shard_map/ppermute | solution.py:42
  62.9 0.0 collective-permute-done.1.refs_5_
  62.9 2.8 %collective-permute-done.9.refs_7_ = bf16[768,1152]{1,0:T(8,128)(2,1)} collective-permute-done((bf16[768,1152]{1,0:T(8,128)(2,1)S(1)}, bf16[768,1152]{1,0:T(8,128)(2,1)}, u32[]{:S(2)}, u32[]{:S(2)}) %collective-permute-start.9) | collective-permute-done | bytes 1769504 | tf_op jit(solution)/shard_map/ppermute | solution.py:42
  65.7 0.0 copy-done
  65.7 0.0 copy-start.7
  65.7 10.6 %project.1 = (bf16[512,384]{1,0:T(8,128)(2,1)}, bf16[512,768]{1,0:T(8,128)(2,1)}) custom-call(s32[12]{0:T(128)} %copy-done.4, s32[1,1]{1,0:T(1,128)S(6)} %copy.10.levels, bf16[8,512,384]{2,1,0:T(8,128)(2,1)} %bitcast.20, f32[32,2,3072]{2,1,0:T(2,128)} %refs_1_.3, f32[1,128]{1,0:T(1,128)} %bitcast.21, f32[1,128]{1,0:T(1,128)} %bitcast.22, ...), custom_call_target="tpu_custom_call" | custom-call | flops 3623878656 | bytes 12582912 | tf_op jit(solution)/shard_map/project/pallas_call | solution.py:242
  76.3 2.3 %collective-permute-start.11 = (bf16[512,768]{1,0:T(8,128)(2,1)}, bf16[512,768]{1,0:T(8,128)(2,1)S(1)}, u32[]{:S(2)}, u32[]{:S(2)}) collective-permute-start(bf16[512,768]{1,0:T(8,128)(2,1)} %get-tuple-element.27.own), channel_id=1, source_target_pairs={{0,128},{32,160},{64,192},{96,224},{128,0},{160,32},{192,64},{224,... | collective-permute-start | bytes 2359304 | tf_op jit(solution)/shard_map/ppermute | solution.py:42
  78.6 1.3 collective-permute-start.10
  79.9 0.8 collective-permute-done.11.pair
  80.7 0.0 copy-done.5
  80.7 0.0 copy-done.6
  80.7 0.0 copy-done.7
  80.7 1.0 copy-done.1
  81.7 1.1 copy-done.8
  82.9 3.1 %near.1 = (f32[512,384]{1,0:T(8,128)S(1)}, f32[512,384]{1,0:T(8,128)S(1)}) custom-call(s32[12]{0:T(128)S(1)} %copy-done.5, s32[1,4]{1,0:T(1,128)S(1)} %copy-done.7, s32[4,4]{1,0:T(4,128)S(1)} %bitcast.17, bf16[512,384]{1,0:T(8,128)(2,1)S(1)} %copy-done.1, bf16[512,768]{1,0:T(8,128)(2,1)S(1)} %copy-done.8, bf16[512,768]{1,0:T(8,128)(2,1)S(1)} %collective-permute-done.11.pair), custom_call_target="tpu_custom_call" | custom-call | flops 805306368 | bytes 6291456 | tf_op jit(solution)/shard_map/near/pallas_call | solution.py:275
  85.9 34.6 %collective-permute-done.10.refs_6_ = bf16[512,768]{1,0:T(8,128)(2,1)S(1)} collective-permute-done((bf16[512,768]{1,0:T(8,128)(2,1)}, bf16[512,768]{1,0:T(8,128)(2,1)S(1)}, u32[]{:S(2)}, u32[]{:S(2)}) %collective-permute-start.10) | collective-permute-done | bytes 786464 | tf_op jit(solution)/shard_map/ppermute | solution.py:42
  120.5 2.8 %collective-permute-start.12 = (bf16[512,768]{1,0:T(8,128)(2,1)S(1)}, bf16[512,768]{1,0:T(8,128)(2,1)S(1)}, u32[]{:S(2)}, u32[]{:S(2)}) collective-permute-start(bf16[512,768]{1,0:T(8,128)(2,1)S(1)} %collective-permute-done.10.refs_6_), channel_id=1, source_target_pairs={{0,128},{32,160},{64,192},{96,224},{128,0},{160,32},{192,64},{224,... | collective-permute-start | bytes 2359304 | tf_op jit(solution)/shard_map/ppermute | solution.py:42
  123.4 1.5 %far.1 = (f32[512,384]{1,0:T(8,128)S(1)}, f32[512,384]{1,0:T(8,128)S(1)}) custom-call(s32[12]{0:T(128)S(1)} %copy-done.5, s32[1,4]{1,0:T(1,128)S(1)} %copy-done.7, s32[4,4]{1,0:T(4,128)S(1)} %bitcast.18, bf16[512,384]{1,0:T(8,128)(2,1)S(1)} %copy-done.1, f32[512,384]{1,0:T(8,128)S(1)} %get-tuple-element.30.refs_4_, ...), custom_call_target="tpu_custom_call" | custom-call | flops 805306368 | bytes 6291456 | tf_op jit(solution)/shard_map/far/pallas_call | solution.py:286
  124.9 0.4 collective-permute-done.12.refs_6_
  125.2 3.3 %last.1 = bf16[512,384]{1,0:T(8,128)(2,1)} custom-call(s32[12]{0:T(128)S(1)} %copy-done.5, s32[1,4]{1,0:T(1,128)S(1)} %copy-done.7, s32[4,4]{1,0:T(4,128)S(1)} %bitcast.19, bf16[512,384]{1,0:T(8,128)(2,1)S(1)} %copy-done.1, f32[512,384]{1,0:T(8,128)S(1)} %get-tuple-element.33.refs_4_, f32[512,384]{1,0:T(8,128)S(1)} %get-tuple-element.34.refs_5_, ...), custom_call_target="tpu_custom_call" | custom-call | flops 805306368 | bytes 6291456 | tf_op jit(solution)/shard_map/last/pallas_call | solution.py:295
  (6 shorter events, 0.0 us)
Async XLA Ops:
  6.5 59.2 %all-gather.3.cloned.1.call-start = ((), (), s32[]{:S(2)}) async-start(), calls=%async_computation | async-start | bytes 3538944 | tf_op jit(solution)/shard_map/all_gather | solution.py:203
  8.4 11.3 %collective-permute-start = (bf16[96,1152]{1,0:T(8,128)(2,1)S(1)}, bf16[96,1152]{1,0:T(8,128)(2,1)S(1)}, u32[]{:S(2)}, u32[]{:S(2)}) collective-permute-start(bf16[96,1152]{1,0:T(8,128)(2,1)S(1)} %get-tuple-element.36), channel_id=1, source_target_pairs={{0,280},{32,312},{64,344},{96,376},{128,408},{160,440},{192,472},{... | collective-permute-start | bytes 663560 | tf_op jit(solution)/shard_map/ppermute | solution.py:42
  19.7 10.2 %collective-permute-start.2 = (bf16[96,1152]{1,0:T(8,128)(2,1)S(1)}, bf16[96,1152]{1,0:T(8,128)(2,1)S(1)}, u32[]{:S(2)}, u32[]{:S(2)}) collective-permute-start(bf16[96,1152]{1,0:T(8,128)(2,1)S(1)} %get-tuple-element.22), channel_id=1, source_target_pairs={{0,280},{32,312},{64,344},{96,376},{128,408},{160,440},{192,472},{... | collective-permute-start | bytes 663560 | tf_op jit(solution)/shard_map/ppermute | solution.py:42
  22.4 8.2 %collective-permute-start.4 = (bf16[96,1152]{1,0:T(8,128)(2,1)S(1)}, bf16[96,1152]{1,0:T(8,128)(2,1)S(1)}, u32[]{:S(2)}, u32[]{:S(2)}) collective-permute-start(bf16[96,1152]{1,0:T(8,128)(2,1)S(1)} %collective-permute-done.refs_0_), channel_id=1, source_target_pairs={{0,96},{32,0},{64,32},{96,64},{128,224},{160,128},{192,160},{224,1... | collective-permute-start | bytes 663560 | tf_op jit(solution)/shard_map/ppermute | solution.py:42
  24.9 7.1 %collective-permute-start.3 = (bf16[96,1152]{1,0:T(8,128)(2,1)S(1)}, bf16[96,1152]{1,0:T(8,128)(2,1)S(1)}, u32[]{:S(2)}, u32[]{:S(2)}) collective-permute-start(bf16[96,1152]{1,0:T(8,128)(2,1)S(1)} %collective-permute-done.refs_0_), channel_id=1, source_target_pairs={{0,32},{32,64},{64,96},{96,0},{128,160},{160,192},{192,224},{224,1... | collective-permute-start | bytes 663560 | tf_op jit(solution)/shard_map/ppermute | solution.py:42
  31.9 10.1 %collective-permute-start.7 = (bf16[96,1152]{1,0:T(8,128)(2,1)S(1)}, bf16[96,1152]{1,0:T(8,128)(2,1)S(1)}, u32[]{:S(2)}, u32[]{:S(2)}) collective-permute-start(bf16[96,1152]{1,0:T(8,128)(2,1)S(1)} %collective-permute-done.2.refs_4_), channel_id=1, source_target_pairs={{0,96},{32,0},{64,32},{96,64},{128,224},{160,128},{192,160},{224,1... | collective-permute-start | bytes 663560 | tf_op jit(solution)/shard_map/ppermute | solution.py:42
  34.1 16.2 %collective-permute-start.6 = (bf16[96,1152]{1,0:T(8,128)(2,1)S(1)}, bf16[96,1152]{1,0:T(8,128)(2,1)S(1)}, u32[]{:S(2)}, u32[]{:S(2)}) collective-permute-start(bf16[96,1152]{1,0:T(8,128)(2,1)S(1)} %collective-permute-done.2.refs_4_), channel_id=1, source_target_pairs={{0,32},{32,64},{64,96},{96,0},{128,160},{160,192},{192,224},{224,1... | collective-permute-start | bytes 663560 | tf_op jit(solution)/shard_map/ppermute | solution.py:42
  38.7 11.5 %collective-permute-start.5 = (bf16[96,1152]{1,0:T(8,128)(2,1)S(1)}, bf16[96,1152]{1,0:T(8,128)(2,1)S(1)}, u32[]{:S(2)}, u32[]{:S(2)}) collective-permute-start(bf16[96,1152]{1,0:T(8,128)(2,1)S(1)} %collective-permute-done.3.refs_1_), channel_id=1, source_target_pairs={{0,32},{32,64},{64,96},{96,0},{128,160},{160,192},{192,224},{224,1... | collective-permute-start | bytes 663560 | tf_op jit(solution)/shard_map/ppermute | solution.py:42
  42.1 8.2 %collective-permute-start.8 = (bf16[96,1152]{1,0:T(8,128)(2,1)S(1)}, bf16[96,1152]{1,0:T(8,128)(2,1)S(1)}, u32[]{:S(2)}, u32[]{:S(2)}) collective-permute-start(bf16[96,1152]{1,0:T(8,128)(2,1)S(1)} %collective-permute-done.7.refs_6_), channel_id=1, source_target_pairs={{0,96},{32,0},{64,32},{96,64},{128,224},{160,128},{192,160},{224,1... | collective-permute-start | bytes 663560 | tf_op jit(solution)/shard_map/ppermute | solution.py:42
  44.2 18.7 %collective-permute-start.1 = (bf16[768,1152]{1,0:T(8,128)(2,1)}, bf16[768,1152]{1,0:T(8,128)(2,1)}, u32[]{:S(2)}, u32[]{:S(2)}) collective-permute-start(bf16[768,1152]{1,0:T(8,128)(2,1)} %refs_4_.1), channel_id=1, source_target_pairs={{0,128},{32,160},{64,192},{96,224},{128,0},{160,32},{192,64},{224,... | collective-permute-start | bytes 5308424 | tf_op jit(solution)/shard_map/ppermute | solution.py:42
  50.3 0.7 copy-start.2
  51.0 0.9 copy-start.3
  54.8 0.6 copy-start.4
  55.4 10.3 %copy-start = (bf16[768,1152]{1,0:T(8,128)(2,1)}, bf16[768,1152]{1,0:T(8,128)(2,1)S(1)}, u32[]{:S(2)}) copy-start(bf16[768,1152]{1,0:T(8,128)(2,1)S(1)} %pack.1.refs_6_) | copy-start | bytes 5308420
  55.4 10.3 %collective-permute-start.9 = (bf16[768,1152]{1,0:T(8,128)(2,1)S(1)}, bf16[768,1152]{1,0:T(8,128)(2,1)}, u32[]{:S(2)}, u32[]{:S(2)}) collective-permute-start(bf16[768,1152]{1,0:T(8,128)(2,1)S(1)} %pack.1.refs_6_), channel_id=1, source_target_pairs={{0,128},{32,160},{64,192},{96,224},{128,0},{160,32},{192,64},{224,... | collective-permute-start | bytes 5308424 | tf_op jit(solution)/shard_map/ppermute | solution.py:42
  65.7 15.0 %copy-start.5 = (s32[12]{0:T(128)S(1)}, s32[12]{0:T(128)}, u32[]{:S(2)}) copy-start(s32[12]{0:T(128)} %copy-done.4) | copy-start | bytes 148
  65.7 15.0 %copy-start.6 = (s32[1,4,4]{2,1,0:T(4,128)S(1)}, s32[1,4,4]{2,1,0:T(4,128)}, u32[]{:S(2)}) copy-start(s32[1,4,4]{2,1,0:T(4,128)} %param.11) | copy-start | bytes 196
  65.7 15.0 %copy-start.7 = (s32[1,4]{1,0:T(1,128)S(1)}, s32[1,4]{1,0:T(1,128)}, u32[]{:S(2)}) copy-start(s32[1,4]{1,0:T(1,128)} %refs_1_.5) | copy-start | bytes 52
  76.3 4.4 %collective-permute-start.11 = (bf16[512,768]{1,0:T(8,128)(2,1)}, bf16[512,768]{1,0:T(8,128)(2,1)S(1)}, u32[]{:S(2)}, u32[]{:S(2)}) collective-permute-start(bf16[512,768]{1,0:T(8,128)(2,1)} %get-tuple-element.27.own), channel_id=1, source_target_pairs={{0,128},{32,160},{64,192},{96,224},{128,0},{160,32},{192,64},{224,... | collective-permute-start | bytes 2359304 | tf_op jit(solution)/shard_map/ppermute | solution.py:42
  78.6 41.9 %collective-permute-start.10 = (bf16[512,768]{1,0:T(8,128)(2,1)}, bf16[512,768]{1,0:T(8,128)(2,1)S(1)}, u32[]{:S(2)}, u32[]{:S(2)}) collective-permute-start(bf16[512,768]{1,0:T(8,128)(2,1)} %get-tuple-element.27.own), channel_id=1, source_target_pairs={{0,256},{32,288},{64,320},{96,352},{128,384},{160,416},{192,448},{... | collective-permute-start | bytes 2359304 | tf_op jit(solution)/shard_map/ppermute | solution.py:42
  80.7 1.0 copy-start.1
  81.7 1.1 copy-start.8
  120.5 4.7 %collective-permute-start.12 = (bf16[512,768]{1,0:T(8,128)(2,1)S(1)}, bf16[512,768]{1,0:T(8,128)(2,1)S(1)}, u32[]{:S(2)}, u32[]{:S(2)}) collective-permute-start(bf16[512,768]{1,0:T(8,128)(2,1)S(1)} %collective-permute-done.10.refs_6_), channel_id=1, source_target_pairs={{0,128},{32,160},{64,192},{96,224},{128,0},{160,32},{192,64},{224,... | collective-permute-start | bytes 2359304 | tf_op jit(solution)/shard_map/ppermute | solution.py:42
Sparse Core Ops, SparseCore 0:
  9.4 50.4 all-gather.2
